TPU v7x, 128 devices: a whole 4x4x4 slice. The times are simulated.
128 devices in a mesh: frame: 8 (over y_hi, z), batch: 16 (over x, y_lo, core).
Axes of the slice: x: 4, y: 4 (y_hi: 2, y_lo: 2; y = y_hi * 2 + y_lo), z: 4, core: 2. Of those that a mesh axis runs over, the one named last changes fastest.
Arguments:
- queries: bfloat16 [16, 1024, 5120], P('batch', 'frame'), may hold values from -180 to 180
- keys: bfloat16 [16, 1024, 5120], P('batch', 'frame'), may hold values from -6 to 6
- values: bfloat16 [16, 1024, 5120], P('batch', 'frame'), may hold values from -24 to 24
- out_weight: bfloat16 [5120, 5120], P(None, 'batch'), may hold values from -0.078125 to 0.078125
- gate: float32 [16, 5120], P('batch'), may hold values from -6 to 6
- kv_frames: int32 [16, 6], replicated, may hold values from -1 to 15, as said below
Outputs:
- branch_out: bfloat16 [16, 1024, 5120], P('batch', 'frame')
Inputs may be any that keep to these rules, and one draw needn't show every extreme that they name: `kv_frames`: row f lists frame f in its first slot; its non-negative entries are distinct frames; -1 marks an empty slot, and empty slots follow the listed ones; every row lists 3 or more frames.
All inputs are finite; a program needn't handle non-finite values.
Results may differ from a plain program's by a relative error of at most 0.012.
Values may be sent and summed in bfloat16 or wider, within the bound.
No kernel may reach another device: no remote copies, remote signals or barrier semaphores. Data moves between devices by JAX's collectives and lax.ppermute only.
A program may use at most 128 MiB of HBM per device.

v0:
```python
import math

import jax
import jax.numpy as jnp
from jax import lax
from jax.sharding import PartitionSpec as P

HEADS = 40
HEAD_DIM = 128
FRAME_TOKENS = 64
FRAME_DEV = 2


def start_state(n_query, n_head, head_size):
    return (
        jnp.full((n_query, n_head), -1e30, jnp.float32),
        jnp.zeros((n_query, n_head), jnp.float32),
        jnp.zeros((n_query, n_head, head_size), jnp.float32),
    )


def attend_keys(state, query_h, key_h, value_h, permit, frame_tokens):
    run_max, run_sum, accum = state
    score_scale = 1.0 / math.sqrt(query_h.shape[2])
    scores = (
        jnp.einsum("qhd,khd->qhk", query_h, key_h, preferred_element_type=jnp.float32) * score_scale
    )
    n_query, n_head, n_key = scores.shape
    token_mask = jnp.broadcast_to(
        permit[:, None, None, :, None],
        (n_query // frame_tokens, frame_tokens, n_head, n_key // frame_tokens, frame_tokens),
    )
    token_mask = token_mask.reshape(n_query, n_head, n_key)
    scores = jnp.where(token_mask, scores, -1e30)
    new_max = jnp.maximum(run_max, jnp.max(scores, axis=2))
    probs = jnp.where(token_mask, jnp.exp(scores - new_max[:, :, None]), 0.0)
    run_sum = jnp.sum(probs, axis=2)
    accum = jnp.einsum(
        "qhk,khd->qhd", probs.astype(jnp.bfloat16), value_h, preferred_element_type=jnp.float32
    )
    return (new_max, run_sum, accum)


def local(queries, keys, values, out_weight, gate, kv_frames):
    local_rows = queries.shape[1]
    width = queries.shape[2]
    total_frames = FRAME_DEV * lax.axis_size("frame")
    frame_ids = jnp.arange(total_frames, dtype=jnp.int32)
    allowed = jnp.any(kv_frames[:, :, None] == frame_ids[None, None, :], axis=1)
    query_h = queries[0].reshape(local_rows, HEADS, HEAD_DIM)
    my_index = lax.axis_index("frame")
    my_permit = lax.dynamic_slice_in_dim(allowed, my_index * FRAME_DEV, FRAME_DEV, 0)
    key_piece = lax.all_gather(keys[0], "frame", axis=0, tiled=True)
    value_piece = lax.all_gather(values[0], "frame", axis=0, tiled=True)
    piece_rows = key_piece.shape[0]
    run_max, run_sum, accum = attend_keys(
        start_state(local_rows, HEADS, HEAD_DIM),
        query_h,
        key_piece.reshape(piece_rows, HEADS, HEAD_DIM),
        value_piece.reshape(piece_rows, HEADS, HEAD_DIM),
        my_permit,
        FRAME_TOKENS,
    )
    attended = (accum / run_sum[:, :, None]).astype(jnp.bfloat16).reshape(local_rows, width)
    projected = jnp.einsum(
        "brd,df->brf",
        lax.all_gather(attended[None], "batch", axis=0, tiled=True),
        out_weight,
        preferred_element_type=jnp.float32,
    ).astype(jnp.bfloat16)
    mine = lax.all_to_all(projected, "batch", split_axis=0, concat_axis=2, tiled=True)
    return (gate[:, None, :] * mine.astype(jnp.float32)).astype(jnp.bfloat16)


def solution(mesh):
    in_specs = (
        P("batch", "frame", None),
        P("batch", "frame", None),
        P("batch", "frame", None),
        P(None, "batch"),
        P("batch", None),
        P(),
    )
    out_specs = P("batch", "frame", None)
    return jax.shard_map(local, mesh=mesh, in_specs=in_specs, out_specs=out_specs, check_vma=False)
```

profile of v0, /device:TPU:24, one launch (start us, length us, event | category | flops | bytes accessed | tf_op | source)
XLA Modules:
  0.0 463.7 jit_solution(17855625825369947330)
XLA Ops:
  6.5 0.0 copy-start
  6.5 0.0 all-gather.8.cloned.1.call-start
  6.5 2.6 copy.32
  9.1 0.0 all-gather.8.cloned.1.call-update
  9.1 0.0 all-gather.10.cloned.1.call-start
  9.2 0.7 all-gather.10.cloned.1.call-update
  9.9 0.0 all-gather.6.cloned.1.call-start
  9.9 0.8 fusion.20
  10.7 0.1 broadcast_in_dim.25
  10.9 1.1 broadcast_in_dim.26
  11.9 1.2 copy.31
  13.1 2.6 copy.41
  15.7 127.8 %all-gather.8.cloned.1.call-done = bf16[1,1024,5120]{1,2,0:T(8,128)(2,1)} async-done(((bf16[1,128,5120]{1,2,0:T(8,128)(2,1)}), bf16[1,1024,5120]{1,2,0:T(8,128)(2,1)}) %all-gather.8.cloned.1.call-update) | async-done | bytes 10485776 | tf_op jit(solution)/shard_map/all_gather | solution.py:53
  143.5 12.8 %fusion = (f32[128,40]{0,1:T(8,128)S(1)}, f32[40,1024,128]{2,1,0:T(8,128)}) fusion(pred[128,1024]{0,1:T(8,128)(4,1)S(1)} %copy.31, bf16[1024,40,128]{0,2,1:T(8,128)(2,1)} %bitcast.40, bf16[128,40,128]{2,1,0:T(8,128)(2,1)} %bitcast.41), kind=kOutput, calls=%fused_computation.2 | convolution fusion | flops 1357900800 | bytes 32919552 | tf_op jit(solution)/shard_map/qhd,khd->qhk/dot_general | solution.py:26
  156.3 10.3 %fusion.1 = f32[128,40]{0,1:T(8,128)S(1)} fusion(f32[40,1024,128]{2,1,0:T(8,128)} %get-tuple-element.6, f32[128,40]{0,1:T(8,128)S(1)} %broadcast_maximum_fusion, pred[128,1024]{0,1:T(8,128)(4,1)S(1)} %copy.31), kind=kLoop, calls=%fused_computation.3 | loop fusion | flops 26209280 | bytes 21143552 | tf_op jit(solution)/shard_map/reduce_sum | solution.py:37
  166.6 103.2 %all-gather.10.cloned.1.call-done = bf16[1,1024,5120]{2,1,0:T(8,128)(2,1)} async-done(((bf16[1,128,5120]{2,1,0:T(8,128)(2,1)}), bf16[1,1024,5120]{2,1,0:T(8,128)(2,1)}) %all-gather.10.cloned.1.call-update) | async-done | bytes 10485776 | tf_op jit(solution)/shard_map/all_gather | solution.py:54
  269.8 14.4 %copy.35 = bf16[1,1024,5120]{1,2,0:T(8,128)(2,1)} copy(bf16[1,1024,5120]{2,1,0:T(8,128)(2,1)} %all-gather.10.cloned.1.call-done) | data formatting | bytes 20971520 | tf_op jit(solution)/shard_map/all_gather | solution.py:54
  284.2 17.8 %fusion.12 = bf16[128,40,128]{0,2,1:T(8,128)(2,1)} fusion(bf16[1024,40,128]{0,2,1:T(8,128)(2,1)} %bitcast.42, f32[40,1024,128]{2,1,0:T(8,128)} %get-tuple-element.6, f32[128,40]{0,1:T(8,128)S(1)} %broadcast_maximum_fusion, pred[128,1024]{0,1:T(8,128)(4,1)S(1)} %copy.31, f32[128,40]{0,1:T(8,128)S(1)} %fusion.1), kind=kOutput, calls=%fused_computation.14 | convolution fusion | flops 1369702400 | bytes 32940032 | tf_op jit(solution)/shard_map/qhk,khd->qhd/dot_general | solution.py:38
  302.1 2.5 copy.37
  304.5 0.0 all-gather.6.cloned.1.call-update
  304.5 110.8 %all-gather.6.cloned.1.call-done = bf16[16,128,5120]{2,1,0:T(8,128)(2,1)} async-done(((bf16[1,128,5120]{2,1,0:T(8,128)(2,1)}), bf16[16,128,5120]{2,1,0:T(8,128)(2,1)}) %all-gather.6.cloned.1.call-update) | async-done | bytes 20971536 | tf_op jit(solution)/shard_map/all_gather | solution.py:67
  415.3 0.0 copy-done
  415.3 10.8 %fusion.15 = bf16[16,128,320]{1,2,0:T(8,128)(2,1)S(1)} fusion(bf16[16,128,5120]{2,1,0:T(8,128)(2,1)} %all-gather.6.cloned.1.call-done, bf16[5120,320]{0,1:T(8,128)(2,1)S(1)} %copy-done), kind=kOutput, calls=%fused_computation.16 | convolution fusion | flops 6711541760 | bytes 25559040 | tf_op jit(solution)/shard_map/brd,df->brf/dot_general | solution.py:65
  426.2 0.0 copy-start.1
  426.2 23.0 %all_to_all.4 = bf16[16,128,320]{1,2,0:T(8,128)(2,1)S(1)} all-to-all(bf16[16,128,320]{1,2,0:T(8,128)(2,1)S(1)} %fusion.15), channel_id=1, replica_groups=mesh['frame'=8,'batch'=16] {'batch'}, dimensions={0} | all-to-all | bytes 2621440 | tf_op jit(solution)/shard_map/all_to_all | solution.py:71
  449.1 1.8 bitcast_convert_fusion
  450.9 3.2 copy.38
  454.1 0.0 copy-done.1
  454.1 3.0 multiply_convert_fusion
  (2 shorter events, 0.0 us)
Async XLA Ops:
  6.5 408.8 %copy-start = (bf16[5120,320]{0,1:T(8,128)(2,1)S(1)}, bf16[5120,320]{0,1:T(8,128)(2,1)}, u32[]{:S(2)}) copy-start(bf16[5120,320]{0,1:T(8,128)(2,1)} %param.9) | copy-start | bytes 9830404
  6.5 137.0 %all-gather.8.cloned.1.call-start = ((), (), s32[]{:S(2)}) async-start(), calls=%async_computation.2 | async-start | bytes 11796480 | tf_op jit(solution)/shard_map/all_gather | solution.py:53
  9.1 260.7 %all-gather.10.cloned.1.call-start = ((), (), s32[]{:S(2)}) async-start(), calls=%async_computation.3 | async-start | bytes 11796480 | tf_op jit(solution)/shard_map/all_gather | solution.py:54
  9.9 405.4 %all-gather.6.cloned.1.call-start = ((), (), s32[]{:S(2)}) async-start(), calls=%async_computation.1 | async-start | bytes 22282240 | tf_op jit(solution)/shard_map/all_gather | solution.py:67
  426.2 28.0 %copy-start.1 = (f32[1,5120]{1,0:T(1,128)S(1)}, f32[1,5120]{1,0:T(1,128)}, u32[]{:S(2)}) copy-start(f32[1,5120]{1,0:T(1,128)} %param.10) | copy-start | bytes 61444
Sparse Core Ops, SparseCore 0:
  9.5 133.9 all-gather.7
  145.8 123.9 all-gather.9
  304.7 110.6 all-gather.5
where the time goes:
time: 467 us; the launch traced here: 464 us
  waiting for transfers between devices  343 us (73%)
  matrix products  41.5 us (9%)
  local copies, waits for them, and re-layouts  27.7 us (6%)
  blocking collectives  23 us (5%)
  other arithmetic  15.8 us (3%)
  between operations  13.2 us (3%)
    all_gather x1, waiting for transfers between devices, local(): key_piece = lax.all_gather(keys[0], 'frame', axis=0, tiled=True)  128 us
    all_gather x1, waiting for transfers between devices, local(): lax.all_gather(attended[None], 'batch', axis=0, tiled=True)  111 us
    all_gather x1, waiting for transfers between devices, local(): value_piece = lax.all_gather(values[0], 'frame', axis=0, tiled=True)  103 us
    all_to_all x1, blocking collectives, local(): lax.all_to_all(projected, 'batch', split_axis=0, concat_axis=2, tiled=True)  23 us
    dot_general x1, matrix products, attend_keys(): jnp.einsum('qhk,khd->qhd', probs.astype(jnp.bfloat16), value_h, preferred...  17.8 us
    all_gather x1, local copies, waits for them, and re-layouts, local(): value_piece = lax.all_gather(values[0], 'frame', axis=0, tiled=True)  14.4 us
    dot_general x1, matrix products, attend_keys(): jnp.einsum('qhd,khd->qhk', query_h, key_h, preferred_element_type=jnp.flo...  12.8 us
    dot_general x1, matrix products, local(): jnp.einsum('brd,df->brf', lax.all_gather(attended[None], 'batch', axis=0,...  10.8 us
  transfers between devices with their start and end apart: 3, of which 3 were waited for; matrix products, arithmetic and copies ran while one was open for 6% of the time, Pallas kernels for 0%

commit v1 on v0

v1 whole, which is shorter than its diff:
```python
import functools
import math

import jax
import jax.numpy as jnp
from jax import lax
from jax.experimental import pallas as pl
from jax.experimental.pallas import tpu as pltpu
from jax.sharding import Mesh
from jax.sharding import PartitionSpec as P

HEAD_DIM = 128
FRAME = 64
VMEM = 40 * 1024 * 1024


def attend_kernel(meta, q_ref, k_ref, v_ref, o_ref, *, slots, heads):
    frame = meta[0] + pl.program_id(0)
    base = 1 + frame * slots
    lane = lax.broadcasted_iota(jnp.int32, (1, slots * FRAME), 1)
    bias = jnp.zeros((1, slots * FRAME), jnp.float32)
    picks = []
    for s in range(slots):
        g = meta[base + s]
        inside = (lane >= s * FRAME) & (lane < (s + 1) * FRAME)
        bias = jnp.where(inside, jnp.where(g >= 0, 0.0, -1e30), bias)
        g = jnp.maximum(g, 0)
        picks.append((g // 2, pl.multiple_of((g % 2) * FRAME, FRAME)))
    scale = 1.0 / math.sqrt(HEAD_DIM)
    for h in range(heads):
        cols = slice(h * HEAD_DIM, (h + 1) * HEAD_DIM)
        key = jnp.concatenate([k_ref[b, pl.ds(r, FRAME), cols] for b, r in picks], 0)
        val = jnp.concatenate([v_ref[b, pl.ds(r, FRAME), cols] for b, r in picks], 0)
        scores = lax.dot_general(
            q_ref[:, cols], key, (((1,), (1,)), ((), ())), preferred_element_type=jnp.float32
        )
        scores = scores * scale + bias
        top = jnp.max(scores, axis=1, keepdims=True)
        probs = jnp.exp(scores - top)
        denom = jnp.sum(probs, axis=1, keepdims=True)
        accum = jnp.dot(probs.astype(jnp.bfloat16), val, preferred_element_type=jnp.float32)
        o_ref[:, cols] = (accum / denom).astype(jnp.bfloat16)


def attend(meta, parts, frames, slots):
    blocks, _, rows, width = parts.shape
    per = rows // FRAME
    whole = lambda which: pl.BlockSpec(
        (blocks, None, rows, width), lambda i, m: (0, which, 0, 0)
    )
    return pl.pallas_call(
        functools.partial(attend_kernel, slots=slots, heads=width // HEAD_DIM),
        grid_spec=pltpu.PrefetchScalarGridSpec(
            num_scalar_prefetch=1,
            grid=(frames,),
            in_specs=[
                pl.BlockSpec(
                    (None, None, FRAME, width),
                    lambda i, m: ((m[0] + i) // per, 0, (m[0] + i) % per, 0),
                ),
                whole(1),
                whole(2),
            ],
            out_specs=pl.BlockSpec((FRAME, width), lambda i, m: (i, 0)),
        ),
        out_shape=jax.ShapeDtypeStruct((frames * FRAME, width), jnp.bfloat16),
        compiler_params=pltpu.CompilerParams(vmem_limit_bytes=VMEM),
        cost_estimate=pl.CostEstimate(
            flops=frames * FRAME * slots * FRAME * width * 4,
            bytes_accessed=3 * blocks * rows * width * 2,
            transcendentals=frames * FRAME * slots * FRAME * width // HEAD_DIM,
        ),
    )(meta, parts, parts, parts)


def project_kernel(meta, a_ref, b_ref, wa_ref, wb_ref, o_ref):
    nt = (((1,), (1,)), ((), ()))
    total = lax.dot_general(a_ref[...], wa_ref[...], nt, preferred_element_type=jnp.float32)
    total += lax.dot_general(b_ref[...], wb_ref[...], nt, preferred_element_type=jnp.float32)
    o_ref[...] = total.astype(jnp.bfloat16)


def project(meta, mine, other, weight_t, tile=512):
    rows, depth = mine.shape
    width = weight_t.shape[0]
    return pl.pallas_call(
        project_kernel,
        grid_spec=pltpu.PrefetchScalarGridSpec(
            num_scalar_prefetch=1,
            grid=(width // tile,),
            in_specs=[
                pl.BlockSpec((rows, depth), lambda i, m: (0, 0)),
                pl.BlockSpec((rows, depth), lambda i, m: (0, 0)),
                pl.BlockSpec((tile, depth), lambda i, m: (i, m[0])),
                pl.BlockSpec((tile, depth), lambda i, m: (i, 1 - m[0])),
            ],
            out_specs=pl.BlockSpec((rows, tile), lambda i, m: (0, i)),
        ),
        out_shape=jax.ShapeDtypeStruct((rows, width), jnp.bfloat16),
        compiler_params=pltpu.CompilerParams(vmem_limit_bytes=VMEM),
        cost_estimate=pl.CostEstimate(
            flops=4 * rows * depth * width,
            bytes_accessed=4 * depth * width + 2 * rows * width,
            transcendentals=0,
        ),
    )(meta, mine, other, weight_t, weight_t)


def local(queries, keys, values, out_weight, gate, kv_frames):
    rows, width = queries.shape[1:]
    n_y, n_z = lax.axis_size("yh"), lax.axis_size("z")
    n = n_y * n_z
    cols = width // n
    frames, slots = kv_frames.shape
    half = frames // n_y
    my_y, my_z = lax.axis_index("yh"), lax.axis_index("z")

    weight = lax.dynamic_slice_in_dim(out_weight, my_z * (n_y * cols), n_y * cols, 0).T
    weight_t = lax.all_gather(weight, ("x", "yl", "c"), axis=0, tiled=True)

    def blocks(array):
        return array[0].reshape(rows, n_z, n_y, cols).transpose(2, 1, 0, 3).reshape(n, rows, cols)

    parts = jnp.stack([blocks(queries), blocks(keys), blocks(values)], 1)
    parts = lax.all_to_all(parts, ("yh", "z"), 0, 0, tiled=True)

    table = kv_frames.reshape(-1)
    first = lambda y: jnp.concatenate([(y * half)[None].astype(jnp.int32), table])
    theirs = attend(first(1 - my_y), parts, half, slots)
    other = lax.ppermute(theirs, "yh", [(i, 1 - i) for i in range(n_y)])
    mine = attend(first(my_y), parts, half, slots)

    partial = project(my_y[None].astype(jnp.int32), mine, other, weight_t)
    total = lax.psum_scatter(partial, "z", scatter_dimension=0, tiled=True)
    return (gate[:, None, :] * total[None].astype(jnp.float32)).astype(jnp.bfloat16)


def solution(mesh):
    fine = Mesh(mesh.devices.reshape(2, 4, 4, 2, 2), ("yh", "z", "x", "yl", "c"))
    frame, batch = ("yh", "z"), ("x", "yl", "c")
    act = P(batch, frame, None)
    return jax.shard_map(
        local,
        mesh=fine,
        in_specs=(act, act, act, P(None, batch), P(batch, None), P()),
        out_specs=act,
        check_vma=False,
    )
```

time: 467 us -> 244 us (0.52)
  waiting for transfers between devices: 343 us -> 142 us
  matrix products: 41.5 us -> 0 us
  Pallas kernels: 0 us -> 40.7 us
  blocking collectives: 23 us -> 0 us
  other arithmetic: 15.8 us -> 4.89 us
  starting transfers between devices: 0.08 us -> 10.9 us
    all_gather x3 -> x1, waiting for transfers between devices: 342 us -> 0.01 us  [local(): weight_t = lax.all_gather(weight, ('x', 'yl', 'c'), axis=0, tiled=True)]
    all_to_all x0 -> x1, waiting for transfers between devices: none -> 85.5 us  [local(): parts = lax.all_to_all(parts, ('yh', 'z'), 0, 0, tiled=True)]
    reduce_scatter x0 -> x1, waiting for transfers between devices: none -> 56.7 us  [local(): total = lax.psum_scatter(partial, 'z', scatter_dimension=0, tiled=True)]
    dot_general x3 -> x0, matrix products: 41.5 us -> none  [the longest x1 17.8 us: attend_keys(): jnp.einsum('qhk,khd->qhd', probs.astype(jnp.bfloat16), value_h, preferred...]
    pallas_call x0 -> x3, Pallas kernels: none -> 40.7 us  [the longest x2 27.8 us: attend(): pl.pallas_call(functools.partial(attend_kernel, slots=slots, heads=width...]
    all_to_all x1 -> x0, blocking collectives: 23 us -> none  [local(): lax.all_to_all(projected, 'batch', split_axis=0, concat_axis=2, tiled=True)]
    another operation x1 -> x6, local copies, waits for them, and re-layouts: 2.46 us -> 19.8 us  [blocks(): array[0].reshape(rows, n_z, n_y, cols).transpose(2, 1, 0, 3)]
    all_gather x1 -> x0, local copies, waits for them, and re-layouts: 14.4 us -> none  [local(): value_piece = lax.all_gather(values[0], 'frame', axis=0, tiled=True)]
  transfers between devices with their start and end apart: 3 -> 4, of which waited for: 3 -> 2; matrix products, arithmetic and copies ran while one was open for 6% -> 9% of each run, Pallas kernels for 0% -> 11%
where the time goes in v1:
time: 244 us; the launch traced here: 242 us
  waiting for transfers between devices  142 us (58%)
  Pallas kernels  40.7 us (17%)
  local copies, waits for them, and re-layouts  29.5 us (12%)
  between operations  13.5 us (6%)
  starting transfers between devices  10.9 us (4%)
  other arithmetic  4.89 us (2%)
    all_to_all x1, waiting for transfers between devices, local(): parts = lax.all_to_all(parts, ('yh', 'z'), 0, 0, tiled=True)  85.5 us
    reduce_scatter x1, waiting for transfers between devices, local(): total = lax.psum_scatter(partial, 'z', scatter_dimension=0, tiled=True)  56.7 us
    pallas_call x2, Pallas kernels, attend(): pl.pallas_call(functools.partial(attend_kernel, slots=slots, heads=width...  27.8 us
    another operation x6, local copies, waits for them, and re-layouts, blocks(): array[0].reshape(rows, n_z, n_y, cols).transpose(2, 1, 0, 3)  19.8 us
    pallas_call x1, Pallas kernels, project(): pl.pallas_call(project_kernel, grid_spec=pltpu.PrefetchScalarGridSpec(num...  12.9 us
    unnamed x21, local copies, waits for them, and re-layouts  8.68 us
    all_to_all x1, starting transfers between devices, local(): parts = lax.all_to_all(parts, ('yh', 'z'), 0, 0, tiled=True)  7.99 us
  transfers between devices with their start and end apart: 4, of which 2 were waited for; matrix products, arithmetic and copies ran while one was open for 9% of the time, Pallas kernels for 11%

profile of v1, /device:TPU:24, one launch (start us, length us, event | category | flops | bytes accessed | tf_op | source)
XLA Modules:
  0.0 241.7 jit_solution(13002400496376133924)
XLA Ops:
  6.5 0.0 copy-start
  6.5 0.0 all-gather.2.cloned.1.call-start
  6.5 1.9 copy-done
  8.5 1.0 dynamic-slice_bitcast_fusion
  9.4 0.0 all-gather.2.cloned.1.call-update
  9.5 4.2 %reshape_squeeze.11 = bf16[128,4,2,640]{3,2,1,0:T(2,128)(2,1)} reshape(bf16[1,128,5120]{2,1,0:T(8,128)(2,1)} %param.8) | data formatting | bytes 2621440 | tf_op jit(solution)/shard_map/reshape;squeeze | solution.py:122
  13.7 2.5 %copy.14 = bf16[128,4,2,640]{3,0,1,2:T(8,128)(2,1)} copy(bf16[128,4,2,640]{3,2,1,0:T(2,128)(2,1)} %reshape_squeeze.11) | data formatting | bytes 2621440 | tf_op jit(solution)/shard_map/reshape;squeeze | solution.py:122
  16.2 4.2 %reshape_squeeze.10 = bf16[128,4,2,640]{3,2,1,0:T(2,128)(2,1)} reshape(bf16[1,128,5120]{2,1,0:T(8,128)(2,1)} %param.7) | data formatting | bytes 2621440 | tf_op jit(solution)/shard_map/reshape;squeeze | solution.py:122
  20.5 2.8 %copy.13 = bf16[128,4,2,640]{3,0,1,2:T(8,128)(2,1)} copy(bf16[128,4,2,640]{3,2,1,0:T(2,128)(2,1)} %reshape_squeeze.10) | data formatting | bytes 2621440 | tf_op jit(solution)/shard_map/reshape;squeeze | solution.py:122
  23.3 4.2 %reshape_squeeze.9 = bf16[128,4,2,640]{3,2,1,0:T(2,128)(2,1)} reshape(bf16[1,128,5120]{2,1,0:T(8,128)(2,1)} %param.6) | data formatting | bytes 2621440 | tf_op jit(solution)/shard_map/reshape;squeeze | solution.py:122
  27.5 0.0 copy-start.6
  27.6 0.0 copy-start.7
  27.6 1.7 copy.12
  29.3 0.1 copy-done.6
  29.4 0.4 copy-done.7
  29.8 2.2 pad_maximum_fusion
  32.0 0.0 copy-start.9
  32.0 8.0 %all-to-all-start = ((bf16[8,3,128,640]{3,2,1,0:T(8,128)(2,1)}), bf16[8,3,128,640]{3,2,1,0:T(8,128)(2,1)}, u32[]{:S(2)}, u32[]{:S(2)}) async-start(bf16[8,3,128,640]{3,2,1,0:T(8,128)(2,1)} %pad_maximum_fusion), calls=%async_computation | async-start | bytes 7864320 | tf_op jit(solution)/shard_map/all_to_all | solution.py:125
  40.0 0.0 reduce-scatter.2.cloned.1.call-start
  40.0 0.0 copy-done.9
  40.0 0.1 copy.11
  40.0 0.1 reshape.9
  40.1 0.1 pad_add_fusion.1
  40.2 85.5 %all-to-all-done.q_ref.k_ref.v_ref = bf16[8,3,128,640]{3,2,1,0:T(8,128)(2,1)} async-done(((bf16[8,3,128,640]{3,2,1,0:T(8,128)(2,1)}), bf16[8,3,128,640]{3,2,1,0:T(8,128)(2,1)}, u32[]{:S(2)}, u32[]{:S(2)}) %all-to-all-start) | async-done | bytes 3932192 | tf_op jit(solution)/shard_map/all_to_all | solution.py:125
  125.7 13.9 %shard_map.65 = bf16[512,640]{1,0:T(8,128)(2,1)S(1)} custom-call(s32[97]{0:T(128)S(1)} %get-tuple-element.5.meta, bf16[8,3,128,640]{3,2,1,0:T(8,128)(2,1)} %all-to-all-done.q_ref.k_ref.v_ref, bf16[8,3,128,640]{3,2,1,0:T(8,128)(2,1)} %all-to-all-done.q_ref.k_ref.v_ref, bf16[8,3,128,640]{3,2,1,0:T(8,128)(2,1)} %all-to-all-done.q_ref.k_ref.v_ref), custom_call_target="tpu_custom_call" | custom-call | flops 503316480 | bytes 3932160 | tf_op jit(solution)/shard_map/pallas_call | solution.py:51
  139.6 2.9 %collective-permute-start = (bf16[512,640]{1,0:T(8,128)(2,1)S(1)}, bf16[512,640]{1,0:T(8,128)(2,1)S(1)}, u32[]{:S(2)}, u32[]{:S(2)}) collective-permute-start(bf16[512,640]{1,0:T(8,128)(2,1)S(1)} %shard_map.65), channel_id=1, source_target_pairs={{0,64},{64,0},{1,65},{65,1},{2,66},{66,2},{3,67},{67,3},{4,68},{68... | collective-permute-start | bytes 1966088 | tf_op jit(solution)/shard_map/ppermute | solution.py:130
  142.5 13.9 %shard_map.64.a_ref = bf16[512,640]{1,0:T(8,128)(2,1)S(1)} custom-call(s32[97]{0:T(128)S(1)} %get-tuple-element.6.meta, bf16[8,3,128,640]{3,2,1,0:T(8,128)(2,1)} %all-to-all-done.q_ref.k_ref.v_ref, bf16[8,3,128,640]{3,2,1,0:T(8,128)(2,1)} %all-to-all-done.q_ref.k_ref.v_ref, bf16[8,3,128,640]{3,2,1,0:T(8,128)(2,1)} %all-to-all-done.q_ref.k_ref.v_ref), custom_call_target="tpu_custom_call" | custom-call | flops 503316480 | bytes 3932160 | tf_op jit(solution)/shard_map/pallas_call | solution.py:51
  156.4 0.0 copy-start.2
  156.4 0.8 copy-done.2
  157.2 0.0 collective-permute-done.b_ref
  157.2 0.0 copy-start.4
  157.2 0.9 copy-done.4
  158.1 0.0 all-gather.2.cloned.1.call-done.wa_ref.wb_ref
  158.1 0.0 copy-start.3
  158.1 1.1 copy-done.3
  159.2 0.0 copy-start.5
  159.2 1.1 copy-done.5
  160.3 12.9 %shard_map.66 = bf16[512,5120]{1,0:T(8,128)(2,1)S(1)} custom-call(s32[1]{0:T(128)} %bitcast.1.meta, bf16[512,640]{1,0:T(8,128)(2,1)S(1)} %copy-done.3, bf16[512,640]{1,0:T(8,128)(2,1)S(1)} %copy-done.5, bf16[5120,1280]{1,0:T(8,128)(2,1)} %all-gather.2.cloned.1.call-done.wa_ref.wb_ref, bf16[5120,1280]{1,0:T(8,128)(2,1)} %all-gather.2.cloned.1.call-done.wa_ref.wb_ref), custom_call_target="tpu_custom_call" | custom-call | flops 6710886400 | bytes 18350080 | tf_op jit(solution)/shard_map/pallas_call | solution.py:86
  173.2 0.0 copy-start.1
  173.2 2.3 copy-done.1
  175.5 0.0 copy-start.8
  175.5 0.0 reduce-scatter.2.cloned.1.call-update
  175.5 56.7 %reduce-scatter.2.cloned.1.call-done = bf16[128,5120]{1,0:T(8,128)(2,1)} async-done(((bf16[512,5120]{1,0:T(8,128)(2,1)}), bf16[128,5120]{1,0:T(8,128)(2,1)}) %reduce-scatter.2.cloned.1.call-update) | async-done | bytes 1310736 | tf_op jit(solution)/shard_map/reduce_scatter | solution.py:134
  232.2 0.0 copy-done.8
  232.2 2.6 %fusion = bf16[1,128,5120]{2,1,0:T(8,128)(2,1)} fusion(bf16[128,5120]{1,0:T(8,128)(2,1)} %reduce-scatter.2.cloned.1.call-done, f32[5120]{0:T(1024)S(1)} %bitcast.20), kind=kLoop, calls=%fused_computation.2 | loop fusion | flops 1966080 | bytes 2641920 | tf_op jit(solution)/shard_map/convert_element_type | solution.py:135
Async XLA Ops:
  6.5 1.9 copy-start
  6.5 151.5 %all-gather.2.cloned.1.call-start = ((), (), s32[]{:S(2)}) async-start(), calls=%async_computation.2 | async-start | bytes 13926400 | tf_op jit(solution)/shard_map/all_gather | solution.py:119
  27.5 1.8 copy-start.6
  27.6 2.2 copy-start.7
  32.0 8.0 %copy-start.9 = (s32[16,6]{0,1:T(8,128)S(1)}, s32[16,6]{0,1:T(8,128)}, u32[]{:S(2)}) copy-start(s32[16,6]{0,1:T(8,128)} %param.11) | copy-start | bytes 1156
  32.0 93.7 %all-to-all-start = ((bf16[8,3,128,640]{3,2,1,0:T(8,128)(2,1)}), bf16[8,3,128,640]{3,2,1,0:T(8,128)(2,1)}, u32[]{:S(2)}, u32[]{:S(2)}) async-start(bf16[8,3,128,640]{3,2,1,0:T(8,128)(2,1)} %pad_maximum_fusion), calls=%async_computation | async-start | bytes 7864320 | tf_op jit(solution)/shard_map/all_to_all | solution.py:125
  40.0 192.3 %reduce-scatter.2.cloned.1.call-start = ((), (), s32[]{:S(2)}) async-start(), calls=%async_computation.3 | async-start | bytes 6553600 | tf_op jit(solution)/shard_map/reduce_scatter | solution.py:134
  139.6 17.7 %collective-permute-start = (bf16[512,640]{1,0:T(8,128)(2,1)S(1)}, bf16[512,640]{1,0:T(8,128)(2,1)S(1)}, u32[]{:S(2)}, u32[]{:S(2)}) collective-permute-start(bf16[512,640]{1,0:T(8,128)(2,1)S(1)} %shard_map.65), channel_id=1, source_target_pairs={{0,64},{64,0},{1,65},{65,1},{2,66},{66,2},{3,67},{67,3},{4,68},{68... | collective-permute-start | bytes 1966088 | tf_op jit(solution)/shard_map/ppermute | solution.py:130
  156.4 0.8 copy-start.2
  157.2 0.9 copy-start.4
  158.1 1.1 copy-start.3
  159.2 1.1 copy-start.5
  173.2 2.3 copy-start.1
  175.5 56.8 %copy-start.8 = (f32[1,5120]{1,0:T(1,128)S(1)}, f32[1,5120]{1,0:T(1,128)}, u32[]{:S(2)}) copy-start(f32[1,5120]{1,0:T(1,128)} %param.10) | copy-start | bytes 61444
Sparse Core Ops, SparseCore 0:
  9.6 117.6 all-gather.1
  175.6 56.5 reduce-scatter.1

commit v2 on v1

v2 whole, which is shorter than its diff:
```python
import functools
import math

import jax
import jax.numpy as jnp
from jax import lax
from jax.experimental import pallas as pl
from jax.experimental.pallas import tpu as pltpu
from jax.sharding import Mesh
from jax.sharding import PartitionSpec as P

HEAD_DIM = 128
FRAME = 64
VMEM = 60 * 1024 * 1024
NT = (((1,), (1,)), ((), ()))


def params():
    return pltpu.CompilerParams(vmem_limit_bytes=VMEM)


def layout_kernel(q_ref, k_ref, v_ref, o_ref):
    n_y, _, rows, cols = o_ref.shape
    for y in range(n_y):
        for i, ref in enumerate((q_ref, k_ref, v_ref)):
            o_ref[y, i] = ref[:, y * cols : (y + 1) * cols]


def layout(q, k, v, n_y, n_z):
    rows, width = q.shape
    cols = width // (n_y * n_z)
    block = pl.BlockSpec((rows, n_y * cols), lambda i: (0, i))
    return pl.pallas_call(
        layout_kernel,
        grid=(n_z,),
        in_specs=[block] * 3,
        out_specs=pl.BlockSpec((n_y, None, 3, rows, cols), lambda i: (0, i, 0, 0, 0)),
        out_shape=jax.ShapeDtypeStruct((n_y, n_z, 3, rows, cols), q.dtype),
        compiler_params=params(),
        cost_estimate=pl.CostEstimate(flops=0, bytes_accessed=12 * rows * width, transcendentals=0),
    )(q, k, v)


def attend_kernel(meta, q_ref, k_ref, v_ref, o_ref, *, slots):
    blocks, rows, width = q_ref.shape
    per = rows // FRAME
    heads = width // HEAD_DIM
    n_key = slots * FRAME
    scale = 1.0 / math.sqrt(HEAD_DIM)
    lane = lax.broadcasted_iota(jnp.int32, (1, n_key), 1)
    work = []
    for r in range(blocks):
        block = lax.rem(meta[1] + r, blocks)
        for p in range(per):
            base = 2 + ((meta[0] * blocks + block) * per + p) * slots
            bias = jnp.zeros((1, n_key), jnp.float32)
            picks = []
            for s in range(slots):
                g = meta[base + s]
                inside = (lane >= s * FRAME) & (lane < (s + 1) * FRAME)
                bias = jnp.where(inside, jnp.where(g >= 0, 0.0, -1e30), bias)
                g = jnp.maximum(g, 0)
                picks.append((g // per, pl.multiple_of((g % per) * FRAME, FRAME)))
            for h in range(heads):
                work.append((r, p, slice(h * HEAD_DIM, (h + 1) * HEAD_DIM), block, picks, bias))
    scores = []
    for r, p, cols, block, picks, bias in work:
        key = jnp.concatenate([k_ref[b, pl.ds(o, FRAME), cols] for b, o in picks], 0)
        query = q_ref[block, p * FRAME : (p + 1) * FRAME, cols]
        score = lax.dot_general(query, key, NT, preferred_element_type=jnp.float32)
        scores.append(score * scale + bias)
    tops = [jnp.max(s, axis=1, keepdims=True) for s in scores]
    probs = [jnp.exp(s - t) for s, t in zip(scores, tops)]
    denoms = [jnp.sum(p, axis=1, keepdims=True) for p in probs]
    for (r, p, cols, block, picks, bias), prob, denom in zip(work, probs, denoms):
        val = jnp.concatenate([v_ref[b, pl.ds(o, FRAME), cols] for b, o in picks], 0)
        accum = jnp.dot(prob.astype(jnp.bfloat16), val, preferred_element_type=jnp.float32)
        o_ref[r, p * FRAME : (p + 1) * FRAME, cols] = (accum / denom).astype(jnp.bfloat16)


def attend(meta, parts, slots, n_y):
    blocks, _, rows, width = parts.shape
    n_z = blocks // n_y
    whole = lambda which: pl.BlockSpec((blocks, None, rows, width), lambda i, m: (0, which, 0, 0))
    work = n_z * rows * slots * FRAME * width
    return pl.pallas_call(
        functools.partial(attend_kernel, slots=slots),
        grid_spec=pltpu.PrefetchScalarGridSpec(
            num_scalar_prefetch=1,
            grid=(1,),
            in_specs=[
                pl.BlockSpec((n_z, None, rows, width), lambda i, m: (m[0], 0, 0, 0)),
                whole(1),
                whole(2),
            ],
            out_specs=pl.BlockSpec((n_z, rows, width), lambda i, m: (0, 0, 0)),
        ),
        out_shape=jax.ShapeDtypeStruct((n_z, rows, width), jnp.bfloat16),
        compiler_params=params(),
        cost_estimate=pl.CostEstimate(
            flops=work * 4, bytes_accessed=3 * blocks * rows * width * 2, transcendentals=work // HEAD_DIM
        ),
    )(meta, parts, parts, parts)


def project_kernel(meta, a_ref, b_ref, w_ref, o0, o1a, o1b, o2a, o2b, o3a, o3b):
    n_z, rows, depth = a_ref.shape
    flat = (n_z * rows, depth)
    step = pl.program_id(0)
    here = pl.ds(pl.multiple_of(meta[0] * depth, 128), depth)
    there = pl.ds(pl.multiple_of((1 - meta[0]) * depth, 128), depth)
    total = lax.dot_general(a_ref[...].reshape(flat), w_ref[:, here], NT, preferred_element_type=jnp.float32)
    total += lax.dot_general(b_ref[...].reshape(flat), w_ref[:, there], NT, preferred_element_type=jnp.float32)
    total = total.astype(jnp.bfloat16)
    o0[...] = total[:rows]

    @pl.when(step == 0)
    def _():
        o1a[...] = total[rows : 2 * rows]
        o2a[...] = total[2 * rows : 3 * rows]
        o3a[...] = total[3 * rows :]

    @pl.when(step == 1)
    def _():
        o1b[...] = total[rows : 2 * rows]
        o2b[...] = total[2 * rows : 3 * rows]
        o3b[...] = total[3 * rows :]


def project(meta, mine, other, weight_t):
    n_z, rows, depth = mine.shape
    width = weight_t.shape[0]
    tile = width // 2
    act = pl.BlockSpec((n_z, rows, depth), lambda i, m: (0, 0, 0))
    part = pl.BlockSpec((rows, tile), lambda i, m: (0, 0))
    return pl.pallas_call(
        project_kernel,
        grid_spec=pltpu.PrefetchScalarGridSpec(
            num_scalar_prefetch=1,
            grid=(2,),
            in_specs=[act, act, pl.BlockSpec((tile, 2 * depth), lambda i, m: (i, 0))],
            out_specs=[pl.BlockSpec((rows, tile), lambda i, m: (0, i))] + [part] * 6,
        ),
        out_shape=[jax.ShapeDtypeStruct((rows, width), jnp.bfloat16)]
        + [jax.ShapeDtypeStruct((rows, tile), jnp.bfloat16)] * 6,
        compiler_params=params(),
        cost_estimate=pl.CostEstimate(
            flops=4 * n_z * rows * depth * width,
            bytes_accessed=4 * depth * width + 2 * n_z * rows * width,
            transcendentals=0,
        ),
    )(meta, mine, other, weight_t)


def add_kernel(a_ref, b_ref, o_ref):
    o_ref[...] = (a_ref[...].astype(jnp.float32) + b_ref[...].astype(jnp.float32)).astype(o_ref.dtype)


def add(a, b):
    return pl.pallas_call(
        add_kernel,
        out_shape=jax.ShapeDtypeStruct(a.shape, a.dtype),
        compiler_params=params(),
        cost_estimate=pl.CostEstimate(flops=a.size, bytes_accessed=6 * a.size, transcendentals=0),
    )(a, b)


def finish_kernel(meta, gate_ref, *refs):
    o_ref = refs[-1]
    width = o_ref.shape[2] // 2
    early = pl.program_id(0) < pl.num_programs(0) // 2
    for part in range(2):
        own, low_a, low_b, high_a, high_b = (r[...].astype(jnp.float32) for r in refs[5 * part : 5 * part + 5])
        total = own + jnp.where(early, low_a, low_b) + jnp.where(early, high_a, high_b)
        total = total.astype(jnp.bfloat16).astype(jnp.float32)
        y = meta[0] if part == 0 else 1 - meta[0]
        cols = pl.ds(pl.multiple_of(y * width, 128), width)
        o_ref[0, :, cols] = (gate_ref[:, cols] * total).astype(o_ref.dtype)


def finish(meta, gate, parts):
    rows, width = parts[0][0].shape
    steps = 4
    tile = width // steps
    half = [pl.BlockSpec((rows, tile), lambda i, m: (0, jnp.minimum(i, steps // 2 - 1)))]
    half += [pl.BlockSpec((rows, tile), lambda i, m: (0, jnp.maximum(i - steps // 2, 0)))]
    args, specs = [], []
    for own, low, high in parts:
        args += [own, *low, *high]
        specs += [pl.BlockSpec((rows, tile), lambda i, m: (0, i))] + half + half
    return pl.pallas_call(
        finish_kernel,
        grid_spec=pltpu.PrefetchScalarGridSpec(
            num_scalar_prefetch=1,
            grid=(steps,),
            in_specs=[pl.BlockSpec((1, 2 * tile), lambda i, m: (0, i))] + specs,
            out_specs=pl.BlockSpec((1, rows, 2 * tile), lambda i, m: (0, 0, i)),
        ),
        out_shape=jax.ShapeDtypeStruct((1, rows, 2 * width), jnp.bfloat16),
        compiler_params=params(),
    )(meta, gate, *args)


def local(queries, keys, values, out_weight, gate, kv_frames):
    rows, width = queries.shape[1:]
    n_y, n_z = lax.axis_size("yh"), lax.axis_size("z")
    n_l = lax.axis_size("yl")
    n = n_y * n_z
    cols = width // n
    slots = kv_frames.shape[1]
    my_y, my_z, my_l = (lax.axis_index(a).astype(jnp.int32) for a in ("yh", "z", "yl"))

    def shift(array, axes, size, by):
        return lax.ppermute(array, axes, [(i, (i + by) % size) for i in range(size)])

    parts = layout(queries[0], keys[0], values[0], n_y, n_z).reshape(n, 3, rows, cols)
    parts = lax.all_to_all(parts, ("yh", "z"), 0, 0, tiled=True)

    weight = lax.dynamic_slice_in_dim(out_weight, my_z * (n_y * cols), n_y * cols, 0).T
    split = weight.shape[0] // 2
    ring = n_y * n_l
    far = jnp.concatenate(
        [shift(weight[:split], ("yh", "yl"), ring, 1), shift(weight[split:], ("yh", "yl"), ring, ring - 1)], 0
    )
    weight_near = lax.all_gather(weight, ("x", "c"), axis=0, tiled=True)
    weight_far = lax.all_gather(far, ("x", "c"), axis=0, tiled=True)

    table = kv_frames.reshape(-1)
    meta = lambda y: jnp.concatenate([jnp.stack([y, my_z]), table])
    theirs = attend(meta(1 - my_y), parts, slots, n_y)
    other = shift(theirs, "yh", n_y, 1)
    mine = attend(meta(my_y), parts, slots, n_y)

    up = lambda array: shift(array, "z", n_z, 1)
    down = lambda array: shift(array, "z", n_z, n_z - 1)
    sums = []
    for piece in (weight_near, weight_far):
        o0, o1a, o1b, o2a, o2b, o3a, o3b = project(my_y[None], mine, other, piece)
        relay_a, relay_b = up(o2a), down(o2b)
        low_b, high_a = up(o1b), down(o3a)
        low_a, high_b = up(add(o1a, relay_a)), down(add(o3b, relay_b))
        sums.append((o0, (low_a, low_b), (high_a, high_b)))
    return finish(my_l[None], gate, sums)


def solution(mesh):
    fine = Mesh(mesh.devices.reshape(2, 4, 4, 2, 2), ("yh", "z", "x", "yl", "c"))
    frame, batch = ("yh", "z"), ("x", "yl", "c")
    act = P(batch, frame, None)
    return jax.shard_map(
        local,
        mesh=fine,
        in_specs=(act, act, act, P(None, batch), P(batch, None), P()),
        out_specs=act,
        check_vma=False,
    )
```

time: 244 us -> 177 us (0.73)
  waiting for transfers between devices: 142 us -> 83.3 us
  local copies, waits for them, and re-layouts: 29.5 us -> 4.35 us
  starting transfers between devices: 10.9 us -> 26.5 us
  Pallas kernels: 40.7 us -> 45.5 us
  other arithmetic: 4.89 us -> 1.58 us
    reduce_scatter x1 -> x0, waiting for transfers between devices: 56.7 us -> none  [local(): total = lax.psum_scatter(partial, 'z', scatter_dimension=0, tiled=True)]
    all_to_all x1, waiting for transfers between devices: 85.5 us -> 43.6 us  [local(): parts = lax.all_to_all(parts, ('yh', 'z'), 0, 0, tiled=True)]
    ppermute x1 -> x15, waiting for transfers between devices: 0.01 us -> 39.6 us  [shift(): lax.ppermute(array, axes, [(i, (i + by) % size) for i in range(size)])]
    another operation x6 -> x0, local copies, waits for them, and re-layouts: 19.8 us -> none  [blocks(): array[0].reshape(rows, n_z, n_y, cols).transpose(2, 1, 0, 3)]
    ppermute x1 -> x15, starting transfers between devices: 2.9 us -> 18.1 us  [shift(): lax.ppermute(array, axes, [(i, (i + by) % size) for i in range(size)])]
    unnamed x21 -> x9, local copies, waits for them, and re-layouts: 8.68 us -> 2.13 us
    pallas_call x1 -> x2, Pallas kernels: 12.9 us -> 16.7 us  [project(): pl.pallas_call(project_kernel, grid_spec=pltpu.PrefetchScalarGridSpec(num...]
    convert_element_type x1 -> x0, other arithmetic: 2.63 us -> none  [local(): (gate[:, None, :] * total[None].astype(jnp.float32)).astype(jnp.bfloat16)]
  transfers between devices with their start and end apart: 4 -> 18, of which waited for: 2 -> 8; matrix products, arithmetic and copies ran while one was open for 9% -> 2% of each run, Pallas kernels for 11% -> 23%
where the time goes in v2:
time: 177 us; the launch traced here: 175 us
  waiting for transfers between devices  83.3 us (47%)
  Pallas kernels  45.5 us (26%)
  starting transfers between devices  26.5 us (15%)
  between operations  13.4 us (8%)
  local copies, waits for them, and re-layouts  4.35 us (2%)
    all_to_all x1, waiting for transfers between devices, local(): parts = lax.all_to_all(parts, ('yh', 'z'), 0, 0, tiled=True)  43.6 us
    ppermute x15, waiting for transfers between devices, shift(): lax.ppermute(array, axes, [(i, (i + by) % size) for i in range(size)])  39.6 us
    ppermute x15, starting transfers between devices, shift(): lax.ppermute(array, axes, [(i, (i + by) % size) for i in range(size)])  18.1 us
    pallas_call x2, Pallas kernels, project(): pl.pallas_call(project_kernel, grid_spec=pltpu.PrefetchScalarGridSpec(num...  16.7 us
    pallas_call x2, Pallas kernels, attend(): pl.pallas_call(functools.partial(attend_kernel, slots=slots), grid_spec=p...  11.9 us
    all_to_all x1, starting transfers between devices, local(): parts = lax.all_to_all(parts, ('yh', 'z'), 0, 0, tiled=True)  8.41 us
    pallas_call x4, Pallas kernels, add(): pl.pallas_call(add_kernel, out_shape=jax.ShapeDtypeStruct(a.shape, a.dtyp...  7.5 us
    pallas_call x1, Pallas kernels, finish(): pl.pallas_call(finish_kernel, grid_spec=pltpu.PrefetchScalarGridSpec(num_...  4.92 us
  transfers between devices with their start and end apart: 18, of which 8 were waited for; matrix products, arithmetic and copies ran while one was open for 2% of the time, Pallas kernels for 23%

profile of v2, /device:TPU:24, one launch (start us, length us, event | category | flops | bytes accessed | tf_op | source)
XLA Modules:
  0.0 174.7 jit_solution(7015085664930436465)
XLA Ops:
  6.5 0.0 copy-start
  6.5 0.0 all-gather.3.cloned.1.call-start
  6.5 1.9 %copy-done = bf16[5120,320]{0,1:T(8,128)(2,1)S(1)} copy-done((bf16[5120,320]{0,1:T(8,128)(2,1)S(1)}, bf16[5120,320]{0,1:T(8,128)(2,1)}, u32[]{:S(2)}) %copy-start) | copy-done | bytes 3276824
  8.5 1.0 dynamic-slice_bitcast_fusion
  9.4 0.0 all-gather.3.cloned.1.call-update
  9.4 0.0 all-gather.5.cloned.1.call-start
  9.5 1.2 fusion
  10.7 0.8 collective-permute-start.8
  11.5 2.5 %collective-permute-start.7 = (bf16[160,1280]{1,0:T(8,128)(2,1)S(1)}, bf16[160,1280]{1,0:T(8,128)(2,1)S(1)}, u32[]{:S(2)}, u32[]{:S(2)}) collective-permute-start(bf16[160,1280]{1,0:T(8,128)(2,1)S(1)} %get-tuple-element.33), channel_id=1, source_target_pairs={{0,2},{2,64},{64,66},{66,0},{1,3},{3,65},{65,67},{67,1},{4,6},{6,6... | collective-permute-start | bytes 1228808 | tf_op jit(solution)/shard_map/ppermute | solution.py:214
  14.0 9.2 %collective-permute-done.8 = bf16[160,1280]{1,0:T(8,128)(2,1)S(1)} collective-permute-done((bf16[160,1280]{1,0:T(8,128)(2,1)S(1)}, bf16[160,1280]{1,0:T(8,128)(2,1)S(1)}, u32[]{:S(2)}, u32[]{:S(2)}) %collective-permute-start.8) | collective-permute-done | bytes 409632 | tf_op jit(solution)/shard_map/ppermute | solution.py:214
  23.2 0.0 collective-permute-done.7
  23.2 1.0 pad_maximum_fusion
  24.1 0.0 all-gather.5.cloned.1.call-update
  24.2 4.6 %shard_map.64 = bf16[2,4,3,128,640]{4,3,2,1,0:T(8,128)(2,1)} custom-call(bf16[128,5120]{1,0:T(8,128)(2,1)} %bitcast.11, bf16[128,5120]{1,0:T(8,128)(2,1)} %bitcast.12, bf16[128,5120]{1,0:T(8,128)(2,1)} %bitcast.13), custom_call_target="tpu_custom_call" | custom-call | bytes 7864320 | tf_op jit(solution)/shard_map/pallas_call | solution.py:33
  28.7 0.0 copy-start.3
  28.7 8.4 %all-to-all-start = ((bf16[8,3,128,640]{3,2,1,0:T(8,128)(2,1)}), bf16[8,3,128,640]{3,2,1,0:T(8,128)(2,1)}, u32[]{:S(2)}, u32[]{:S(2)}) async-start(bf16[8,3,128,640]{3,2,1,0:T(8,128)(2,1)} %bitcast.10), calls=%async_computation | async-start | bytes 7864320 | tf_op jit(solution)/shard_map/all_to_all | solution.py:217
  37.2 0.0 copy-done.3
  37.2 0.1 copy.8
  37.2 0.1 reshape.6
  37.3 0.6 add_add_fusion.1
  37.9 43.6 %all-to-all-done.q_ref.k_ref.v_ref = bf16[8,3,128,640]{3,2,1,0:T(8,128)(2,1)} async-done(((bf16[8,3,128,640]{3,2,1,0:T(8,128)(2,1)}), bf16[8,3,128,640]{3,2,1,0:T(8,128)(2,1)}, u32[]{:S(2)}, u32[]{:S(2)}) %all-to-all-start) | async-done | bytes 3932192 | tf_op jit(solution)/shard_map/all_to_all | solution.py:217
  81.5 5.9 %shard_map.66 = bf16[4,128,640]{2,1,0:T(8,128)(2,1)} custom-call(s32[98]{0:T(128)} %get-tuple-element.35.meta, bf16[8,3,128,640]{3,2,1,0:T(8,128)(2,1)} %all-to-all-done.q_ref.k_ref.v_ref, bf16[8,3,128,640]{3,2,1,0:T(8,128)(2,1)} %all-to-all-done.q_ref.k_ref.v_ref, bf16[8,3,128,640]{3,2,1,0:T(8,128)(2,1)} %all-to-all-done.q_ref.k_ref.v_ref), custom_call_target="tpu_custom_call" | custom-call | flops 503316480 | bytes 3932160 | tf_op jit(solution)/shard_map/pallas_call | solution.py:86
  87.4 1.0 collective-permute-start
  88.4 6.0 %shard_map.65.a_ref = bf16[4,128,640]{2,1,0:T(8,128)(2,1)} custom-call(s32[98]{0:T(128)} %get-tuple-element.36.meta, bf16[8,3,128,640]{3,2,1,0:T(8,128)(2,1)} %all-to-all-done.q_ref.k_ref.v_ref, bf16[8,3,128,640]{3,2,1,0:T(8,128)(2,1)} %all-to-all-done.q_ref.k_ref.v_ref, bf16[8,3,128,640]{3,2,1,0:T(8,128)(2,1)} %all-to-all-done.q_ref.k_ref.v_ref), custom_call_target="tpu_custom_call" | custom-call | flops 503316480 | bytes 3932160 | tf_op jit(solution)/shard_map/pallas_call | solution.py:86
  94.3 11.2 %collective-permute-done.b_ref = bf16[4,128,640]{2,1,0:T(8,128)(2,1)} collective-permute-done((bf16[4,128,640]{2,1,0:T(8,128)(2,1)}, bf16[4,128,640]{2,1,0:T(8,128)(2,1)}, u32[]{:S(2)}, u32[]{:S(2)}) %collective-permute-start) | collective-permute-done | bytes 655392 | tf_op jit(solution)/shard_map/ppermute | solution.py:214
  105.5 0.0 all-gather.3.cloned.1.call-done.w_ref
  105.5 8.3 %shard_map.67 = (bf16[128,2560]{1,0:T(8,128)(2,1)}, bf16[128,1280]{1,0:T(8,128)(2,1)}, bf16[128,1280]{1,0:T(8,128)(2,1)}, bf16[128,1280]{1,0:T(8,128)(2,1)}, bf1...) custom-call(s32[1]{0:T(128)} %bitcast.1.meta, bf16[4,128,640]{2,1,0:T(8,128)(2,1)} %shard_map.65.a_ref, ...), custom_call_target="tpu_custom_call" | custom-call | flops 3355443200 | bytes 9175040 | tf_op jit(solution)/shard_map/pallas_call | solution.py:136
  113.9 1.2 collective-permute-start.1
  115.1 2.0 %collective-permute-start.5 = (bf16[128,1280]{1,0:T(8,128)(2,1)}, bf16[128,1280]{1,0:T(8,128)(2,1)}, u32[]{:S(2)}, u32[]{:S(2)}) collective-permute-start(bf16[128,1280]{1,0:T(8,128)(2,1)} %get-tuple-element.25), channel_id=1, source_target_pairs={{0,48},{16,0},{32,16},{48,32},{1,49},{17,1},{33,17},{49,33},{2,50}... | collective-permute-start | bytes 983048 | tf_op jit(solution)/shard_map/ppermute | solution.py:214
  117.1 0.0 all-gather.5.cloned.1.call-done.w_ref
  117.1 8.3 %shard_map.70 = (bf16[128,2560]{1,0:T(8,128)(2,1)}, bf16[128,1280]{1,0:T(8,128)(2,1)}, bf16[128,1280]{1,0:T(8,128)(2,1)}, bf16[128,1280]{1,0:T(8,128)(2,1)}, bf1...) custom-call(s32[1]{0:T(128)} %bitcast.1.meta, bf16[4,128,640]{2,1,0:T(8,128)(2,1)} %shard_map.65.a_ref, ...), custom_call_target="tpu_custom_call" | custom-call | flops 3355443200 | bytes 9175040 | tf_op jit(solution)/shard_map/pallas_call | solution.py:136
  125.5 0.0 collective-permute-start.9
  125.5 3.2 %collective-permute-start.13 = (bf16[128,1280]{1,0:T(8,128)(2,1)}, bf16[128,1280]{1,0:T(8,128)(2,1)S(1)}, u32[]{:S(2)}, u32[]{:S(2)}) collective-permute-start(bf16[128,1280]{1,0:T(8,128)(2,1)} %get-tuple-element.32), channel_id=1, source_target_pairs={{0,48},{16,0},{32,16},{48,32},{1,49},{17,1},{33,17},{49,33},{2,50}... | collective-permute-start | bytes 983048 | tf_op jit(solution)/shard_map/ppermute | solution.py:214
  128.7 0.0 collective-permute-start.3
  128.7 0.0 collective-permute-done.1.b_ref
  128.7 3.2 %collective-permute-start.4 = (bf16[128,1280]{1,0:T(8,128)(2,1)}, bf16[128,1280]{1,0:T(8,128)(2,1)}, u32[]{:S(2)}, u32[]{:S(2)}) collective-permute-start(bf16[128,1280]{1,0:T(8,128)(2,1)} %get-tuple-element.23), channel_id=1, source_target_pairs={{0,48},{16,0},{32,16},{48,32},{1,49},{17,1},{33,17},{49,33},{2,50}... | collective-permute-start | bytes 983048 | tf_op jit(solution)/shard_map/ppermute | solution.py:214
  132.0 1.9 %shard_map.68 = bf16[128,1280]{1,0:T(8,128)(2,1)} custom-call(bf16[128,1280]{1,0:T(8,128)(2,1)} %get-tuple-element.20.a_ref, bf16[128,1280]{1,0:T(8,128)(2,1)} %collective-permute-done.1.b_ref), custom_call_target="tpu_custom_call" | custom-call | flops 163840 | bytes 983040 | tf_op jit(solution)/shard_map/pallas_call | solution.py:160
  133.8 0.0 collective-permute-done.5.b_ref
  133.8 0.0 collective-permute-start.2
  133.8 1.9 %shard_map.69 = bf16[128,1280]{1,0:T(8,128)(2,1)} custom-call(bf16[128,1280]{1,0:T(8,128)(2,1)} %get-tuple-element.24.a_ref, bf16[128,1280]{1,0:T(8,128)(2,1)} %collective-permute-done.5.b_ref), custom_call_target="tpu_custom_call" | custom-call | flops 163840 | bytes 983040 | tf_op jit(solution)/shard_map/pallas_call | solution.py:160
  135.7 1.8 %collective-permute-done.9.b_ref = bf16[128,1280]{1,0:T(8,128)(2,1)S(1)} collective-permute-done((bf16[128,1280]{1,0:T(8,128)(2,1)}, bf16[128,1280]{1,0:T(8,128)(2,1)S(1)}, u32[]{:S(2)}, u32[]{:S(2)}) %collective-permute-start.9) | collective-permute-done | bytes 327712 | tf_op jit(solution)/shard_map/ppermute | solution.py:214
  137.6 0.0 copy-start.2
  137.6 1.4 collective-permute-start.6
  139.0 0.0 copy-done.2
  139.0 1.9 %shard_map.71 = bf16[128,1280]{1,0:T(8,128)(2,1)} custom-call(bf16[128,1280]{1,0:T(8,128)(2,1)} %get-tuple-element.27.a_ref, bf16[128,1280]{1,0:T(8,128)(2,1)} %copy-done.2), custom_call_target="tpu_custom_call" | custom-call | flops 163840 | bytes 983040 | tf_op jit(solution)/shard_map/pallas_call | solution.py:160
  140.8 0.0 collective-permute-done.13.b_ref
  140.8 0.0 copy-start.1
  140.8 0.6 collective-permute-start.11
  141.5 0.1 copy-done.1
  141.6 1.9 %shard_map.72 = bf16[128,1280]{1,0:T(8,128)(2,1)} custom-call(bf16[128,1280]{1,0:T(8,128)(2,1)} %get-tuple-element.31.a_ref, bf16[128,1280]{1,0:T(8,128)(2,1)} %copy-done.1), custom_call_target="tpu_custom_call" | custom-call | flops 163840 | bytes 983040 | tf_op jit(solution)/shard_map/pallas_call | solution.py:160
  143.5 1.2 collective-permute-done.3.refs_2_
  144.7 1.3 collective-permute-start.12
  146.0 0.0 collective-permute-done.4.refs_3_
  146.0 0.7 collective-permute-start.10
  146.7 5.0 %collective-permute-done.2.refs_1_ = bf16[128,1280]{1,0:T(8,128)(2,1)} collective-permute-done((bf16[128,1280]{1,0:T(8,128)(2,1)}, bf16[128,1280]{1,0:T(8,128)(2,1)}, u32[]{:S(2)}, u32[]{:S(2)}) %collective-permute-start.2) | collective-permute-done | bytes 327712 | tf_op jit(solution)/shard_map/ppermute | solution.py:214
  151.7 0.0 collective-permute-start.14
  151.7 0.0 collective-permute-done.6.refs_4_
  151.7 7.0 %collective-permute-done.11.refs_7_ = bf16[128,1280]{1,0:T(8,128)(2,1)} collective-permute-done((bf16[128,1280]{1,0:T(8,128)(2,1)}, bf16[128,1280]{1,0:T(8,128)(2,1)}, u32[]{:S(2)}, u32[]{:S(2)}) %collective-permute-start.11) | collective-permute-done | bytes 327712 | tf_op jit(solution)/shard_map/ppermute | solution.py:214
  158.7 0.0 collective-permute-done.12.refs_8_
  158.7 4.2 %collective-permute-done.10.refs_6_ = bf16[128,1280]{1,0:T(8,128)(2,1)} collective-permute-done((bf16[128,1280]{1,0:T(8,128)(2,1)}, bf16[128,1280]{1,0:T(8,128)(2,1)}, u32[]{:S(2)}, u32[]{:S(2)}) %collective-permute-start.10) | collective-permute-done | bytes 327712 | tf_op jit(solution)/shard_map/ppermute | solution.py:214
  162.9 0.0 collective-permute-done.14.refs_9_
  162.9 4.9 %shard_map.73 = bf16[1,128,5120]{2,1,0:T(8,128)(2,1)} custom-call(s32[1]{0:T(128)} %bitcast.meta, f32[1,5120]{1,0:T(1,128)} %gate_ref.1, bf16[128,2560]{1,0:T(8,128)(2,1)} %get-tuple-element.19.refs_0_, bf16[128,1280]{1,0:T(8,128)(2,1)} %collective-permute-done.2.refs_1_, bf16[128,1280]{1,0:T(8,128)(2,1)} %collective-permute-done.3.refs_2_, ...), custom_call_target="tpu_custom_call" | custom-call | tf_op jit(solution)/shard_map/pallas_call | solution.py:191
Async XLA Ops:
  6.5 1.9 %copy-start = (bf16[5120,320]{0,1:T(8,128)(2,1)S(1)}, bf16[5120,320]{0,1:T(8,128)(2,1)}, u32[]{:S(2)}) copy-start(bf16[5120,320]{0,1:T(8,128)(2,1)} %param.9) | copy-start | bytes 9830404
  6.5 99.0 %all-gather.3.cloned.1.call-start = ((), (), s32[]{:S(2)}) async-start(), calls=%async_computation.1 | async-start | bytes 7372800 | tf_op jit(solution)/shard_map/all_gather | solution.py:225
  9.4 107.7 %all-gather.5.cloned.1.call-start = ((), (), s32[]{:S(2)}) async-start(), calls=%async_computation.2 | async-start | bytes 7372800 | tf_op jit(solution)/shard_map/all_gather | solution.py:226
  10.7 12.5 %collective-permute-start.8 = (bf16[160,1280]{1,0:T(8,128)(2,1)S(1)}, bf16[160,1280]{1,0:T(8,128)(2,1)S(1)}, u32[]{:S(2)}, u32[]{:S(2)}) collective-permute-start(bf16[160,1280]{1,0:T(8,128)(2,1)S(1)} %get-tuple-element.34), channel_id=1, source_target_pairs={{0,66},{2,0},{64,2},{66,64},{1,67},{3,1},{65,3},{67,65},{4,70},{6,... | collective-permute-start | bytes 1228808 | tf_op jit(solution)/shard_map/ppermute | solution.py:214
  11.5 11.7 %collective-permute-start.7 = (bf16[160,1280]{1,0:T(8,128)(2,1)S(1)}, bf16[160,1280]{1,0:T(8,128)(2,1)S(1)}, u32[]{:S(2)}, u32[]{:S(2)}) collective-permute-start(bf16[160,1280]{1,0:T(8,128)(2,1)S(1)} %get-tuple-element.33), channel_id=1, source_target_pairs={{0,2},{2,64},{64,66},{66,0},{1,3},{3,65},{65,67},{67,1},{4,6},{6,6... | collective-permute-start | bytes 1228808 | tf_op jit(solution)/shard_map/ppermute | solution.py:214
  28.7 8.4 %copy-start.3 = (s32[16,6]{0,1:T(8,128)S(1)}, s32[16,6]{0,1:T(8,128)}, u32[]{:S(2)}) copy-start(s32[16,6]{0,1:T(8,128)} %param.11) | copy-start | bytes 1156
  28.7 52.8 %all-to-all-start = ((bf16[8,3,128,640]{3,2,1,0:T(8,128)(2,1)}), bf16[8,3,128,640]{3,2,1,0:T(8,128)(2,1)}, u32[]{:S(2)}, u32[]{:S(2)}) async-start(bf16[8,3,128,640]{3,2,1,0:T(8,128)(2,1)} %bitcast.10), calls=%async_computation | async-start | bytes 7864320 | tf_op jit(solution)/shard_map/all_to_all | solution.py:217
  87.4 18.1 %collective-permute-start = (bf16[4,128,640]{2,1,0:T(8,128)(2,1)}, bf16[4,128,640]{2,1,0:T(8,128)(2,1)}, u32[]{:S(2)}, u32[]{:S(2)}) collective-permute-start(bf16[4,128,640]{2,1,0:T(8,128)(2,1)} %shard_map.66), channel_id=1, source_target_pairs={{0,64},{64,0},{1,65},{65,1},{2,66},{66,2},{3,67},{67,3},{4,68},{68... | collective-permute-start | bytes 1966088 | tf_op jit(solution)/shard_map/ppermute | solution.py:214
  113.9 14.9 %collective-permute-start.1 = (bf16[128,1280]{1,0:T(8,128)(2,1)}, bf16[128,1280]{1,0:T(8,128)(2,1)}, u32[]{:S(2)}, u32[]{:S(2)}) collective-permute-start(bf16[128,1280]{1,0:T(8,128)(2,1)} %get-tuple-element.21), channel_id=1, source_target_pairs={{0,16},{16,32},{32,48},{48,0},{1,17},{17,33},{33,49},{49,1},{2,18}... | collective-permute-start | bytes 983048 | tf_op jit(solution)/shard_map/ppermute | solution.py:214
  115.1 18.7 %collective-permute-start.5 = (bf16[128,1280]{1,0:T(8,128)(2,1)}, bf16[128,1280]{1,0:T(8,128)(2,1)}, u32[]{:S(2)}, u32[]{:S(2)}) collective-permute-start(bf16[128,1280]{1,0:T(8,128)(2,1)} %get-tuple-element.25), channel_id=1, source_target_pairs={{0,48},{16,0},{32,16},{48,32},{1,49},{17,1},{33,17},{49,33},{2,50}... | collective-permute-start | bytes 983048 | tf_op jit(solution)/shard_map/ppermute | solution.py:214
  125.5 12.1 %collective-permute-start.9 = (bf16[128,1280]{1,0:T(8,128)(2,1)}, bf16[128,1280]{1,0:T(8,128)(2,1)S(1)}, u32[]{:S(2)}, u32[]{:S(2)}) collective-permute-start(bf16[128,1280]{1,0:T(8,128)(2,1)} %get-tuple-element.28), channel_id=1, source_target_pairs={{0,16},{16,32},{32,48},{48,0},{1,17},{17,33},{33,49},{49,1},{2,18}... | collective-permute-start | bytes 983048 | tf_op jit(solution)/shard_map/ppermute | solution.py:214
  125.5 15.3 %collective-permute-start.13 = (bf16[128,1280]{1,0:T(8,128)(2,1)}, bf16[128,1280]{1,0:T(8,128)(2,1)S(1)}, u32[]{:S(2)}, u32[]{:S(2)}) collective-permute-start(bf16[128,1280]{1,0:T(8,128)(2,1)} %get-tuple-element.32), channel_id=1, source_target_pairs={{0,48},{16,0},{32,16},{48,32},{1,49},{17,1},{33,17},{49,33},{2,50}... | collective-permute-start | bytes 983048 | tf_op jit(solution)/shard_map/ppermute | solution.py:214
  128.7 16.0 %collective-permute-start.3 = (bf16[128,1280]{1,0:T(8,128)(2,1)}, bf16[128,1280]{1,0:T(8,128)(2,1)}, u32[]{:S(2)}, u32[]{:S(2)}) collective-permute-start(bf16[128,1280]{1,0:T(8,128)(2,1)} %get-tuple-element.22), channel_id=1, source_target_pairs={{0,16},{16,32},{32,48},{48,0},{1,17},{17,33},{33,49},{49,1},{2,18}... | collective-permute-start | bytes 983048 | tf_op jit(solution)/shard_map/ppermute | solution.py:214
  128.7 17.2 %collective-permute-start.4 = (bf16[128,1280]{1,0:T(8,128)(2,1)}, bf16[128,1280]{1,0:T(8,128)(2,1)}, u32[]{:S(2)}, u32[]{:S(2)}) collective-permute-start(bf16[128,1280]{1,0:T(8,128)(2,1)} %get-tuple-element.23), channel_id=1, source_target_pairs={{0,48},{16,0},{32,16},{48,32},{1,49},{17,1},{33,17},{49,33},{2,50}... | collective-permute-start | bytes 983048 | tf_op jit(solution)/shard_map/ppermute | solution.py:214
  133.8 17.9 %collective-permute-start.2 = (bf16[128,1280]{1,0:T(8,128)(2,1)}, bf16[128,1280]{1,0:T(8,128)(2,1)}, u32[]{:S(2)}, u32[]{:S(2)}) collective-permute-start(bf16[128,1280]{1,0:T(8,128)(2,1)} %shard_map.68), channel_id=1, source_target_pairs={{0,16},{16,32},{32,48},{48,0},{1,17},{17,33},{33,49},{49,1},{2,18}... | collective-permute-start | bytes 983048 | tf_op jit(solution)/shard_map/ppermute | solution.py:214
  137.6 1.4 copy-start.2
  137.6 14.2 %collective-permute-start.6 = (bf16[128,1280]{1,0:T(8,128)(2,1)}, bf16[128,1280]{1,0:T(8,128)(2,1)}, u32[]{:S(2)}, u32[]{:S(2)}) collective-permute-start(bf16[128,1280]{1,0:T(8,128)(2,1)} %shard_map.69), channel_id=1, source_target_pairs={{0,48},{16,0},{32,16},{48,32},{1,49},{17,1},{33,17},{49,33},{2,50}... | collective-permute-start | bytes 983048 | tf_op jit(solution)/shard_map/ppermute | solution.py:214
  140.8 0.7 copy-start.1
  140.8 17.9 %collective-permute-start.11 = (bf16[128,1280]{1,0:T(8,128)(2,1)}, bf16[128,1280]{1,0:T(8,128)(2,1)}, u32[]{:S(2)}, u32[]{:S(2)}) collective-permute-start(bf16[128,1280]{1,0:T(8,128)(2,1)} %get-tuple-element.29), channel_id=1, source_target_pairs={{0,16},{16,32},{32,48},{48,0},{1,17},{17,33},{33,49},{49,1},{2,18}... | collective-permute-start | bytes 983048 | tf_op jit(solution)/shard_map/ppermute | solution.py:214
  144.7 14.0 %collective-permute-start.12 = (bf16[128,1280]{1,0:T(8,128)(2,1)}, bf16[128,1280]{1,0:T(8,128)(2,1)}, u32[]{:S(2)}, u32[]{:S(2)}) collective-permute-start(bf16[128,1280]{1,0:T(8,128)(2,1)} %get-tuple-element.30), channel_id=1, source_target_pairs={{0,48},{16,0},{32,16},{48,32},{1,49},{17,1},{33,17},{49,33},{2,50}... | collective-permute-start | bytes 983048 | tf_op jit(solution)/shard_map/ppermute | solution.py:214
  146.0 16.9 %collective-permute-start.10 = (bf16[128,1280]{1,0:T(8,128)(2,1)}, bf16[128,1280]{1,0:T(8,128)(2,1)}, u32[]{:S(2)}, u32[]{:S(2)}) collective-permute-start(bf16[128,1280]{1,0:T(8,128)(2,1)} %shard_map.71), channel_id=1, source_target_pairs={{0,16},{16,32},{32,48},{48,0},{1,17},{17,33},{33,49},{49,1},{2,18}... | collective-permute-start | bytes 983048 | tf_op jit(solution)/shard_map/ppermute | solution.py:214
  151.7 11.2 %collective-permute-start.14 = (bf16[128,1280]{1,0:T(8,128)(2,1)}, bf16[128,1280]{1,0:T(8,128)(2,1)}, u32[]{:S(2)}, u32[]{:S(2)}) collective-permute-start(bf16[128,1280]{1,0:T(8,128)(2,1)} %shard_map.72), channel_id=1, source_target_pairs={{0,48},{16,0},{32,16},{48,32},{1,49},{17,1},{33,17},{49,33},{2,50}... | collective-permute-start | bytes 983048 | tf_op jit(solution)/shard_map/ppermute | solution.py:214
Sparse Core Ops, SparseCore 0:
  9.6 44.0 all-gather.2
  55.4 42.0 all-gather.4

commit v3 on v2

--- a/solution.py
+++ b/solution.py
@@ -103,102 +103,191 @@
     )(meta, parts, parts, parts)
 
 
-def project_kernel(meta, a_ref, b_ref, w_ref, o0, o1a, o1b, o2a, o2b, o3a, o3b):
+def own_kernel(meta, a_ref, w_ref, o_ref):
+    n_z, rows, depth = a_ref.shape
+    act = a_ref[...].reshape(n_z * rows, depth)
+    o_ref[...] = lax.dot_general(act, w_ref[...], NT, preferred_element_type=jnp.float32)
+
+
+def project_own(meta, mine, weight_t, tile=640):
+    n_z, rows, depth = mine.shape
+    width = weight_t.shape[0]
+    return pl.pallas_call(
+        own_kernel,
+        grid_spec=pltpu.PrefetchScalarGridSpec(
+            num_scalar_prefetch=1,
+            grid=(width // tile,),
+            in_specs=[
+                pl.BlockSpec((n_z, rows, depth), lambda i, m: (0, 0, 0)),
+                pl.BlockSpec((tile, depth), lambda i, m: (i, m[0])),
+            ],
+            out_specs=pl.BlockSpec((n_z * rows, tile), lambda i, m: (0, i)),
+        ),
+        out_shape=jax.ShapeDtypeStruct((n_z * rows, width), jnp.float32),
+        compiler_params=params(),
+        cost_estimate=pl.CostEstimate(
+            flops=2 * n_z * rows * depth * width,
+            bytes_accessed=2 * depth * width + 4 * n_z * rows * width,
+            transcendentals=0,
+        ),
+    )(meta, mine, weight_t)
+
+
+def project_kernel(meta, *refs, with_own):
+    if with_own:
+        base_ref, a_ref, w_ref, stay, up, down, up_late, down_late = refs
+    else:
+        m_ref, a_ref, w_ref, stay, up, down, up_late, down_late, act = refs
     n_z, rows, depth = a_ref.shape
     flat = (n_z * rows, depth)
-    step = pl.program_id(0)
-    here = pl.ds(pl.multiple_of(meta[0] * depth, 128), depth)
-    there = pl.ds(pl.multiple_of((1 - meta[0]) * depth, 128), depth)
-    total = lax.dot_general(a_ref[...].reshape(flat), w_ref[:, here], NT, preferred_element_type=jnp.float32)
-    total += lax.dot_general(b_ref[...].reshape(flat), w_ref[:, there], NT, preferred_element_type=jnp.float32)
+    step, half = pl.program_id(0), pl.num_programs(0) // 2
+    if with_own:
+        total = base_ref[...] + lax.dot_general(
+            a_ref[...].reshape(flat), w_ref[...], NT, preferred_element_type=jnp.float32
+        )
+    else:
+
+        @pl.when(step == 0)
+        def _():
+            act[:, pl.ds(pl.multiple_of(meta[0] * depth, 128), depth)] = m_ref[...].reshape(flat)
+            act[:, pl.ds(pl.multiple_of((1 - meta[0]) * depth, 128), depth)] = a_ref[...].reshape(flat)
+
+        total = lax.dot_general(act[...], w_ref[...], NT, preferred_element_type=jnp.float32)
     total = total.astype(jnp.bfloat16)
-    o0[...] = total[:rows]
-
-    @pl.when(step == 0)
+    stay[...] = total[:rows]
+    tile = total.shape[1]
+    cols = pl.ds(pl.multiple_of(lax.rem(step, half) * tile, 128), tile)
+
+    @pl.when(step < half)
     def _():
-        o1a[...] = total[rows : 2 * rows]
-        o2a[...] = total[2 * rows : 3 * rows]
-        o3a[...] = total[3 * rows :]
-
-    @pl.when(step == 1)
+        up[0, :, cols] = total[2 * rows : 3 * rows]
+        down[1, :, cols] = total[3 * rows :]
+        up_late[...] = total[rows : 2 * rows]
+
+    @pl.when(step >= half)
     def _():
-        o1b[...] = total[rows : 2 * rows]
-        o2b[...] = total[2 * rows : 3 * rows]
-        o3b[...] = total[3 * rows :]
-
-
-def project(meta, mine, other, weight_t):
-    n_z, rows, depth = mine.shape
+        up[1, :, cols] = total[rows : 2 * rows]
+        down[0, :, cols] = total[2 * rows : 3 * rows]
+        down_late[...] = total[3 * rows :]
+
+
+def project(meta, own, other, weight_t, tile=640):
+    n_z, rows, depth = other.shape
     width = weight_t.shape[0]
-    tile = width // 2
+    with_own = own.ndim == 2
+    steps = width // tile
+    half = steps // 2
     act = pl.BlockSpec((n_z, rows, depth), lambda i, m: (0, 0, 0))
-    part = pl.BlockSpec((rows, tile), lambda i, m: (0, 0))
-    return pl.pallas_call(
-        project_kernel,
+    first = lambda i: jnp.minimum(i, half - 1)
+    second = lambda i: jnp.maximum(i - half, 0)
+    if with_own:
+        in_specs = [
+            pl.BlockSpec((n_z * rows, tile), lambda i, m: (0, i)),
+            act,
+            pl.BlockSpec((tile, depth), lambda i, m: (i, 1 - m[0])),
+        ]
+        scratch = []
+    else:
+        in_specs = [act, act, pl.BlockSpec((tile, 2 * depth), lambda i, m: (i, 0))]
+        scratch = [pltpu.VMEM((n_z * rows, 2 * depth), jnp.bfloat16)]
+    pair = pl.BlockSpec((2, rows, width // 2), lambda i, m: (0, 0, 0))
+    return pl.pallas_call(
+        functools.partial(project_kernel, with_own=with_own),
         grid_spec=pltpu.PrefetchScalarGridSpec(
             num_scalar_prefetch=1,
-            grid=(2,),
-            in_specs=[act, act, pl.BlockSpec((tile, 2 * depth), lambda i, m: (i, 0))],
-            out_specs=[pl.BlockSpec((rows, tile), lambda i, m: (0, i))] + [part] * 6,
-        ),
-        out_shape=[jax.ShapeDtypeStruct((rows, width), jnp.bfloat16)]
-        + [jax.ShapeDtypeStruct((rows, tile), jnp.bfloat16)] * 6,
+            grid=(steps,),
+            in_specs=in_specs,
+            out_specs=[
+                pl.BlockSpec((rows, tile), lambda i, m: (0, i)),
+                pair,
+                pair,
+                pl.BlockSpec((rows, tile), lambda i, m: (0, first(i))),
+                pl.BlockSpec((rows, tile), lambda i, m: (0, second(i))),
+            ],
+            scratch_shapes=scratch,
+        ),
+        out_shape=[
+            jax.ShapeDtypeStruct((rows, width), jnp.bfloat16),
+            jax.ShapeDtypeStruct((2, rows, width // 2), jnp.bfloat16),
+            jax.ShapeDtypeStruct((2, rows, width // 2), jnp.bfloat16),
+            jax.ShapeDtypeStruct((rows, width // 2), jnp.bfloat16),
+            jax.ShapeDtypeStruct((rows, width // 2), jnp.bfloat16),
+        ],
         compiler_params=params(),
         cost_estimate=pl.CostEstimate(
             flops=4 * n_z * rows * depth * width,
             bytes_accessed=4 * depth * width + 2 * n_z * rows * width,
             transcendentals=0,
         ),
-    )(meta, mine, other, weight_t)
-
-
-def add_kernel(a_ref, b_ref, o_ref):
-    o_ref[...] = (a_ref[...].astype(jnp.float32) + b_ref[...].astype(jnp.float32)).astype(o_ref.dtype)
-
-
-def add(a, b):
+    )(meta, own, other, weight_t)
+
+
+def add_kernel(a_ref, x_ref, b_ref, y_ref, oa_ref, ob_ref):
+    wide = lambda ref: ref[...].astype(jnp.float32)
+    oa_ref[...] = (wide(a_ref) + wide(x_ref)).astype(oa_ref.dtype)
+    ob_ref[...] = (wide(b_ref) + wide(y_ref)).astype(ob_ref.dtype)
+
+
+def add_relayed(a, from_low, b, from_high, steps=2):
+    rows, width = a.shape
+    tile = width // steps
+    flat = pl.BlockSpec((rows, tile), lambda i: (0, i))
+    lead = pl.BlockSpec((None, rows, tile), lambda i: (0, 0, i))
     return pl.pallas_call(
         add_kernel,
-        out_shape=jax.ShapeDtypeStruct(a.shape, a.dtype),
-        compiler_params=params(),
-        cost_estimate=pl.CostEstimate(flops=a.size, bytes_accessed=6 * a.size, transcendentals=0),
-    )(a, b)
-
-
-def finish_kernel(meta, gate_ref, *refs):
+        grid=(steps,),
+        in_specs=[flat, lead, flat, lead],
+        out_specs=[flat, flat],
+        out_shape=[jax.ShapeDtypeStruct(a.shape, a.dtype)] * 2,
+        compiler_params=params(),
+        cost_estimate=pl.CostEstimate(flops=2 * a.size, bytes_accessed=12 * a.size, transcendentals=0),
+    )(a, from_low, b, from_high)
+
+
+def finish_kernel(meta, gate_ref, own, low_b, low_a, high_a, high_b, *refs):
     o_ref = refs[-1]
-    width = o_ref.shape[2] // 2
     early = pl.program_id(0) < pl.num_programs(0) // 2
-    for part in range(2):
-        own, low_a, low_b, high_a, high_b = (r[...].astype(jnp.float32) for r in refs[5 * part : 5 * part + 5])
-        total = own + jnp.where(early, low_a, low_b) + jnp.where(early, high_a, high_b)
-        total = total.astype(jnp.bfloat16).astype(jnp.float32)
-        y = meta[0] if part == 0 else 1 - meta[0]
-        cols = pl.ds(pl.multiple_of(y * width, 128), width)
-        o_ref[0, :, cols] = (gate_ref[:, cols] * total).astype(o_ref.dtype)
-
-
-def finish(meta, gate, parts):
-    rows, width = parts[0][0].shape
+    wide = lambda ref: ref[...].astype(jnp.float32)
+    total = wide(own) + jnp.where(early, wide(low_a), wide(low_b)) + jnp.where(early, wide(high_a), wide(high_b))
+    total = total.astype(jnp.bfloat16).astype(jnp.float32)
+    o_ref[0] = (gate_ref[...] * total).astype(o_ref.dtype)
+
+
+def finish(meta, gate, piece, out=None):
+    own, low, low_a, high, high_b = piece
+    rows, width = own.shape
     steps = 4
     tile = width // steps
-    half = [pl.BlockSpec((rows, tile), lambda i, m: (0, jnp.minimum(i, steps // 2 - 1)))]
-    half += [pl.BlockSpec((rows, tile), lambda i, m: (0, jnp.maximum(i - steps // 2, 0)))]
-    args, specs = [], []
-    for own, low, high in parts:
-        args += [own, *low, *high]
-        specs += [pl.BlockSpec((rows, tile), lambda i, m: (0, i))] + half + half
+    half = steps // 2
+    first = lambda i: jnp.minimum(i, half - 1)
+    second = lambda i: jnp.maximum(i - half, 0)
+    specs = [
+        pl.BlockSpec((1, tile), lambda i, m: (0, 2 * i + m[0])),
+        pl.BlockSpec((rows, tile), lambda i, m: (0, i)),
+        pl.BlockSpec((None, rows, tile), lambda i, m: (1, 0, second(i))),
+        pl.BlockSpec((rows, tile), lambda i, m: (0, first(i))),
+        pl.BlockSpec((None, rows, tile), lambda i, m: (1, 0, first(i))),
+        pl.BlockSpec((rows, tile), lambda i, m: (0, second(i))),
+    ]
+    args = [meta, gate, own, low, low_a, high, high_b]
+    alias = {}
+    if out is not None:
+        alias = {len(args): 0}
+        args.append(out)
+        specs.append(pl.BlockSpec(memory_space=pl.ANY))
     return pl.pallas_call(
         finish_kernel,
         grid_spec=pltpu.PrefetchScalarGridSpec(
             num_scalar_prefetch=1,
             grid=(steps,),
-            in_specs=[pl.BlockSpec((1, 2 * tile), lambda i, m: (0, i))] + specs,
-            out_specs=pl.BlockSpec((1, rows, 2 * tile), lambda i, m: (0, 0, i)),
+            in_specs=specs,
+            out_specs=pl.BlockSpec((1, rows, tile), lambda i, m: (0, 0, 2 * i + m[0])),
         ),
         out_shape=jax.ShapeDtypeStruct((1, rows, 2 * width), jnp.bfloat16),
-        compiler_params=params(),
-    )(meta, gate, *args)
+        input_output_aliases=alias,
+        compiler_params=params(),
+        cost_estimate=pl.CostEstimate(flops=4 * rows * width, bytes_accessed=8 * rows * width, transcendentals=0),
+    )(*args)
 
 
 def local(queries, keys, values, out_weight, gate, kv_frames):
@@ -213,17 +302,18 @@
     def shift(array, axes, size, by):
         return lax.ppermute(array, axes, [(i, (i + by) % size) for i in range(size)])
 
+    weight = lax.dynamic_slice_in_dim(out_weight, my_z * (n_y * cols), n_y * cols, 0)
+    split = weight.shape[1] // 2
+    ring = n_y * n_l
+    lower, upper = weight[:, :split].T, weight[:, split:].T
+    lower, upper, queries = lax.optimization_barrier((lower, upper, queries))
+    far = shift(lower, ("yh", "yl"), ring, 1), shift(upper, ("yh", "yl"), ring, ring - 1)
+    weight_near = lax.all_gather(jnp.concatenate([lower, upper], 0), ("x", "c"), axis=0, tiled=True)
+
     parts = layout(queries[0], keys[0], values[0], n_y, n_z).reshape(n, 3, rows, cols)
+    parts, *far = lax.optimization_barrier((parts, *far))
+    weight_far = lax.all_gather(jnp.concatenate(far, 0), ("x", "c"), axis=0, tiled=True)
     parts = lax.all_to_all(parts, ("yh", "z"), 0, 0, tiled=True)
-
-    weight = lax.dynamic_slice_in_dim(out_weight, my_z * (n_y * cols), n_y * cols, 0).T
-    split = weight.shape[0] // 2
-    ring = n_y * n_l
-    far = jnp.concatenate(
-        [shift(weight[:split], ("yh", "yl"), ring, 1), shift(weight[split:], ("yh", "yl"), ring, ring - 1)], 0
-    )
-    weight_near = lax.all_gather(weight, ("x", "c"), axis=0, tiled=True)
-    weight_far = lax.all_gather(far, ("x", "c"), axis=0, tiled=True)
 
     table = kv_frames.reshape(-1)
     meta = lambda y: jnp.concatenate([jnp.stack([y, my_z]), table])
@@ -233,14 +323,17 @@
 
     up = lambda array: shift(array, "z", n_z, 1)
     down = lambda array: shift(array, "z", n_z, n_z - 1)
-    sums = []
-    for piece in (weight_near, weight_far):
-        o0, o1a, o1b, o2a, o2b, o3a, o3b = project(my_y[None], mine, other, piece)
-        relay_a, relay_b = up(o2a), down(o2b)
-        low_b, high_a = up(o1b), down(o3a)
-        low_a, high_b = up(add(o1a, relay_a)), down(add(o3b, relay_b))
-        sums.append((o0, (low_a, low_b), (high_a, high_b)))
-    return finish(my_l[None], gate, sums)
+
+    def scatter(own, weight_t):
+        stay, to_high, to_low, late_high, late_low = project(my_y[None], own, other, weight_t)
+        low, high = up(to_high), down(to_low)
+        late_high, late_low = add_relayed(late_high, low, late_low, high)
+        return stay, low, up(late_high), high, down(late_low)
+
+    near = scatter(project_own(my_y[None], mine, weight_near), weight_near)
+    far = scatter(mine, weight_far)
+    out = finish(my_l[None], gate, near)
+    return finish(1 - my_l[None], gate, far, out)
 
 
 def solution(mesh):

time: 177 us -> 165 us (0.932)
  waiting for transfers between devices: 83.3 us -> 66.4 us
  Pallas kernels: 45.5 us -> 51.3 us
  starting transfers between devices: 26.5 us -> 24.3 us
    ppermute x15 -> x11, waiting for transfers between devices: 39.6 us -> 22.9 us  [shift(): lax.ppermute(array, axes, [(i, (i + by) % size) for i in range(size)])]
    pallas_call x1 -> x2, Pallas kernels: 4.92 us -> 7.92 us  [finish(): pl.pallas_call(finish_kernel, grid_spec=pltpu.PrefetchScalarGridSpec(num_...]
    pallas_call x6 -> x5, Pallas kernels: 24.2 us -> 26.8 us  [the longest x2 15.9 us: project(): pl.pallas_call(functools.partial(project_kernel, with_own=with_own), grid...]
    unnamed x9 -> x21, local copies, waits for them, and re-layouts: 2.13 us -> 4.54 us
    ppermute x15 -> x11, starting transfers between devices: 18.1 us -> 15.9 us  [shift(): lax.ppermute(array, axes, [(i, (i + by) % size) for i in range(size)])]
  transfers between devices with their start and end apart: 18 -> 14, of which waited for: 8 -> 9; matrix products, arithmetic and copies ran while one was open for 2% -> 1% of each run, Pallas kernels for 23% -> 29%
where the time goes in v3:
time: 165 us; the launch traced here: 164 us
  waiting for transfers between devices  66.4 us (40%)
  Pallas kernels  51.3 us (31%)
  starting transfers between devices  24.3 us (15%)
  between operations  13.5 us (8%)
  local copies, waits for them, and re-layouts  5.81 us (4%)
  other arithmetic  2.54 us (2%)
    all_to_all x1, waiting for transfers between devices, local(): parts = lax.all_to_all(parts, ('yh', 'z'), 0, 0, tiled=True)  43.5 us
    ppermute x11, waiting for transfers between devices, shift(): lax.ppermute(array, axes, [(i, (i + by) % size) for i in range(size)])  22.9 us
    ppermute x11, starting transfers between devices, shift(): lax.ppermute(array, axes, [(i, (i + by) % size) for i in range(size)])  15.9 us
    pallas_call x2, Pallas kernels, project(): pl.pallas_call(functools.partial(project_kernel, with_own=with_own), grid...  15.9 us
    pallas_call x2, Pallas kernels, attend(): pl.pallas_call(functools.partial(attend_kernel, slots=slots), grid_spec=p...  12 us
    all_to_all x1, starting transfers between devices, local(): parts = lax.all_to_all(parts, ('yh', 'z'), 0, 0, tiled=True)  8.29 us
    pallas_call x2, Pallas kernels, finish(): pl.pallas_call(finish_kernel, grid_spec=pltpu.PrefetchScalarGridSpec(num_...  7.92 us
    pallas_call x1, Pallas kernels, project_own(): pl.pallas_call(own_kernel, grid_spec=pltpu.PrefetchScalarGridSpec(num_sca...  6.51 us
  transfers between devices with their start and end apart: 14, of which 9 were waited for; matrix products, arithmetic and copies ran while one was open for 1% of the time, Pallas kernels for 29%

profile of v3, /device:TPU:24, one launch (start us, length us, event | category | flops | bytes accessed | tf_op | source)
XLA Modules:
  0.0 163.8 jit_solution(1492538388482283108)
XLA Ops:
  6.5 0.0 all-gather.5.cloned.1.call-start
  6.5 1.2 dynamic-slice_bitcast_fusion
  7.7 1.0 pad_maximum_fusion.1
  8.7 0.0 all-gather.5.cloned.1.call-update
  8.7 0.0 all-gather.3.cloned.1.call-start
  8.8 0.2 collective-permute-start
  9.0 1.9 %collective-permute-start.1 = (bf16[160,1280]{1,0:T(8,128)(2,1)S(1)}, bf16[160,1280]{1,0:T(8,128)(2,1)S(1)}, u32[]{:S(2)}, u32[]{:S(2)}) collective-permute-start(bf16[160,1280]{1,0:T(8,128)(2,1)S(1)} %get-tuple-element.27), channel_id=1, source_target_pairs={{0,66},{2,0},{64,2},{66,64},{1,67},{3,1},{65,3},{67,65},{4,70},{6,... | collective-permute-start | bytes 1228808 | tf_op jit(solution)/shard_map/ppermute | solution.py:303
  10.9 4.6 %shard_map.64 = bf16[2,4,3,128,640]{4,3,2,1,0:T(8,128)(2,1)} custom-call(bf16[128,5120]{1,0:T(8,128)(2,1)} %bitcast.13, bf16[128,5120]{1,0:T(8,128)(2,1)} %bitcast.14, bf16[128,5120]{1,0:T(8,128)(2,1)} %bitcast.15), custom_call_target="tpu_custom_call" | custom-call | bytes 7864320 | tf_op jit(solution)/shard_map/pallas_call | solution.py:33
  15.4 4.6 %collective-permute-done = bf16[160,1280]{1,0:T(8,128)(2,1)S(1)} collective-permute-done((bf16[160,1280]{1,0:T(8,128)(2,1)S(1)}, bf16[160,1280]{1,0:T(8,128)(2,1)S(1)}, u32[]{:S(2)}, u32[]{:S(2)}) %collective-permute-start) | collective-permute-done | bytes 409632 | tf_op jit(solution)/shard_map/ppermute | solution.py:303
  20.0 1.3 collective-permute-done.1
  21.3 0.9 pad_maximum_fusion
  22.3 0.0 all-gather.3.cloned.1.call-update
  22.3 0.0 copy-start.9
  22.3 8.3 %all-to-all-start = ((bf16[8,3,128,640]{3,2,1,0:T(8,128)(2,1)}), bf16[8,3,128,640]{3,2,1,0:T(8,128)(2,1)}, u32[]{:S(2)}, u32[]{:S(2)}) async-start(bf16[8,3,128,640]{3,2,1,0:T(8,128)(2,1)} %bitcast.12), calls=%async_computation | async-start | bytes 7864320 | tf_op jit(solution)/shard_map/all_to_all | solution.py:316
  30.6 0.0 copy-done.9
  30.6 0.1 copy.9
  30.7 0.1 reshape.6
  30.8 0.6 add_add_fusion.1
  31.4 43.5 %all-to-all-done.q_ref.k_ref.v_ref = bf16[8,3,128,640]{3,2,1,0:T(8,128)(2,1)} async-done(((bf16[8,3,128,640]{3,2,1,0:T(8,128)(2,1)}), bf16[8,3,128,640]{3,2,1,0:T(8,128)(2,1)}, u32[]{:S(2)}, u32[]{:S(2)}) %all-to-all-start) | async-done | bytes 3932192 | tf_op jit(solution)/shard_map/all_to_all | solution.py:316
  74.9 6.0 %shard_map.66 = bf16[4,128,640]{2,1,0:T(8,128)(2,1)} custom-call(s32[98]{0:T(128)} %get-tuple-element.47.meta, bf16[8,3,128,640]{3,2,1,0:T(8,128)(2,1)} %all-to-all-done.q_ref.k_ref.v_ref, bf16[8,3,128,640]{3,2,1,0:T(8,128)(2,1)} %all-to-all-done.q_ref.k_ref.v_ref, bf16[8,3,128,640]{3,2,1,0:T(8,128)(2,1)} %all-to-all-done.q_ref.k_ref.v_ref), custom_call_target="tpu_custom_call" | custom-call | flops 503316480 | bytes 3932160 | tf_op jit(solution)/shard_map/pallas_call | solution.py:86
  80.9 0.8 collective-permute-start.2
  81.8 6.0 %shard_map.65.refs_0_.a_ref = bf16[4,128,640]{2,1,0:T(8,128)(2,1)} custom-call(s32[98]{0:T(128)} %get-tuple-element.48.meta, bf16[8,3,128,640]{3,2,1,0:T(8,128)(2,1)} %all-to-all-done.q_ref.k_ref.v_ref, bf16[8,3,128,640]{3,2,1,0:T(8,128)(2,1)} %all-to-all-done.q_ref.k_ref.v_ref, bf16[8,3,128,640]{3,2,1,0:T(8,128)(2,1)} %all-to-all-done.q_ref.k_ref.v_ref), custom_call_target="tpu_custom_call" | custom-call | flops 503316480 | bytes 3932160 | tf_op jit(solution)/shard_map/pallas_call | solution.py:86
  87.8 0.0 all-gather.5.cloned.1.call-done.w_ref.refs_2_
  87.8 6.5 %shard_map.69.refs_0_ = f32[512,2560]{1,0:T(8,128)} custom-call(s32[1]{0:T(128)} %bitcast.1.meta, bf16[4,128,640]{2,1,0:T(8,128)(2,1)} %shard_map.65.refs_0_.a_ref, bf16[2560,1280]{1,0:T(8,128)(2,1)} %all-gather.5.cloned.1.call-done.w_ref.refs_2_), custom_call_target="tpu_custom_call" | custom-call | flops 1677721600 | bytes 8519680 | tf_op jit(solution)/shard_map/pallas_call | solution.py:115
  94.3 4.6 %collective-permute-done.2.refs_1_ = bf16[4,128,640]{2,1,0:T(8,128)(2,1)S(1)} collective-permute-done((bf16[4,128,640]{2,1,0:T(8,128)(2,1)}, bf16[4,128,640]{2,1,0:T(8,128)(2,1)S(1)}, u32[]{:S(2)}, u32[]{:S(2)}) %collective-permute-start.2) | collective-permute-done | bytes 655392 | tf_op jit(solution)/shard_map/ppermute | solution.py:303
  98.9 0.0 copy-start.4
  99.0 0.8 copy-done.4
  99.8 7.4 %shard_map.70 = (bf16[128,2560]{1,0:T(8,128)(2,1)}, bf16[2,128,1280]{2,1,0:T(8,128)(2,1)}, bf16[2,128,1280]{2,1,0:T(8,128)(2,1)}, bf16[128,1280]{1,0:T(8,128)(2,1)}, bf16[128,1280]{1,0:T(8,128)(2,1)}) custom-call(s32[1]{0:T(128)} %bitcast.1.meta, f32[512,2560]{1,0:T(8,128)} %shard_map.69.refs_0_, bf16[4,128,640]{2,1,0:T(8,128)(2,1)} %copy-done.4, ...), custom_call_target="tpu_custom_call" | custom-call | flops 3355443200 | bytes 9175040 | tf_op jit(solution)/shard_map/pallas_call | solution.py:194
  107.2 1.2 collective-permute-start.7
  108.4 2.0 %collective-permute-start.8 = (bf16[2,128,1280]{2,1,0:T(8,128)(2,1)}, bf16[2,128,1280]{2,1,0:T(8,128)(2,1)S(1)}, u32[]{:S(2)}, u32[]{:S(2)}) collective-permute-start(bf16[2,128,1280]{2,1,0:T(8,128)(2,1)} %get-tuple-element.42), channel_id=1, source_target_pairs={{0,48},{16,0},{32,16},{48,32},{1,49},{17,1},{33,17},{49,33},{2,50}... | collective-permute-start | bytes 1966088 | tf_op jit(solution)/shard_map/ppermute | solution.py:303
  110.4 0.0 all-gather.3.cloned.1.call-done.refs_2_
  110.4 8.5 %shard_map.67 = (bf16[128,2560]{1,0:T(8,128)(2,1)}, bf16[2,128,1280]{2,1,0:T(8,128)(2,1)}, bf16[2,128,1280]{2,1,0:T(8,128)(2,1)}, bf16[128,1280]{1,0:T(8,128)(2,1)}, bf16[128,1280]{1,0:T(8,128)(2,1)}) custom-call(s32[1]{0:T(128)} %bitcast.1.meta, bf16[4,128,640]{2,1,0:T(8,128)(2,1)} %shard_map.65.refs_0_.a_ref, bf16[4,128,640]{2,1,0:T(8,128)(2,1)} %copy-done.4, ...), custom_call_target="tpu_custom_call" | custom-call | flops 3355443200 | bytes 9175040 | tf_op jit(solution)/shard_map/pallas_call | solution.py:194
  119.0 0.1 collective-permute-start.3
  119.0 3.2 %collective-permute-start.4 = (bf16[2,128,1280]{2,1,0:T(8,128)(2,1)}, bf16[2,128,1280]{2,1,0:T(8,128)(2,1)S(1)}, u32[]{:S(2)}, u32[]{:S(2)}) collective-permute-start(bf16[2,128,1280]{2,1,0:T(8,128)(2,1)} %get-tuple-element.35), channel_id=1, source_target_pairs={{0,48},{16,0},{32,16},{48,32},{1,49},{17,1},{33,17},{49,33},{2,50}... | collective-permute-start | bytes 1966088 | tf_op jit(solution)/shard_map/ppermute | solution.py:303
  122.2 4.0 %collective-permute-done.7.x_ref.low_b = bf16[2,128,1280]{2,1,0:T(8,128)(2,1)S(1)} collective-permute-done((bf16[2,128,1280]{2,1,0:T(8,128)(2,1)}, bf16[2,128,1280]{2,1,0:T(8,128)(2,1)S(1)}, u32[]{:S(2)}, u32[]{:S(2)}) %collective-permute-start.7) | collective-permute-done | bytes 655392 | tf_op jit(solution)/shard_map/ppermute | solution.py:303
  126.3 0.0 copy-start
  126.3 0.0 collective-permute-done.8.y_ref.high_a
  126.3 0.0 copy-start.1
  126.3 0.8 copy-done
  127.1 0.3 copy-done.1
  127.4 2.2 %shard_map.71 = (bf16[128,1280]{1,0:T(8,128)(2,1)}, bf16[128,1280]{1,0:T(8,128)(2,1)}) custom-call(bf16[128,1280]{1,0:T(8,128)(2,1)} %get-tuple-element.40.a_ref, bf16[2,128,1280]{2,1,0:T(8,128)(2,1)} %copy-done, bf16[128,1280]{1,0:T(8,128)(2,1)} %get-tuple-element.41.b_ref, bf16[2,128,1280]{2,1,0:T(8,128)(2,1)} %copy-done.1), custom_call_target="tpu_custom_call" | custom-call | flops 327680 | bytes 1966080 | tf_op jit(solution)/shard_map/pallas_call | solution.py:236
  129.6 0.0 collective-permute-start.9
  129.6 3.2 %collective-permute-start.10 = (bf16[128,1280]{1,0:T(8,128)(2,1)}, bf16[128,1280]{1,0:T(8,128)(2,1)S(1)}, u32[]{:S(2)}, u32[]{:S(2)}) collective-permute-start(bf16[128,1280]{1,0:T(8,128)(2,1)} %get-tuple-element.44), channel_id=1, source_target_pairs={{0,48},{16,0},{32,16},{48,32},{1,49},{17,1},{33,17},{49,33},{2,50}... | collective-permute-start | bytes 983048 | tf_op jit(solution)/shard_map/ppermute | solution.py:303
  132.8 7.5 %collective-permute-done.3.x_ref.low_b = bf16[2,128,1280]{2,1,0:T(8,128)(2,1)S(1)} collective-permute-done((bf16[2,128,1280]{2,1,0:T(8,128)(2,1)}, bf16[2,128,1280]{2,1,0:T(8,128)(2,1)S(1)}, u32[]{:S(2)}, u32[]{:S(2)}) %collective-permute-start.3) | collective-permute-done | bytes 655392 | tf_op jit(solution)/shard_map/ppermute | solution.py:303
  140.3 0.0 copy-start.2
  140.3 0.0 collective-permute-done.4.y_ref.high_a
  140.3 0.8 copy-done.2
  141.1 0.2 copy-done.3
  141.4 2.2 %shard_map.68 = (bf16[128,1280]{1,0:T(8,128)(2,1)}, bf16[128,1280]{1,0:T(8,128)(2,1)}) custom-call(bf16[128,1280]{1,0:T(8,128)(2,1)} %get-tuple-element.33.a_ref, bf16[2,128,1280]{2,1,0:T(8,128)(2,1)} %copy-done.2, bf16[128,1280]{1,0:T(8,128)(2,1)} %get-tuple-element.34.b_ref, bf16[2,128,1280]{2,1,0:T(8,128)(2,1)} %copy-done.3), custom_call_target="tpu_custom_call" | custom-call | flops 327680 | bytes 1966080 | tf_op jit(solution)/shard_map/pallas_call | solution.py:236
  143.6 0.0 collective-permute-start.5
  143.6 3.2 %collective-permute-start.6 = (bf16[128,1280]{1,0:T(8,128)(2,1)}, bf16[128,1280]{1,0:T(8,128)(2,1)S(1)}, u32[]{:S(2)}, u32[]{:S(2)}) collective-permute-start(bf16[128,1280]{1,0:T(8,128)(2,1)} %get-tuple-element.37), channel_id=1, source_target_pairs={{0,48},{16,0},{32,16},{48,32},{1,49},{17,1},{33,17},{49,33},{2,50}... | collective-permute-start | bytes 983048 | tf_op jit(solution)/shard_map/ppermute | solution.py:303
  146.8 0.0 collective-permute-done.9.low_a
  146.8 0.0 copy-start.5
  146.8 0.5 collective-permute-done.10.high_b
  147.3 0.0 copy-start.6
  147.3 0.2 copy-done.5
  147.5 0.5 copy-done.6
  148.1 4.0 %shard_map.72.refs_0_ = bf16[1,128,5120]{2,1,0:T(8,128)(2,1)} custom-call(s32[1]{0:T(128)} %bitcast.meta, f32[1,5120]{1,0:T(1,128)} %gate_ref.3, bf16[128,2560]{1,0:T(8,128)(2,1)} %get-tuple-element.38.own, bf16[2,128,1280]{2,1,0:T(8,128)(2,1)} %copy-done, bf16[128,1280]{1,0:T(8,128)(2,1)} %copy-done.5, bf16[2,128,1280]{2,1,0:T(8,128)(2,1)} %copy-done.1, ...), custom_call_target="tpu_custom_call" | custom-call | flops 1310720 | bytes 2621440 | tf_op jit(solution)/shard_map/pallas_call | solution.py:278
  152.0 0.1 collective-permute-done.5.low_a
  152.1 0.0 copy-start.7
  152.1 0.2 collective-permute-done.6.high_b
  152.3 0.5 copy-done.7
  152.8 0.2 copy-done.8
  153.0 4.0 %shard_map.73 = bf16[1,128,5120]{2,1,0:T(8,128)(2,1)} custom-call(s32[1]{0:T(128)S(6)} %sub.6.meta, f32[1,5120]{1,0:T(1,128)} %gate_ref.3, bf16[128,2560]{1,0:T(8,128)(2,1)} %get-tuple-element.31.own, bf16[2,128,1280]{2,1,0:T(8,128)(2,1)} %copy-done.2, bf16[128,1280]{1,0:T(8,128)(2,1)} %copy-done.7, ...), custom_call_target="tpu_custom_call", output_to_operand_aliasing={{}: (7, {})} | custom-call | flops 1310720 | bytes 2621440 | tf_op jit(solution)/shard_map/pallas_call | solution.py:278
  (2 shorter events, 0.0 us)
Async XLA Ops:
  6.5 81.3 %all-gather.5.cloned.1.call-start = ((), (), s32[]{:S(2)}) async-start(), calls=%async_computation.2 | async-start | bytes 7372800 | tf_op jit(solution)/shard_map/all_gather | solution.py:311
  8.7 101.7 %all-gather.3.cloned.1.call-start = ((), (), s32[]{:S(2)}) async-start(), calls=%async_computation.1 | async-start | bytes 7372800 | tf_op jit(solution)/shard_map/all_gather | solution.py:315
  8.8 11.3 %collective-permute-start = (bf16[160,1280]{1,0:T(8,128)(2,1)S(1)}, bf16[160,1280]{1,0:T(8,128)(2,1)S(1)}, u32[]{:S(2)}, u32[]{:S(2)}) collective-permute-start(bf16[160,1280]{1,0:T(8,128)(2,1)S(1)} %get-tuple-element.26), channel_id=1, source_target_pairs={{0,2},{2,64},{64,66},{66,0},{1,3},{3,65},{65,67},{67,1},{4,6},{6,6... | collective-permute-start | bytes 1228808 | tf_op jit(solution)/shard_map/ppermute | solution.py:303
  9.0 12.4 %collective-permute-start.1 = (bf16[160,1280]{1,0:T(8,128)(2,1)S(1)}, bf16[160,1280]{1,0:T(8,128)(2,1)S(1)}, u32[]{:S(2)}, u32[]{:S(2)}) collective-permute-start(bf16[160,1280]{1,0:T(8,128)(2,1)S(1)} %get-tuple-element.27), channel_id=1, source_target_pairs={{0,66},{2,0},{64,2},{66,64},{1,67},{3,1},{65,3},{67,65},{4,70},{6,... | collective-permute-start | bytes 1228808 | tf_op jit(solution)/shard_map/ppermute | solution.py:303
  22.3 8.3 %copy-start.9 = (s32[16,6]{0,1:T(8,128)S(1)}, s32[16,6]{0,1:T(8,128)}, u32[]{:S(2)}) copy-start(s32[16,6]{0,1:T(8,128)} %param.11) | copy-start | bytes 1156
  22.3 52.6 %all-to-all-start = ((bf16[8,3,128,640]{3,2,1,0:T(8,128)(2,1)}), bf16[8,3,128,640]{3,2,1,0:T(8,128)(2,1)}, u32[]{:S(2)}, u32[]{:S(2)}) async-start(bf16[8,3,128,640]{3,2,1,0:T(8,128)(2,1)} %bitcast.12), calls=%async_computation | async-start | bytes 7864320 | tf_op jit(solution)/shard_map/all_to_all | solution.py:316
  80.9 18.0 %collective-permute-start.2 = (bf16[4,128,640]{2,1,0:T(8,128)(2,1)}, bf16[4,128,640]{2,1,0:T(8,128)(2,1)S(1)}, u32[]{:S(2)}, u32[]{:S(2)}) collective-permute-start(bf16[4,128,640]{2,1,0:T(8,128)(2,1)} %shard_map.66), channel_id=1, source_target_pairs={{0,64},{64,0},{1,65},{65,1},{2,66},{66,2},{3,67},{67,3},{4,68},{68... | collective-permute-start | bytes 1966088 | tf_op jit(solution)/shard_map/ppermute | solution.py:303
  98.9 0.8 copy-start.4
  107.2 19.1 %collective-permute-start.7 = (bf16[2,128,1280]{2,1,0:T(8,128)(2,1)}, bf16[2,128,1280]{2,1,0:T(8,128)(2,1)S(1)}, u32[]{:S(2)}, u32[]{:S(2)}) collective-permute-start(bf16[2,128,1280]{2,1,0:T(8,128)(2,1)} %get-tuple-element.39), channel_id=1, source_target_pairs={{0,16},{16,32},{32,48},{48,0},{1,17},{17,33},{33,49},{49,1},{2,18}... | collective-permute-start | bytes 1966088 | tf_op jit(solution)/shard_map/ppermute | solution.py:303
  108.4 17.9 %collective-permute-start.8 = (bf16[2,128,1280]{2,1,0:T(8,128)(2,1)}, bf16[2,128,1280]{2,1,0:T(8,128)(2,1)S(1)}, u32[]{:S(2)}, u32[]{:S(2)}) collective-permute-start(bf16[2,128,1280]{2,1,0:T(8,128)(2,1)} %get-tuple-element.42), channel_id=1, source_target_pairs={{0,48},{16,0},{32,16},{48,32},{1,49},{17,1},{33,17},{49,33},{2,50}... | collective-permute-start | bytes 1966088 | tf_op jit(solution)/shard_map/ppermute | solution.py:303
  119.0 21.4 %collective-permute-start.3 = (bf16[2,128,1280]{2,1,0:T(8,128)(2,1)}, bf16[2,128,1280]{2,1,0:T(8,128)(2,1)S(1)}, u32[]{:S(2)}, u32[]{:S(2)}) collective-permute-start(bf16[2,128,1280]{2,1,0:T(8,128)(2,1)} %get-tuple-element.32), channel_id=1, source_target_pairs={{0,16},{16,32},{32,48},{48,0},{1,17},{17,33},{33,49},{49,1},{2,18}... | collective-permute-start | bytes 1966088 | tf_op jit(solution)/shard_map/ppermute | solution.py:303
  119.0 21.3 %collective-permute-start.4 = (bf16[2,128,1280]{2,1,0:T(8,128)(2,1)}, bf16[2,128,1280]{2,1,0:T(8,128)(2,1)S(1)}, u32[]{:S(2)}, u32[]{:S(2)}) collective-permute-start(bf16[2,128,1280]{2,1,0:T(8,128)(2,1)} %get-tuple-element.35), channel_id=1, source_target_pairs={{0,48},{16,0},{32,16},{48,32},{1,49},{17,1},{33,17},{49,33},{2,50}... | collective-permute-start | bytes 1966088 | tf_op jit(solution)/shard_map/ppermute | solution.py:303
  126.3 0.8 copy-start
  126.3 1.1 copy-start.1
  129.6 17.3 %collective-permute-start.9 = (bf16[128,1280]{1,0:T(8,128)(2,1)}, bf16[128,1280]{1,0:T(8,128)(2,1)S(1)}, u32[]{:S(2)}, u32[]{:S(2)}) collective-permute-start(bf16[128,1280]{1,0:T(8,128)(2,1)} %get-tuple-element.43), channel_id=1, source_target_pairs={{0,16},{16,32},{32,48},{48,0},{1,17},{17,33},{33,49},{49,1},{2,18}... | collective-permute-start | bytes 983048 | tf_op jit(solution)/shard_map/ppermute | solution.py:303
  129.6 17.8 %collective-permute-start.10 = (bf16[128,1280]{1,0:T(8,128)(2,1)}, bf16[128,1280]{1,0:T(8,128)(2,1)S(1)}, u32[]{:S(2)}, u32[]{:S(2)}) collective-permute-start(bf16[128,1280]{1,0:T(8,128)(2,1)} %get-tuple-element.44), channel_id=1, source_target_pairs={{0,48},{16,0},{32,16},{48,32},{1,49},{17,1},{33,17},{49,33},{2,50}... | collective-permute-start | bytes 983048 | tf_op jit(solution)/shard_map/ppermute | solution.py:303
  140.3 0.8 copy-start.2
  140.3 1.1 copy-start.3
  143.6 8.5 %collective-permute-start.5 = (bf16[128,1280]{1,0:T(8,128)(2,1)}, bf16[128,1280]{1,0:T(8,128)(2,1)S(1)}, u32[]{:S(2)}, u32[]{:S(2)}) collective-permute-start(bf16[128,1280]{1,0:T(8,128)(2,1)} %get-tuple-element.36), channel_id=1, source_target_pairs={{0,16},{16,32},{32,48},{48,0},{1,17},{17,33},{33,49},{49,1},{2,18}... | collective-permute-start | bytes 983048 | tf_op jit(solution)/shard_map/ppermute | solution.py:303
  143.6 8.7 %collective-permute-start.6 = (bf16[128,1280]{1,0:T(8,128)(2,1)}, bf16[128,1280]{1,0:T(8,128)(2,1)S(1)}, u32[]{:S(2)}, u32[]{:S(2)}) collective-permute-start(bf16[128,1280]{1,0:T(8,128)(2,1)} %get-tuple-element.37), channel_id=1, source_target_pairs={{0,48},{16,0},{32,16},{48,32},{1,49},{17,1},{33,17},{49,33},{2,50}... | collective-permute-start | bytes 983048 | tf_op jit(solution)/shard_map/ppermute | solution.py:303
  146.8 0.7 copy-start.5
  147.3 0.7 copy-start.6
  152.1 0.7 copy-start.7
  152.3 0.7 copy-start.8
Sparse Core Ops, SparseCore 0:
  9.0 44.0 all-gather.4
  54.8 42.0 all-gather.2

commit v4 on v3

v4 whole, which is shorter than its diff:
```python
import functools
import math

import jax
import jax.numpy as jnp
from jax import lax
from jax.experimental import pallas as pl
from jax.experimental.pallas import tpu as pltpu
from jax.sharding import Mesh
from jax.sharding import PartitionSpec as P

HEAD_DIM = 128
FRAME = 64
MIB = 1024 * 1024
VMEM = 60 * MIB
NT = (((1,), (1,)), ((), ()))


def params(limit=VMEM):
    return pltpu.CompilerParams(vmem_limit_bytes=limit)


def layout_kernel(q_ref, k_ref, v_ref, o_ref):
    n_y, _, rows, cols = o_ref.shape
    for y in range(n_y):
        for i, ref in enumerate((q_ref, k_ref, v_ref)):
            o_ref[y, i] = ref[:, y * cols : (y + 1) * cols]


def layout(q, k, v, n_y, n_z):
    rows, width = q.shape
    cols = width // (n_y * n_z)
    block = pl.BlockSpec((rows, n_y * cols), lambda i: (0, i))
    return pl.pallas_call(
        layout_kernel,
        grid=(n_z,),
        in_specs=[block] * 3,
        out_specs=pl.BlockSpec((n_y, None, 3, rows, cols), lambda i: (0, i, 0, 0, 0)),
        out_shape=jax.ShapeDtypeStruct((n_y, n_z, 3, rows, cols), q.dtype),
        compiler_params=params(),
        cost_estimate=pl.CostEstimate(flops=0, bytes_accessed=12 * rows * width, transcendentals=0),
    )(q, k, v)


def attend_half(meta, half, q_ref, k_ref, v_ref, o_ref, slots):
    blocks, rows, width = o_ref.shape
    per = rows // FRAME
    heads = width // HEAD_DIM
    n_key = slots * FRAME
    scale = 1.0 / math.sqrt(HEAD_DIM)
    lane = lax.broadcasted_iota(jnp.int32, (1, n_key), 1)
    work = []
    for r in range(blocks):
        block = half * blocks + lax.rem(meta[1] + r, blocks)
        for p in range(per):
            base = 2 + (block * per + p) * slots
            bias = jnp.zeros((1, n_key), jnp.float32)
            picks = []
            for s in range(slots):
                g = meta[base + s]
                inside = (lane >= s * FRAME) & (lane < (s + 1) * FRAME)
                bias = jnp.where(inside, jnp.where(g >= 0, 0.0, -1e30), bias)
                g = jnp.maximum(g, 0)
                picks.append((g // per, pl.multiple_of((g % per) * FRAME, FRAME)))
            for h in range(heads):
                work.append((r, p, slice(h * HEAD_DIM, (h + 1) * HEAD_DIM), block, picks, bias))
    scores = []
    for r, p, cols, block, picks, bias in work:
        key = jnp.concatenate([k_ref[b, pl.ds(o, FRAME), cols] for b, o in picks], 0)
        query = q_ref[block, p * FRAME : (p + 1) * FRAME, cols]
        score = lax.dot_general(query, key, NT, preferred_element_type=jnp.float32)
        scores.append(score * scale + bias)
    tops = [jnp.max(s, axis=1, keepdims=True) for s in scores]
    probs = [jnp.exp(s - t) for s, t in zip(scores, tops)]
    denoms = [jnp.sum(p, axis=1, keepdims=True) for p in probs]
    for (r, p, cols, block, picks, bias), prob, denom in zip(work, probs, denoms):
        val = jnp.concatenate([v_ref[b, pl.ds(o, FRAME), cols] for b, o in picks], 0)
        accum = jnp.dot(prob.astype(jnp.bfloat16), val, preferred_element_type=jnp.float32)
        o_ref[r, p * FRAME : (p + 1) * FRAME, cols] = (accum / denom).astype(jnp.bfloat16)


def attend_kernel(meta, q_ref, k_ref, v_ref, theirs_ref, mine_ref, *, slots):
    attend_half(meta, 1 - meta[0], q_ref, k_ref, v_ref, theirs_ref, slots)
    attend_half(meta, meta[0], q_ref, k_ref, v_ref, mine_ref, slots)


def attend(meta, parts, slots, n_y):
    blocks, _, rows, width = parts.shape
    n_z = blocks // n_y
    whole = lambda which: pl.BlockSpec((blocks, None, rows, width), lambda i, m: (0, which, 0, 0))
    work = blocks * rows * slots * FRAME * width
    return pl.pallas_call(
        functools.partial(attend_kernel, slots=slots),
        grid_spec=pltpu.PrefetchScalarGridSpec(
            num_scalar_prefetch=1,
            grid=(1,),
            in_specs=[whole(0), whole(1), whole(2)],
            out_specs=[pl.BlockSpec((n_z, rows, width), lambda i, m: (0, 0, 0))] * 2,
        ),
        out_shape=[jax.ShapeDtypeStruct((n_z, rows, width), jnp.bfloat16)] * 2,
        compiler_params=params(),
        cost_estimate=pl.CostEstimate(
            flops=work * 4, bytes_accessed=4 * blocks * rows * width * 2, transcendentals=work // HEAD_DIM
        ),
    )(meta, parts, parts, parts)


def project_kernel(meta, mine_ref, other_ref, *refs, spots, n_piece):
    n_x = len(spots)
    pieces, refs = refs[:n_piece], refs[n_piece:]
    outs, (act, w_buf, r_buf, a_sem, w_sem, r_sem) = refs[:5], refs[5:]
    n_z, rows, depth = mine_ref.shape
    tile = w_buf.shape[0] // n_x
    part = tile // 4
    half, core = meta[0], meta[1]
    loads = {}

    def load(x):
        copies = []
        for k in range(4):
            buffer, row = spots[x][k % 2]
            src = pieces[buffer + k // 2 * (n_piece // 2)].at[pl.ds(row, part)]
            row = x * tile + ((core if k < 2 else 1 - core) * 2 + k % 2) * part
            dst = w_buf.at[pl.ds(pl.multiple_of(row, part), part)]
            copies.append(pltpu.make_async_copy(src, dst, w_sem.at[4 * x + k]))
        for copy in copies:
            copy.start()
        loads[x] = copies

    acts = []
    for i, (ref, at) in enumerate(((mine_ref, half), (other_ref, 1 - half))):
        cols = pl.ds(pl.multiple_of(at * depth, 128), depth)
        acts.append(pltpu.make_async_copy(ref, act.at[:, :, cols], a_sem.at[i]))
        acts[-1].start()
    load(0)
    load(1)
    for copy in acts:
        copy.wait()

    stores = []
    for x in range(n_x):
        for copy in loads[x]:
            copy.wait()
        if x + 2 < n_x:
            load(x + 2)
        left = act[...].reshape(n_z * rows, 2 * depth)
        weight = w_buf[x * tile : (x + 1) * tile]
        total = lax.dot_general(left, weight, NT, preferred_element_type=jnp.float32)
        r_buf[x] = total.astype(r_buf.dtype)
        stay, up, down, up_late, down_late = outs
        late, col = divmod(x, n_x // 2)
        block = lambda r: r_buf.at[x, pl.ds(r * rows, rows)]
        cols = pl.ds(col * tile, tile)
        targets = [(block(0), stay.at[:, pl.ds(x * tile, tile)])]
        if late:
            targets += [(block(1), up.at[1, :, cols]), (block(2), down.at[0, :, cols]), (block(3), down_late.at[:, cols])]
        else:
            targets += [(block(2), up.at[0, :, cols]), (block(3), down.at[1, :, cols]), (block(1), up_late.at[:, cols])]
        for src, dst in targets:
            copy = pltpu.make_async_copy(src, dst, r_sem.at[len(stores)])
            copy.start()
            stores.append(copy)
    for copy in stores:
        copy.wait()


def project(meta, mine, other, pieces, spots, part):
    n_z, rows, depth = mine.shape
    n_x = len(spots)
    tile = 4 * part
    width = n_x * tile
    shape = lambda *dims: jax.ShapeDtypeStruct(dims, jnp.bfloat16)
    hbm = pl.BlockSpec(memory_space=pl.ANY)
    return pl.pallas_call(
        functools.partial(project_kernel, spots=spots, n_piece=len(pieces)),
        grid_spec=pltpu.PrefetchScalarGridSpec(
            num_scalar_prefetch=1,
            grid=(1,),
            in_specs=[hbm] * (2 + len(pieces)),
            out_specs=[hbm] * 5,
            scratch_shapes=[
                pltpu.VMEM((n_z, rows, 2 * depth), jnp.bfloat16),
                pltpu.VMEM((width, 2 * depth), jnp.bfloat16),
                pltpu.VMEM((n_x, n_z * rows, tile), jnp.bfloat16),
                pltpu.SemaphoreType.DMA((2,)),
                pltpu.SemaphoreType.DMA((4 * n_x,)),
                pltpu.SemaphoreType.DMA((n_x * n_z,)),
            ],
        ),
        out_shape=[shape(rows, width)] + [shape(2, rows, width // 2)] * 2 + [shape(rows, width // 2)] * 2,
        compiler_params=params(),
        cost_estimate=pl.CostEstimate(
            flops=4 * n_z * rows * depth * width,
            bytes_accessed=4 * depth * width + 4 * n_z * rows * width,
            transcendentals=0,
        ),
    )(meta, mine, other, *pieces)


def add_kernel(a_ref, x_ref, b_ref, y_ref, oa_ref, ob_ref):
    wide = lambda ref: ref[...].astype(jnp.float32)
    oa_ref[...] = (wide(a_ref) + wide(x_ref)).astype(oa_ref.dtype)
    ob_ref[...] = (wide(b_ref) + wide(y_ref)).astype(ob_ref.dtype)


def add_relayed(a, from_low, b, from_high, steps=2):
    rows, width = a.shape
    tile = width // steps
    flat = pl.BlockSpec((rows, tile), lambda i: (0, i))
    lead = pl.BlockSpec((None, rows, tile), lambda i: (0, 0, i))
    return pl.pallas_call(
        add_kernel,
        grid=(steps,),
        in_specs=[flat, lead, flat, lead],
        out_specs=[flat, flat],
        out_shape=[jax.ShapeDtypeStruct(a.shape, a.dtype)] * 2,
        compiler_params=params(8 * MIB),
        cost_estimate=pl.CostEstimate(flops=2 * a.size, bytes_accessed=12 * a.size, transcendentals=0),
    )(a, from_low, b, from_high)


def finish_kernel(meta, gate_ref, own, low_b, low_a, high_a, high_b, *refs):
    o_ref = refs[-1]
    early = pl.program_id(0) < pl.num_programs(0) // 2
    wide = lambda ref: ref[...].astype(jnp.float32)
    total = wide(own) + jnp.where(early, wide(low_a), wide(low_b)) + jnp.where(early, wide(high_a), wide(high_b))
    total = total.astype(jnp.bfloat16).astype(jnp.float32)
    o_ref[0] = (gate_ref[...] * total).astype(o_ref.dtype)


def finish(meta, gate, piece, out=None):
    own, low, low_a, high, high_b = piece
    rows, width = own.shape
    steps = 4
    tile = width // steps
    half = steps // 2
    first = lambda i: jnp.minimum(i, half - 1)
    second = lambda i: jnp.maximum(i - half, 0)
    place = lambda i, m: 2 * lax.rem(m[1] + i, steps) + m[0]
    specs = [
        pl.BlockSpec((1, tile), lambda i, m: (0, place(i, m))),
        pl.BlockSpec((rows, tile), lambda i, m: (0, i)),
        pl.BlockSpec((None, rows, tile), lambda i, m: (1, 0, second(i))),
        pl.BlockSpec((rows, tile), lambda i, m: (0, first(i))),
        pl.BlockSpec((None, rows, tile), lambda i, m: (1, 0, first(i))),
        pl.BlockSpec((rows, tile), lambda i, m: (0, second(i))),
    ]
    args = [meta, gate, own, low, low_a, high, high_b]
    alias = {}
    if out is not None:
        alias = {len(args): 0}
        args.append(out)
        specs.append(pl.BlockSpec(memory_space=pl.ANY))
    return pl.pallas_call(
        finish_kernel,
        grid_spec=pltpu.PrefetchScalarGridSpec(
            num_scalar_prefetch=1,
            grid=(steps,),
            in_specs=specs,
            out_specs=pl.BlockSpec((1, rows, tile), lambda i, m: (0, 0, place(i, m))),
        ),
        out_shape=jax.ShapeDtypeStruct((1, rows, 2 * width), jnp.bfloat16),
        input_output_aliases=alias,
        compiler_params=params(12 * MIB),
        cost_estimate=pl.CostEstimate(flops=4 * rows * width, bytes_accessed=8 * rows * width, transcendentals=0),
    )(*args)


def local(queries, keys, values, out_weight, gate, kv_frames):
    rows, width = queries.shape[1:]
    n_y, n_z, n_l = lax.axis_size("yh"), lax.axis_size("z"), lax.axis_size("yl")
    n = n_y * n_z
    cols = width // n
    slots = kv_frames.shape[1]
    axes = ("yh", "z", "x", "yl", "c")
    my_y, my_z, my_x, my_l, my_c = (lax.axis_index(a).astype(jnp.int32) for a in axes)
    after = lax.optimization_barrier

    def shift(array, axes, size, by):
        return lax.ppermute(array, axes, [(i, (i + by) % size) for i in range(size)])

    up = lambda array: shift(array, "z", n_z, 1)
    down = lambda array: shift(array, "z", n_z, n_z - 1)
    swap = lambda array: shift(array, "c", 2, 1)

    weight = lax.dynamic_slice_in_dim(out_weight, my_z * (n_y * cols), n_y * cols, 0)
    part = weight.shape[1] // 2
    ring, n_x = n_y * n_l, lax.axis_size("x")
    right = lambda *arrays: shift(jnp.concatenate(arrays, 0), "x", n_x, 1)
    left = lambda *arrays: shift(jnp.concatenate(arrays, 0), "x", n_x, n_x - 1)
    lower, upper = weight[:, :part].T, weight[:, part:].T
    lower, upper, queries = after((lower, upper, queries))
    far_l, far_u = shift(lower, ("yh", "yl"), ring, 1), shift(upper, ("yh", "yl"), ring, ring - 1)
    near_l, near_u = right(lower), left(upper)
    parts = layout(queries[0], keys[0], values[0], n_y, n_z).reshape(n, 3, rows, cols)
    parts, far_l, far_u, near_l, near_u = after((parts, far_l, far_u, near_l, near_u))
    parts = lax.all_to_all(parts, ("yh", "z"), 0, 0, tiled=True)
    held = jnp.concatenate([lower, upper, near_l, near_u, far_l, far_u], 0)
    low, high = right(upper, near_l, far_l), left(lower, near_u, far_u)
    near = [held, low, high]
    near = near + [swap(piece) for piece in near]
    far = [right(far_u, low[2 * part :]), left(far_l, high[2 * part :])]
    rows_of = lambda *spots: [(buffer, row * part) for buffer, row in spots]
    near_spots = [rows_of(*pair) for pair in (((0, 0), (0, 1)), ((2, 0), (0, 3)), ((1, 1), (2, 1)), ((0, 2), (1, 0)))]
    far_spots = [rows_of(*pair) for pair in (((0, 4), (0, 5)), ((4, 0), (2, 2)), ((3, 1), (4, 1)), ((1, 2), (3, 0)))]

    table = kv_frames.reshape(-1)
    meta = jnp.concatenate([jnp.stack([my_y, my_z]), table])
    parts, near = after((parts, near))
    theirs, mine = attend(meta, parts, slots, n_y)
    other = shift(theirs, "yh", n_y, 1)

    def relay(sent):
        stay, to_up, to_down, late_up, late_down = sent
        return stay, up(to_up), down(to_down), late_up, late_down

    def last(relayed):
        stay, low, high, late_up, late_down = relayed
        late_up, late_down = add_relayed(late_up, low, late_down, high)
        return stay, low, up(late_up), high, down(late_down)

    here = jnp.stack([my_y, my_c])
    other, far = after((other, far))
    far = near[:3] + far + near[3:] + [swap(piece) for piece in far]
    sent = relay(project(here, mine, other, near, near_spots, part))
    sent_far = relay(project(here, mine, other, far, far_spots, part))
    out = finish(jnp.stack([my_l, my_x]), gate, last(sent))
    return finish(jnp.stack([1 - my_l, my_x]), gate, last(sent_far), out)


def solution(mesh):
    fine = Mesh(mesh.devices.reshape(2, 4, 4, 2, 2), ("yh", "z", "x", "yl", "c"))
    frame, batch = ("yh", "z"), ("x", "yl", "c")
    act = P(batch, frame, None)
    return jax.shard_map(
        local,
        mesh=fine,
        in_specs=(act, act, act, P(None, batch), P(batch, None), P()),
        out_specs=act,
        check_vma=False,
    )
```

time: 165 us -> 158 us (0.958)
  between operations: 13.5 us -> 0.13 us
  starting transfers between devices: 24.3 us -> 35.3 us
  Pallas kernels: 51.3 us -> 44 us
  local copies, waits for them, and re-layouts: 5.81 us -> 12.9 us
  waiting for transfers between devices: 66.4 us -> 61.7 us
    all_to_all x1, waiting for transfers between devices: 43.5 us -> 7 us  [local(): parts = lax.all_to_all(parts, ('yh', 'z'), 0, 0, tiled=True)]
    ppermute x11 -> x22, waiting for transfers between devices: 22.9 us -> 54.7 us  [shift(): lax.ppermute(array, axes, [(i, (i + by) % size) for i in range(size)])]
    ppermute x11 -> x22, starting transfers between devices: 15.9 us -> 27 us  [shift(): lax.ppermute(array, axes, [(i, (i + by) % size) for i in range(size)])]
    unnamed x21 -> x30, local copies, waits for them, and re-layouts: 4.54 us -> 8.75 us
    pallas_call x2 -> x1, Pallas kernels: 12 us -> 8.56 us  [attend(): pl.pallas_call(functools.partial(attend_kernel, slots=slots), grid_spec=p...]
    pallas_call x2, Pallas kernels: 4.4 us -> 2.05 us  [add_relayed(): pl.pallas_call(add_kernel, grid=(steps,), in_specs=[flat, lead, flat, lea...]
    slice x0 -> x2, local copies, waits for them, and re-layouts: none -> 2.06 us  [local(): far = [right(far_u, low[2 * part:]), left(far_l, high[2 * part:])]]
    pallas_call x3 -> x2, Pallas kernels: 22.4 us -> 20.5 us  [project(): pl.pallas_call(functools.partial(project_kernel, spots=spots, n_piece=len...]
  transfers between devices with their start and end apart: 14 -> 23, of which waited for: 9 -> 9; matrix products, arithmetic and copies ran while one was open for 1% -> 7% of each run, Pallas kernels for 29% -> 25%
where the time goes in v4:
time: 158 us; the launch traced here: 157 us
  waiting for transfers between devices  61.7 us (39%)
  Pallas kernels  44 us (28%)
  starting transfers between devices  35.3 us (22%)
  local copies, waits for them, and re-layouts  12.9 us (8%)
  other arithmetic  3.45 us (2%)
    ppermute x22, waiting for transfers between devices, shift(): lax.ppermute(array, axes, [(i, (i + by) % size) for i in range(size)])  54.7 us
    ppermute x22, starting transfers between devices, shift(): lax.ppermute(array, axes, [(i, (i + by) % size) for i in range(size)])  27 us
    pallas_call x2, Pallas kernels, project(): pl.pallas_call(functools.partial(project_kernel, spots=spots, n_piece=len...  20.5 us
    unnamed x30, local copies, waits for them, and re-layouts  8.75 us
    pallas_call x1, Pallas kernels, attend(): pl.pallas_call(functools.partial(attend_kernel, slots=slots), grid_spec=p...  8.56 us
    pallas_call x2, Pallas kernels, finish(): pl.pallas_call(finish_kernel, grid_spec=pltpu.PrefetchScalarGridSpec(num_...  8.31 us
    all_to_all x1, starting transfers between devices, local(): parts = lax.all_to_all(parts, ('yh', 'z'), 0, 0, tiled=True)  8.28 us
    all_to_all x1, waiting for transfers between devices, local(): parts = lax.all_to_all(parts, ('yh', 'z'), 0, 0, tiled=True)  7 us
  transfers between devices with their start and end apart: 23, of which 9 were waited for; matrix products, arithmetic and copies ran while one was open for 7% of the time, Pallas kernels for 25%

profile of v4, /device:TPU:24, one launch (start us, length us, event | category | flops | bytes accessed | tf_op | source)
XLA Modules:
  0.0 157.5 jit_solution(3055170344070310900)
XLA Ops:
  0.0 1.2 dynamic-slice_bitcast_fusion
  1.2 1.6 collective-permute-start.2
  2.7 0.2 collective-permute-start
  3.0 1.7 %collective-permute-start.3 = (bf16[160,1280]{1,0:T(8,128)(2,1)S(1)}, bf16[160,1280]{1,0:T(8,128)(2,1)S(1)}, u32[]{:S(2)}, u32[]{:S(2)}) collective-permute-start(bf16[160,1280]{1,0:T(8,128)(2,1)S(1)} %get-tuple-element.41), channel_id=1, source_target_pairs={{0,12},{4,0},{8,4},{12,8},{1,13},{5,1},{9,5},{13,9},{2,14},{6,2},{... | collective-permute-start | bytes 1228808 | tf_op jit(solution)/shard_map/ppermute | solution.py:280
  4.6 1.9 %collective-permute-start.1 = (bf16[160,1280]{1,0:T(8,128)(2,1)S(1)}, bf16[160,1280]{1,0:T(8,128)(2,1)S(1)}, u32[]{:S(2)}, u32[]{:S(2)}) collective-permute-start(bf16[160,1280]{1,0:T(8,128)(2,1)S(1)} %get-tuple-element.41), channel_id=1, source_target_pairs={{0,66},{2,0},{64,2},{66,64},{1,67},{3,1},{65,3},{67,65},{4,70},{6,... | collective-permute-start | bytes 1228808 | tf_op jit(solution)/shard_map/ppermute | solution.py:280
  6.5 4.6 %shard_map.64 = bf16[2,4,3,128,640]{4,3,2,1,0:T(8,128)(2,1)} custom-call(bf16[128,5120]{1,0:T(8,128)(2,1)} %bitcast.15, bf16[128,5120]{1,0:T(8,128)(2,1)} %bitcast.16, bf16[128,5120]{1,0:T(8,128)(2,1)} %bitcast.17), custom_call_target="tpu_custom_call" | custom-call | bytes 7864320 | tf_op jit(solution)/shard_map/pallas_call | solution.py:34
  11.1 0.8 constant_dynamic-update-slice_fusion.5
  11.9 0.8 constant_dynamic-update-slice_fusion.4
  12.7 1.0 collective-permute-done.2
  13.7 0.0 collective-permute-done
  13.7 0.0 collective-permute-done.3
  13.7 2.7 %collective-permute-done.1 = bf16[160,1280]{1,0:T(8,128)(2,1)S(1)} collective-permute-done((bf16[160,1280]{1,0:T(8,128)(2,1)S(1)}, bf16[160,1280]{1,0:T(8,128)(2,1)S(1)}, u32[]{:S(2)}, u32[]{:S(2)}) %collective-permute-start.1) | collective-permute-done | bytes 409632 | tf_op jit(solution)/shard_map/ppermute | solution.py:280
  16.4 8.3 %all-to-all-start = ((bf16[8,3,128,640]{3,2,1,0:T(8,128)(2,1)}), bf16[8,3,128,640]{3,2,1,0:T(8,128)(2,1)}, u32[]{:S(2)}, u32[]{:S(2)}) async-start(bf16[8,3,128,640]{3,2,1,0:T(8,128)(2,1)} %bitcast.14), calls=%async_computation | async-start | bytes 7864320 | tf_op jit(solution)/shard_map/all_to_all | solution.py:297
  24.6 0.1 pad_maximum_fusion
  24.7 0.0 copy-start.11
  24.7 0.3 collective-permute-start.4
  25.1 0.1 pad_maximum_fusion.1
  25.2 3.0 %collective-permute-start.5 = (bf16[480,1280]{1,0:T(8,128)(2,1)S(1)}, bf16[480,1280]{1,0:T(8,128)(2,1)}, u32[]{:S(2)}, u32[]{:S(2)}) collective-permute-start(bf16[480,1280]{1,0:T(8,128)(2,1)S(1)} %pad_maximum_fusion.1), channel_id=1, source_target_pairs={{0,12},{4,0},{8,4},{12,8},{1,13},{5,1},{9,5},{13,9},{2,14},{6,2},{... | collective-permute-start | bytes 3686408 | tf_op jit(solution)/shard_map/ppermute | solution.py:280
  28.2 0.8 constant_dynamic-update-slice_fusion.3
  29.0 0.8 constant_dynamic-update-slice_fusion.2
  29.7 0.8 constant_dynamic-update-slice_fusion.1
  30.5 0.8 constant_dynamic-update-slice_fusion.refs_0_
  31.4 21.2 %collective-permute-done.4.refs_1_ = bf16[480,1280]{1,0:T(8,128)(2,1)} collective-permute-done((bf16[480,1280]{1,0:T(8,128)(2,1)S(1)}, bf16[480,1280]{1,0:T(8,128)(2,1)}, u32[]{:S(2)}, u32[]{:S(2)}) %collective-permute-start.4) | collective-permute-done | bytes 1228832 | tf_op jit(solution)/shard_map/ppermute | solution.py:280
  52.6 0.5 collective-permute-start.8
  53.1 0.1 copy.9
  53.2 0.1 reshape.6
  53.3 1.0 slice.16
  54.3 0.9 pad_maximum_fusion.2
  55.3 1.0 slice.17
  56.3 1.0 pad_maximum_fusion.3
  57.3 3.2 %collective-permute-start.11 = (bf16[320,1280]{1,0:T(8,128)(2,1)}, bf16[320,1280]{1,0:T(8,128)(2,1)}, u32[]{:S(2)}, u32[]{:S(2)}) collective-permute-start(bf16[320,1280]{1,0:T(8,128)(2,1)} %pad_maximum_fusion.3), channel_id=1, source_target_pairs={{0,12},{4,0},{8,4},{12,8},{1,13},{5,1},{9,5},{13,9},{2,14},{6,2},{... | collective-permute-start | bytes 2457608 | tf_op jit(solution)/shard_map/ppermute | solution.py:280
  60.5 0.6 pad_add_fusion.2.meta
  61.1 0.0 collective-permute-done.7.refs_6_.refs_4_
  61.1 0.0 collective-permute-done.8.refs_7_.refs_5_
  61.2 0.0 collective-permute-done.6.refs_5_.refs_3_
  61.2 7.0 %all-to-all-done.q_ref.k_ref.v_ref = bf16[8,3,128,640]{3,2,1,0:T(8,128)(2,1)} async-done(((bf16[8,3,128,640]{3,2,1,0:T(8,128)(2,1)}), bf16[8,3,128,640]{3,2,1,0:T(8,128)(2,1)}, u32[]{:S(2)}, u32[]{:S(2)}) %all-to-all-start) | async-done | bytes 3932192 | tf_op jit(solution)/shard_map/all_to_all | solution.py:297
  68.2 8.6 %shard_map.65 = (bf16[4,128,640]{2,1,0:T(8,128)(2,1)}, bf16[4,128,640]{2,1,0:T(8,128)(2,1)}) custom-call(s32[98]{0:T(128)} %pad_add_fusion.2.meta, bf16[8,3,128,640]{3,2,1,0:T(8,128)(2,1)} %all-to-all-done.q_ref.k_ref.v_ref, bf16[8,3,128,640]{3,2,1,0:T(8,128)(2,1)} %all-to-all-done.q_ref.k_ref.v_ref, bf16[8,3,128,640]{3,2,1,0:T(8,128)(2,1)} %all-to-all-done.q_ref.k_ref.v_ref), custom_call_target="tpu_custom_call" | custom-call | flops 1006632960 | bytes 5242880 | tf_op jit(solution)/shard_map/pallas_call | solution.py:92
  76.7 0.9 collective-permute-start.9
  77.7 0.7 collective-permute-done.11.refs_4_
  78.4 16.4 %collective-permute-done.9.other_ref = bf16[4,128,640]{2,1,0:T(8,128)(2,1)S(1)} collective-permute-done((bf16[4,128,640]{2,1,0:T(8,128)(2,1)}, bf16[4,128,640]{2,1,0:T(8,128)(2,1)S(1)}, u32[]{:S(2)}, u32[]{:S(2)}) %collective-permute-start.9) | collective-permute-done | bytes 655392 | tf_op jit(solution)/shard_map/ppermute | solution.py:280
  94.7 0.0 collective-permute-start.12
  94.7 0.5 collective-permute-start.13
  95.3 0.7 pad_add_fusion.1.meta
  95.9 10.2 %shard_map.68 = (bf16[128,2560]{1,0:T(8,128)(2,1)}, bf16[2,128,1280]{2,1,0:T(8,128)(2,1)}, bf16[2,128,1280]{2,1,0:T(8,128)(2,1)}, bf16[128,1280]{1,0:T(8,128)(2,1)}, bf16[128,1280]{1,0:T(8,128)(2,1)}) custom-call(s32[2]{0:T(128)} %pad_add_fusion.1.meta, bf16[4,128,640]{2,1,0:T(8,128)(2,1)} %get-tuple-element.48.mine_ref, bf16[4,128,640]{2,1,0:T(8,128)(2,1)} %copy-done.10, ...), custom_call_target="tpu_custom_call" | custom-call | flops 3355443200 | bytes 11796480 | tf_op jit(solution)/shard_map/pallas_call | solution.py:174
  106.1 1.3 collective-permute-start.18
  107.4 2.0 %collective-permute-start.19 = (bf16[2,128,1280]{2,1,0:T(8,128)(2,1)}, bf16[2,128,1280]{2,1,0:T(8,128)(2,1)S(1)}, u32[]{:S(2)}, u32[]{:S(2)}) collective-permute-start(bf16[2,128,1280]{2,1,0:T(8,128)(2,1)} %get-tuple-element.70), channel_id=1, source_target_pairs={{0,48},{16,0},{32,16},{48,32},{1,49},{17,1},{33,17},{49,33},{2,50}... | collective-permute-start | bytes 1966088 | tf_op jit(solution)/shard_map/ppermute | solution.py:280
  109.5 0.9 copy-done.8
  110.3 0.9 copy-done.9
  111.3 10.3 %shard_map.66 = (bf16[128,2560]{1,0:T(8,128)(2,1)}, bf16[2,128,1280]{2,1,0:T(8,128)(2,1)}, bf16[2,128,1280]{2,1,0:T(8,128)(2,1)}, bf16[128,1280]{1,0:T(8,128)(2,1)}, bf16[128,1280]{1,0:T(8,128)(2,1)}) custom-call(s32[2]{0:T(128)} %pad_add_fusion.1.meta, bf16[4,128,640]{2,1,0:T(8,128)(2,1)} %get-tuple-element.48.mine_ref, bf16[4,128,640]{2,1,0:T(8,128)(2,1)} %copy-done.10, ...), custom_call_target="tpu_custom_call" | custom-call | flops 3355443200 | bytes 11796480 | tf_op jit(solution)/shard_map/pallas_call | solution.py:174
  121.6 0.1 collective-permute-start.14
  121.7 3.2 %collective-permute-start.15 = (bf16[2,128,1280]{2,1,0:T(8,128)(2,1)}, bf16[2,128,1280]{2,1,0:T(8,128)(2,1)S(1)}, u32[]{:S(2)}, u32[]{:S(2)}) collective-permute-start(bf16[2,128,1280]{2,1,0:T(8,128)(2,1)} %get-tuple-element.63), channel_id=1, source_target_pairs={{0,48},{16,0},{32,16},{48,32},{1,49},{17,1},{33,17},{49,33},{2,50}... | collective-permute-start | bytes 1966088 | tf_op jit(solution)/shard_map/ppermute | solution.py:280
  124.9 1.0 copy-done.5
  125.9 1.0 shard_map.69
  126.9 3.2 %collective-permute-start.21 = (bf16[128,1280]{1,0:T(8,128)(2,1)}, bf16[128,1280]{1,0:T(8,128)(2,1)}, u32[]{:S(2)}, u32[]{:S(2)}) collective-permute-start(bf16[128,1280]{1,0:T(8,128)(2,1)} %get-tuple-element.72), channel_id=1, source_target_pairs={{0,48},{16,0},{32,16},{48,32},{1,49},{17,1},{33,17},{49,33},{2,50}... | collective-permute-start | bytes 983048 | tf_op jit(solution)/shard_map/ppermute | solution.py:280
  130.2 10.6 %collective-permute-done.14.x_ref.low_b = bf16[2,128,1280]{2,1,0:T(8,128)(2,1)S(1)} collective-permute-done((bf16[2,128,1280]{2,1,0:T(8,128)(2,1)}, bf16[2,128,1280]{2,1,0:T(8,128)(2,1)S(1)}, u32[]{:S(2)}, u32[]{:S(2)}) %collective-permute-start.14) | collective-permute-done | bytes 655392 | tf_op jit(solution)/shard_map/ppermute | solution.py:280
  140.8 1.0 copy-done.2
  141.8 1.0 copy-done.3
  142.7 1.0 shard_map.67
  143.8 3.2 %collective-permute-start.17 = (bf16[128,1280]{1,0:T(8,128)(2,1)}, bf16[128,1280]{1,0:T(8,128)(2,1)}, u32[]{:S(2)}, u32[]{:S(2)}) collective-permute-start(bf16[128,1280]{1,0:T(8,128)(2,1)} %get-tuple-element.65), channel_id=1, source_target_pairs={{0,48},{16,0},{32,16},{48,32},{1,49},{17,1},{33,17},{49,33},{2,50}... | collective-permute-start | bytes 983048 | tf_op jit(solution)/shard_map/ppermute | solution.py:280
  147.0 0.1 pad_add_fusion
  147.1 0.7 collective-permute-done.20.low_a
  147.8 4.2 %shard_map.70.refs_0_ = bf16[1,128,5120]{2,1,0:T(8,128)(2,1)} custom-call(s32[2]{0:T(128)S(1)} %get-tuple-element.76.meta, f32[1,5120]{1,0:T(1,128)S(1)} %copy-done.6, bf16[128,2560]{1,0:T(8,128)(2,1)S(1)} %copy-done, bf16[2,128,1280]{2,1,0:T(8,128)(2,1)S(1)} %collective-permute-done.18.x_ref.low_b, bf16[128,1280]{1,0:T(8,128)(2,1)} %collective-permute-done.20.low_a, ...), custom_call_target="tpu_custom_call" | custom-call | flops 1310720 | bytes 2621440 | tf_op jit(solution)/shard_map/pallas_call | solution.py:254
  151.9 1.4 collective-permute-done.16.low_a
  153.3 4.2 %shard_map.71 = bf16[1,128,5120]{2,1,0:T(8,128)(2,1)} custom-call(s32[2]{0:T(128)S(1)} %get-tuple-element.75.meta, f32[1,5120]{1,0:T(1,128)S(1)} %copy-done.6, bf16[128,2560]{1,0:T(8,128)(2,1)S(1)} %copy-done.1, bf16[2,128,1280]{2,1,0:T(8,128)(2,1)S(1)} %collective-permute-done.14.x_ref.low_b, ...), custom_call_target="tpu_custom_call", output_to_operand_aliasing={{}: (7, {})} | custom-call | flops 1310720 | bytes 2621440 | tf_op jit(solution)/shard_map/pallas_call | solution.py:254
  (32 shorter events, 0.1 us)
Async XLA Ops:
  1.2 12.5 %collective-permute-start.2 = (bf16[160,1280]{1,0:T(8,128)(2,1)S(1)}, bf16[160,1280]{1,0:T(8,128)(2,1)S(1)}, u32[]{:S(2)}, u32[]{:S(2)}) collective-permute-start(bf16[160,1280]{1,0:T(8,128)(2,1)S(1)} %get-tuple-element.40), channel_id=1, source_target_pairs={{0,4},{4,8},{8,12},{12,0},{1,5},{5,9},{9,13},{13,1},{2,6},{6,10},{... | collective-permute-start | bytes 1228808 | tf_op jit(solution)/shard_map/ppermute | solution.py:280
  2.7 10.9 %collective-permute-start = (bf16[160,1280]{1,0:T(8,128)(2,1)S(1)}, bf16[160,1280]{1,0:T(8,128)(2,1)S(1)}, u32[]{:S(2)}, u32[]{:S(2)}) collective-permute-start(bf16[160,1280]{1,0:T(8,128)(2,1)S(1)} %get-tuple-element.40), channel_id=1, source_target_pairs={{0,2},{2,64},{64,66},{66,0},{1,3},{3,65},{65,67},{67,1},{4,6},{6,6... | collective-permute-start | bytes 1228808 | tf_op jit(solution)/shard_map/ppermute | solution.py:280
  3.0 10.7 %collective-permute-start.3 = (bf16[160,1280]{1,0:T(8,128)(2,1)S(1)}, bf16[160,1280]{1,0:T(8,128)(2,1)S(1)}, u32[]{:S(2)}, u32[]{:S(2)}) collective-permute-start(bf16[160,1280]{1,0:T(8,128)(2,1)S(1)} %get-tuple-element.41), channel_id=1, source_target_pairs={{0,12},{4,0},{8,4},{12,8},{1,13},{5,1},{9,5},{13,9},{2,14},{6,2},{... | collective-permute-start | bytes 1228808 | tf_op jit(solution)/shard_map/ppermute | solution.py:280
  4.6 11.7 %collective-permute-start.1 = (bf16[160,1280]{1,0:T(8,128)(2,1)S(1)}, bf16[160,1280]{1,0:T(8,128)(2,1)S(1)}, u32[]{:S(2)}, u32[]{:S(2)}) collective-permute-start(bf16[160,1280]{1,0:T(8,128)(2,1)S(1)} %get-tuple-element.41), channel_id=1, source_target_pairs={{0,66},{2,0},{64,2},{66,64},{1,67},{3,1},{65,3},{67,65},{4,70},{6,... | collective-permute-start | bytes 1228808 | tf_op jit(solution)/shard_map/ppermute | solution.py:280
  16.4 51.8 %all-to-all-start = ((bf16[8,3,128,640]{3,2,1,0:T(8,128)(2,1)}), bf16[8,3,128,640]{3,2,1,0:T(8,128)(2,1)}, u32[]{:S(2)}, u32[]{:S(2)}) async-start(bf16[8,3,128,640]{3,2,1,0:T(8,128)(2,1)} %bitcast.14), calls=%async_computation | async-start | bytes 7864320 | tf_op jit(solution)/shard_map/all_to_all | solution.py:297
  24.7 28.4 %copy-start.11 = (s32[16,6]{0,1:T(8,128)S(1)}, s32[16,6]{0,1:T(8,128)}, u32[]{:S(2)}) copy-start(s32[16,6]{0,1:T(8,128)} %param.11) | copy-start | bytes 1156
  24.7 27.9 %collective-permute-start.4 = (bf16[480,1280]{1,0:T(8,128)(2,1)S(1)}, bf16[480,1280]{1,0:T(8,128)(2,1)}, u32[]{:S(2)}, u32[]{:S(2)}) collective-permute-start(bf16[480,1280]{1,0:T(8,128)(2,1)S(1)} %pad_maximum_fusion), channel_id=1, source_target_pairs={{0,4},{4,8},{8,12},{12,0},{1,5},{5,9},{9,13},{13,1},{2,6},{6,10},{... | collective-permute-start | bytes 3686408 | tf_op jit(solution)/shard_map/ppermute | solution.py:280
  25.2 27.5 %collective-permute-start.5 = (bf16[480,1280]{1,0:T(8,128)(2,1)S(1)}, bf16[480,1280]{1,0:T(8,128)(2,1)}, u32[]{:S(2)}, u32[]{:S(2)}) collective-permute-start(bf16[480,1280]{1,0:T(8,128)(2,1)S(1)} %pad_maximum_fusion.1), channel_id=1, source_target_pairs={{0,12},{4,0},{8,4},{12,8},{1,13},{5,1},{9,5},{13,9},{2,14},{6,2},{... | collective-permute-start | bytes 3686408 | tf_op jit(solution)/shard_map/ppermute | solution.py:280
  31.4 29.8 %collective-permute-start.6 = (bf16[960,1280]{1,0:T(8,128)(2,1)}, bf16[960,1280]{1,0:T(8,128)(2,1)S(1)}, u32[]{:S(2)}, u32[]{:S(2)}) collective-permute-start(bf16[960,1280]{1,0:T(8,128)(2,1)} %constant_dynamic-update-slice_fusion.refs_0_), channel_id=1, source_target_pairs={{0,1},{1,0},{2,3},{3,2},{4,5},{5,4},{6,7},{7,6},{8,9},{9,8},{10,11... | collective-permute-start | bytes 7372808 | tf_op jit(solution)/shard_map/ppermute | solution.py:280
  52.6 8.5 %collective-permute-start.7 = (bf16[480,1280]{1,0:T(8,128)(2,1)}, bf16[480,1280]{1,0:T(8,128)(2,1)}, u32[]{:S(2)}, u32[]{:S(2)}) collective-permute-start(bf16[480,1280]{1,0:T(8,128)(2,1)} %collective-permute-done.4.refs_1_), channel_id=1, source_target_pairs={{0,1},{1,0},{2,3},{3,2},{4,5},{5,4},{6,7},{7,6},{8,9},{9,8},{10,11... | collective-permute-start | bytes 3686408 | tf_op jit(solution)/shard_map/ppermute | solution.py:280
  52.6 8.5 %collective-permute-start.8 = (bf16[480,1280]{1,0:T(8,128)(2,1)}, bf16[480,1280]{1,0:T(8,128)(2,1)}, u32[]{:S(2)}, u32[]{:S(2)}) collective-permute-start(bf16[480,1280]{1,0:T(8,128)(2,1)} %collective-permute-done.5.refs_2_), channel_id=1, source_target_pairs={{0,1},{1,0},{2,3},{3,2},{4,5},{5,4},{6,7},{7,6},{8,9},{9,8},{10,11... | collective-permute-start | bytes 3686408 | tf_op jit(solution)/shard_map/ppermute | solution.py:280
  55.3 22.4 %collective-permute-start.10 = (bf16[320,1280]{1,0:T(8,128)(2,1)}, bf16[320,1280]{1,0:T(8,128)(2,1)}, u32[]{:S(2)}, u32[]{:S(2)}) collective-permute-start(bf16[320,1280]{1,0:T(8,128)(2,1)} %pad_maximum_fusion.2), channel_id=1, source_target_pairs={{0,4},{4,8},{8,12},{12,0},{1,5},{5,9},{9,13},{13,1},{2,6},{6,10},{... | collective-permute-start | bytes 2457608 | tf_op jit(solution)/shard_map/ppermute | solution.py:280
  57.3 21.1 %collective-permute-start.11 = (bf16[320,1280]{1,0:T(8,128)(2,1)}, bf16[320,1280]{1,0:T(8,128)(2,1)}, u32[]{:S(2)}, u32[]{:S(2)}) collective-permute-start(bf16[320,1280]{1,0:T(8,128)(2,1)} %pad_maximum_fusion.3), channel_id=1, source_target_pairs={{0,12},{4,0},{8,4},{12,8},{1,13},{5,1},{9,5},{13,9},{2,14},{6,2},{... | collective-permute-start | bytes 2457608 | tf_op jit(solution)/shard_map/ppermute | solution.py:280
  61.2 15.6 %copy-start.7 = (bf16[960,1280]{1,0:T(8,128)(2,1)}, bf16[960,1280]{1,0:T(8,128)(2,1)S(1)}, u32[]{:S(2)}) copy-start(bf16[960,1280]{1,0:T(8,128)(2,1)S(1)} %collective-permute-done.6.refs_5_.refs_3_) | copy-start | bytes 7372804
  76.7 18.0 %collective-permute-start.9 = (bf16[4,128,640]{2,1,0:T(8,128)(2,1)}, bf16[4,128,640]{2,1,0:T(8,128)(2,1)S(1)}, u32[]{:S(2)}, u32[]{:S(2)}) collective-permute-start(bf16[4,128,640]{2,1,0:T(8,128)(2,1)} %get-tuple-element.49), channel_id=1, source_target_pairs={{0,64},{64,0},{1,65},{65,1},{2,66},{66,2},{3,67},{67,3},{4,68},{68... | collective-permute-start | bytes 1966088 | tf_op jit(solution)/shard_map/ppermute | solution.py:280
  94.7 1.2 copy-start.10
  94.7 14.7 %collective-permute-start.12 = (bf16[320,1280]{1,0:T(8,128)(2,1)}, bf16[320,1280]{1,0:T(8,128)(2,1)S(1)}, u32[]{:S(2)}, u32[]{:S(2)}) collective-permute-start(bf16[320,1280]{1,0:T(8,128)(2,1)} %collective-permute-done.10.refs_3_), channel_id=1, source_target_pairs={{0,1},{1,0},{2,3},{3,2},{4,5},{5,4},{6,7},{7,6},{8,9},{9,8},{10,11... | collective-permute-start | bytes 2457608 | tf_op jit(solution)/shard_map/ppermute | solution.py:280
  94.7 14.7 %collective-permute-start.13 = (bf16[320,1280]{1,0:T(8,128)(2,1)}, bf16[320,1280]{1,0:T(8,128)(2,1)S(1)}, u32[]{:S(2)}, u32[]{:S(2)}) collective-permute-start(bf16[320,1280]{1,0:T(8,128)(2,1)} %collective-permute-done.11.refs_4_), channel_id=1, source_target_pairs={{0,1},{1,0},{2,3},{3,2},{4,5},{5,4},{6,7},{7,6},{8,9},{9,8},{10,11... | collective-permute-start | bytes 2457608 | tf_op jit(solution)/shard_map/ppermute | solution.py:280
  106.1 18.8 %collective-permute-start.18 = (bf16[2,128,1280]{2,1,0:T(8,128)(2,1)}, bf16[2,128,1280]{2,1,0:T(8,128)(2,1)S(1)}, u32[]{:S(2)}, u32[]{:S(2)}) collective-permute-start(bf16[2,128,1280]{2,1,0:T(8,128)(2,1)} %get-tuple-element.67), channel_id=1, source_target_pairs={{0,16},{16,32},{32,48},{48,0},{1,17},{17,33},{33,49},{49,1},{2,18}... | collective-permute-start | bytes 1966088 | tf_op jit(solution)/shard_map/ppermute | solution.py:280
  107.4 17.5 %copy-start.4 = (bf16[128,1280]{1,0:T(8,128)(2,1)S(1)}, bf16[128,1280]{1,0:T(8,128)(2,1)}, u32[]{:S(2)}) copy-start(bf16[128,1280]{1,0:T(8,128)(2,1)} %get-tuple-element.68.a_ref) | copy-start | bytes 983044
  107.4 17.5 %collective-permute-start.19 = (bf16[2,128,1280]{2,1,0:T(8,128)(2,1)}, bf16[2,128,1280]{2,1,0:T(8,128)(2,1)S(1)}, u32[]{:S(2)}, u32[]{:S(2)}) collective-permute-start(bf16[2,128,1280]{2,1,0:T(8,128)(2,1)} %get-tuple-element.70), channel_id=1, source_target_pairs={{0,48},{16,0},{32,16},{48,32},{1,49},{17,1},{33,17},{49,33},{2,50}... | collective-permute-start | bytes 1966088 | tf_op jit(solution)/shard_map/ppermute | solution.py:280
  109.4 0.9 copy-start.8
  110.3 0.9 copy-start.9
  111.3 36.5 %copy-start.6 = (f32[1,5120]{1,0:T(1,128)S(1)}, f32[1,5120]{1,0:T(1,128)}, u32[]{:S(2)}) copy-start(f32[1,5120]{1,0:T(1,128)} %gate_ref.3) | copy-start | bytes 61444
  121.6 26.2 %copy-start = (bf16[128,2560]{1,0:T(8,128)(2,1)S(1)}, bf16[128,2560]{1,0:T(8,128)(2,1)}, u32[]{:S(2)}) copy-start(bf16[128,2560]{1,0:T(8,128)(2,1)} %get-tuple-element.66.own) | copy-start | bytes 1966084
  121.6 19.2 %collective-permute-start.14 = (bf16[2,128,1280]{2,1,0:T(8,128)(2,1)}, bf16[2,128,1280]{2,1,0:T(8,128)(2,1)S(1)}, u32[]{:S(2)}, u32[]{:S(2)}) collective-permute-start(bf16[2,128,1280]{2,1,0:T(8,128)(2,1)} %get-tuple-element.60), channel_id=1, source_target_pairs={{0,16},{16,32},{32,48},{48,0},{1,17},{17,33},{33,49},{49,1},{2,18}... | collective-permute-start | bytes 1966088 | tf_op jit(solution)/shard_map/ppermute | solution.py:280
  121.7 19.1 %collective-permute-start.15 = (bf16[2,128,1280]{2,1,0:T(8,128)(2,1)}, bf16[2,128,1280]{2,1,0:T(8,128)(2,1)S(1)}, u32[]{:S(2)}, u32[]{:S(2)}) collective-permute-start(bf16[2,128,1280]{2,1,0:T(8,128)(2,1)} %get-tuple-element.63), channel_id=1, source_target_pairs={{0,48},{16,0},{32,16},{48,32},{1,49},{17,1},{33,17},{49,33},{2,50}... | collective-permute-start | bytes 1966088 | tf_op jit(solution)/shard_map/ppermute | solution.py:280
  124.9 1.0 copy-start.5
  126.9 20.8 %collective-permute-start.20 = (bf16[128,1280]{1,0:T(8,128)(2,1)}, bf16[128,1280]{1,0:T(8,128)(2,1)}, u32[]{:S(2)}, u32[]{:S(2)}) collective-permute-start(bf16[128,1280]{1,0:T(8,128)(2,1)} %get-tuple-element.71), channel_id=1, source_target_pairs={{0,16},{16,32},{32,48},{48,0},{1,17},{17,33},{33,49},{49,1},{2,18}... | collective-permute-start | bytes 983048 | tf_op jit(solution)/shard_map/ppermute | solution.py:280
  126.9 20.8 %collective-permute-start.21 = (bf16[128,1280]{1,0:T(8,128)(2,1)}, bf16[128,1280]{1,0:T(8,128)(2,1)}, u32[]{:S(2)}, u32[]{:S(2)}) collective-permute-start(bf16[128,1280]{1,0:T(8,128)(2,1)} %get-tuple-element.72), channel_id=1, source_target_pairs={{0,48},{16,0},{32,16},{48,32},{1,49},{17,1},{33,17},{49,33},{2,50}... | collective-permute-start | bytes 983048 | tf_op jit(solution)/shard_map/ppermute | solution.py:280
  140.8 1.0 copy-start.2
  141.7 1.0 copy-start.3
  143.8 9.6 %collective-permute-start.16 = (bf16[128,1280]{1,0:T(8,128)(2,1)}, bf16[128,1280]{1,0:T(8,128)(2,1)}, u32[]{:S(2)}, u32[]{:S(2)}) collective-permute-start(bf16[128,1280]{1,0:T(8,128)(2,1)} %get-tuple-element.64), channel_id=1, source_target_pairs={{0,16},{16,32},{32,48},{48,0},{1,17},{17,33},{33,49},{49,1},{2,18}... | collective-permute-start | bytes 983048 | tf_op jit(solution)/shard_map/ppermute | solution.py:280
  143.8 9.6 %collective-permute-start.17 = (bf16[128,1280]{1,0:T(8,128)(2,1)}, bf16[128,1280]{1,0:T(8,128)(2,1)}, u32[]{:S(2)}, u32[]{:S(2)}) collective-permute-start(bf16[128,1280]{1,0:T(8,128)(2,1)} %get-tuple-element.65), channel_id=1, source_target_pairs={{0,48},{16,0},{32,16},{48,32},{1,49},{17,1},{33,17},{49,33},{2,50}... | collective-permute-start | bytes 983048 | tf_op jit(solution)/shard_map/ppermute | solution.py:280
  147.0 6.3 %copy-start.1 = (bf16[128,2560]{1,0:T(8,128)(2,1)S(1)}, bf16[128,2560]{1,0:T(8,128)(2,1)}, u32[]{:S(2)}) copy-start(bf16[128,2560]{1,0:T(8,128)(2,1)} %get-tuple-element.59.own) | copy-start | bytes 1966084

commit v5 on v4

--- a/solution.py
+++ b/solution.py
@@ -37,13 +37,13 @@
         in_specs=[block] * 3,
         out_specs=pl.BlockSpec((n_y, None, 3, rows, cols), lambda i: (0, i, 0, 0, 0)),
         out_shape=jax.ShapeDtypeStruct((n_y, n_z, 3, rows, cols), q.dtype),
-        compiler_params=params(),
+        compiler_params=params(8 * MIB),
         cost_estimate=pl.CostEstimate(flops=0, bytes_accessed=12 * rows * width, transcendentals=0),
     )(q, k, v)
 
 
-def attend_half(meta, half, q_ref, k_ref, v_ref, o_ref, slots):
-    blocks, rows, width = o_ref.shape
+def attend_kernel(meta, q_ref, k_ref, v_ref, o_ref, *, slots):
+    blocks, rows, width = q_ref.shape
     per = rows // FRAME
     heads = width // HEAD_DIM
     n_key = slots * FRAME
@@ -51,9 +51,9 @@
     lane = lax.broadcasted_iota(jnp.int32, (1, n_key), 1)
     work = []
     for r in range(blocks):
-        block = half * blocks + lax.rem(meta[1] + r, blocks)
+        block = lax.rem(meta[1] + r, blocks)
         for p in range(per):
-            base = 2 + (block * per + p) * slots
+            base = 2 + ((meta[0] * blocks + block) * per + p) * slots
             bias = jnp.zeros((1, n_key), jnp.float32)
             picks = []
             for s in range(slots):
@@ -79,36 +79,40 @@
         o_ref[r, p * FRAME : (p + 1) * FRAME, cols] = (accum / denom).astype(jnp.bfloat16)
 
 
-def attend_kernel(meta, q_ref, k_ref, v_ref, theirs_ref, mine_ref, *, slots):
-    attend_half(meta, 1 - meta[0], q_ref, k_ref, v_ref, theirs_ref, slots)
-    attend_half(meta, meta[0], q_ref, k_ref, v_ref, mine_ref, slots)
-
-
 def attend(meta, parts, slots, n_y):
     blocks, _, rows, width = parts.shape
     n_z = blocks // n_y
     whole = lambda which: pl.BlockSpec((blocks, None, rows, width), lambda i, m: (0, which, 0, 0))
-    work = blocks * rows * slots * FRAME * width
+    work = n_z * rows * slots * FRAME * width
     return pl.pallas_call(
         functools.partial(attend_kernel, slots=slots),
         grid_spec=pltpu.PrefetchScalarGridSpec(
             num_scalar_prefetch=1,
             grid=(1,),
-            in_specs=[whole(0), whole(1), whole(2)],
-            out_specs=[pl.BlockSpec((n_z, rows, width), lambda i, m: (0, 0, 0))] * 2,
-        ),
-        out_shape=[jax.ShapeDtypeStruct((n_z, rows, width), jnp.bfloat16)] * 2,
-        compiler_params=params(),
+            in_specs=[
+                pl.BlockSpec((n_z, None, rows, width), lambda i, m: (m[0], 0, 0, 0)),
+                whole(1),
+                whole(2),
+            ],
+            out_specs=pl.BlockSpec((n_z, rows, width), lambda i, m: (0, 0, 0)),
+        ),
+        out_shape=jax.ShapeDtypeStruct((n_z, rows, width), jnp.bfloat16),
+        compiler_params=params(32 * MIB),
         cost_estimate=pl.CostEstimate(
-            flops=work * 4, bytes_accessed=4 * blocks * rows * width * 2, transcendentals=work // HEAD_DIM
+            flops=work * 4, bytes_accessed=3 * blocks * rows * width * 2, transcendentals=work // HEAD_DIM
         ),
     )(meta, parts, parts, parts)
 
 
-def project_kernel(meta, mine_ref, other_ref, *refs, spots, n_piece):
+def project_kernel(meta, mine_ref, other_ref, *refs, spots, n_piece, paired):
     n_x = len(spots)
     pieces, refs = refs[:n_piece], refs[n_piece:]
-    outs, (act, w_buf, r_buf, a_sem, w_sem, r_sem) = refs[:5], refs[5:]
+    outs, (act, w_buf, r_buf, a_sem, w_sem, r_sem) = refs[:-6], refs[-6:]
+    if paired:
+        stay, up, down, up_late, down_late = outs
+        up, up_next, down, down_next = up.at[0], up.at[1], down.at[0], down.at[1]
+    else:
+        stay, up, up_next, down, down_next, up_late, down_late = outs
     n_z, rows, depth = mine_ref.shape
     tile = w_buf.shape[0] // n_x
     part = tile // 4
@@ -147,15 +151,15 @@
         weight = w_buf[x * tile : (x + 1) * tile]
         total = lax.dot_general(left, weight, NT, preferred_element_type=jnp.float32)
         r_buf[x] = total.astype(r_buf.dtype)
-        stay, up, down, up_late, down_late = outs
         late, col = divmod(x, n_x // 2)
         block = lambda r: r_buf.at[x, pl.ds(r * rows, rows)]
         cols = pl.ds(col * tile, tile)
         targets = [(block(0), stay.at[:, pl.ds(x * tile, tile)])]
         if late:
-            targets += [(block(1), up.at[1, :, cols]), (block(2), down.at[0, :, cols]), (block(3), down_late.at[:, cols])]
+            there = (up_next, down, down_late)
         else:
-            targets += [(block(2), up.at[0, :, cols]), (block(3), down.at[1, :, cols]), (block(1), up_late.at[:, cols])]
+            there = (up_late, up, down_next)
+        targets += [(block(r + 1), ref.at[:, cols]) for r, ref in enumerate(there)]
         for src, dst in targets:
             copy = pltpu.make_async_copy(src, dst, r_sem.at[len(stores)])
             copy.start()
@@ -164,20 +168,22 @@
         copy.wait()
 
 
-def project(meta, mine, other, pieces, spots, part):
+def project(meta, mine, other, pieces, spots, part, paired):
     n_z, rows, depth = mine.shape
     n_x = len(spots)
     tile = 4 * part
     width = n_x * tile
     shape = lambda *dims: jax.ShapeDtypeStruct(dims, jnp.bfloat16)
+    half = shape(rows, width // 2)
+    sent = [shape(2, rows, width // 2)] * 2 if paired else [half] * 4
     hbm = pl.BlockSpec(memory_space=pl.ANY)
     return pl.pallas_call(
-        functools.partial(project_kernel, spots=spots, n_piece=len(pieces)),
+        functools.partial(project_kernel, spots=spots, n_piece=len(pieces), paired=paired),
         grid_spec=pltpu.PrefetchScalarGridSpec(
             num_scalar_prefetch=1,
             grid=(1,),
             in_specs=[hbm] * (2 + len(pieces)),
-            out_specs=[hbm] * 5,
+            out_specs=[hbm] * (3 + len(sent)),
             scratch_shapes=[
                 pltpu.VMEM((n_z, rows, 2 * depth), jnp.bfloat16),
                 pltpu.VMEM((width, 2 * depth), jnp.bfloat16),
@@ -187,8 +193,8 @@
                 pltpu.SemaphoreType.DMA((n_x * n_z,)),
             ],
         ),
-        out_shape=[shape(rows, width)] + [shape(2, rows, width // 2)] * 2 + [shape(rows, width // 2)] * 2,
-        compiler_params=params(),
+        out_shape=[shape(rows, width), *sent, half, half],
+        compiler_params=params(16 * MIB if paired else VMEM),
         cost_estimate=pl.CostEstimate(
             flops=4 * n_z * rows * depth * width,
             bytes_accessed=4 * depth * width + 4 * n_z * rows * width,
@@ -203,67 +209,68 @@
     ob_ref[...] = (wide(b_ref) + wide(y_ref)).astype(ob_ref.dtype)
 
 
-def add_relayed(a, from_low, b, from_high, steps=2):
+def add_relayed(a, from_low, b, from_high):
     rows, width = a.shape
-    tile = width // steps
-    flat = pl.BlockSpec((rows, tile), lambda i: (0, i))
-    lead = pl.BlockSpec((None, rows, tile), lambda i: (0, 0, i))
+    flat = pl.BlockSpec((rows, width), lambda i: (0, 0))
+    lead = pl.BlockSpec((None, rows, width), lambda i: (0, 0, 0))
+    got = lead if from_low.ndim == 3 else flat
     return pl.pallas_call(
         add_kernel,
-        grid=(steps,),
-        in_specs=[flat, lead, flat, lead],
+        grid=(1,),
+        in_specs=[flat, got, flat, got],
         out_specs=[flat, flat],
         out_shape=[jax.ShapeDtypeStruct(a.shape, a.dtype)] * 2,
-        compiler_params=params(8 * MIB),
+        compiler_params=params(4 * MIB),
         cost_estimate=pl.CostEstimate(flops=2 * a.size, bytes_accessed=12 * a.size, transcendentals=0),
     )(a, from_low, b, from_high)
 
 
 def finish_kernel(meta, gate_ref, own, low_b, low_a, high_a, high_b, *refs):
-    o_ref = refs[-1]
-    early = pl.program_id(0) < pl.num_programs(0) // 2
-    wide = lambda ref: ref[...].astype(jnp.float32)
-    total = wide(own) + jnp.where(early, wide(low_a), wide(low_b)) + jnp.where(early, wide(high_a), wide(high_b))
-    total = total.astype(jnp.bfloat16).astype(jnp.float32)
-    o_ref[0] = (gate_ref[...] * total).astype(o_ref.dtype)
+    o_ref, buf, sem = refs[-3:]
+    n_x, _, tile = buf.shape
+    half = n_x // 2
+    wide = lambda value: value.astype(jnp.float32)
+    whole = lambda ref: ref[1] if len(ref.shape) == 3 else ref[...]
+    low, high = (whole(low_a), whole(low_b)), (whole(high_a), whole(high_b))
+    copies = []
+    for x in range(n_x):
+        late, at = divmod(x, half)
+        cols = slice(at * tile, (at + 1) * tile)
+        total = wide(own[:, x * tile : (x + 1) * tile]) + wide(low[late][:, cols]) + wide(high[late][:, cols])
+        total = total.astype(jnp.bfloat16).astype(jnp.float32)
+        place = pl.ds(pl.multiple_of((2 * lax.rem(meta[1] + x, n_x) + meta[0]) * tile, 128), tile)
+        buf[x] = (gate_ref[:, place] * total).astype(buf.dtype)
+        copies.append(pltpu.make_async_copy(buf.at[x], o_ref.at[0, :, place], sem.at[x]))
+        copies[-1].start()
+    for copy in copies:
+        copy.wait()
 
 
 def finish(meta, gate, piece, out=None):
-    own, low, low_a, high, high_b = piece
-    rows, width = own.shape
-    steps = 4
-    tile = width // steps
-    half = steps // 2
-    first = lambda i: jnp.minimum(i, half - 1)
-    second = lambda i: jnp.maximum(i - half, 0)
-    place = lambda i, m: 2 * lax.rem(m[1] + i, steps) + m[0]
-    specs = [
-        pl.BlockSpec((1, tile), lambda i, m: (0, place(i, m))),
-        pl.BlockSpec((rows, tile), lambda i, m: (0, i)),
-        pl.BlockSpec((None, rows, tile), lambda i, m: (1, 0, second(i))),
-        pl.BlockSpec((rows, tile), lambda i, m: (0, first(i))),
-        pl.BlockSpec((None, rows, tile), lambda i, m: (1, 0, first(i))),
-        pl.BlockSpec((rows, tile), lambda i, m: (0, second(i))),
-    ]
-    args = [meta, gate, own, low, low_a, high, high_b]
+    rows, width = piece[0].shape
+    n_x = 4
+    hbm = pl.BlockSpec(memory_space=pl.ANY)
+    whole = lambda array: pl.BlockSpec(array.shape, lambda i, m: (0,) * array.ndim)
+    args, specs = [gate, *piece], [whole(array) for array in (gate, *piece)]
     alias = {}
     if out is not None:
-        alias = {len(args): 0}
+        alias = {len(args) + 1: 0}
         args.append(out)
-        specs.append(pl.BlockSpec(memory_space=pl.ANY))
+        specs.append(hbm)
     return pl.pallas_call(
         finish_kernel,
         grid_spec=pltpu.PrefetchScalarGridSpec(
             num_scalar_prefetch=1,
-            grid=(steps,),
+            grid=(1,),
             in_specs=specs,
-            out_specs=pl.BlockSpec((1, rows, tile), lambda i, m: (0, 0, place(i, m))),
+            out_specs=hbm,
+            scratch_shapes=[pltpu.VMEM((n_x, rows, width // n_x), jnp.bfloat16), pltpu.SemaphoreType.DMA((n_x,))],
         ),
         out_shape=jax.ShapeDtypeStruct((1, rows, 2 * width), jnp.bfloat16),
         input_output_aliases=alias,
-        compiler_params=params(12 * MIB),
+        compiler_params=params(8 * MIB),
         cost_estimate=pl.CostEstimate(flops=4 * rows * width, bytes_accessed=8 * rows * width, transcendentals=0),
-    )(*args)
+    )(meta, *args)
 
 
 def local(queries, keys, values, out_weight, gate, kv_frames):
@@ -291,9 +298,10 @@
     lower, upper = weight[:, :part].T, weight[:, part:].T
     lower, upper, queries = after((lower, upper, queries))
     far_l, far_u = shift(lower, ("yh", "yl"), ring, 1), shift(upper, ("yh", "yl"), ring, ring - 1)
+    parts = layout(queries[0], keys[0], values[0], n_y, n_z).reshape(n, 3, rows, cols)
+    parts, lower, upper = after((parts, lower, upper))
     near_l, near_u = right(lower), left(upper)
-    parts = layout(queries[0], keys[0], values[0], n_y, n_z).reshape(n, 3, rows, cols)
-    parts, far_l, far_u, near_l, near_u = after((parts, far_l, far_u, near_l, near_u))
+    parts, far_l, far_u = after((parts, far_l, far_u))
     parts = lax.all_to_all(parts, ("yh", "z"), 0, 0, tiled=True)
     held = jnp.concatenate([lower, upper, near_l, near_u, far_l, far_u], 0)
     low, high = right(upper, near_l, far_l), left(lower, near_u, far_u)
@@ -305,25 +313,31 @@
     far_spots = [rows_of(*pair) for pair in (((0, 4), (0, 5)), ((4, 0), (2, 2)), ((3, 1), (4, 1)), ((1, 2), (3, 0)))]
 
     table = kv_frames.reshape(-1)
-    meta = jnp.concatenate([jnp.stack([my_y, my_z]), table])
+    meta = lambda y: jnp.concatenate([jnp.stack([y, my_z]), table])
     parts, near = after((parts, near))
-    theirs, mine = attend(meta, parts, slots, n_y)
+    theirs = attend(meta(1 - my_y), parts, slots, n_y)
     other = shift(theirs, "yh", n_y, 1)
+    mine = attend(meta(my_y), parts, slots, n_y)
 
     def relay(sent):
-        stay, to_up, to_down, late_up, late_down = sent
-        return stay, up(to_up), down(to_down), late_up, late_down
+        if len(sent) == 5:
+            stay, to_up, to_down, late_up, late_down = sent
+            low, high = up(to_up), down(to_down)
+            return stay, low, low, high, high, late_up, late_down
+        stay, to_up, next_up, to_down, next_down, late_up, late_down = sent
+        return stay, up(to_up), up(next_up), down(to_down), down(next_down), late_up, late_down
 
     def last(relayed):
-        stay, low, high, late_up, late_down = relayed
+        stay, low, low_b, high, high_a, late_up, late_down = relayed
         late_up, late_down = add_relayed(late_up, low, late_down, high)
-        return stay, low, up(late_up), high, down(late_down)
+        return stay, low_b, up(late_up), high_a, down(late_down)
 
     here = jnp.stack([my_y, my_c])
-    other, far = after((other, far))
+    sent = project(here, mine, other, near, near_spots, part, True)
+    far, sent = after((far, sent))
     far = near[:3] + far + near[3:] + [swap(piece) for piece in far]
-    sent = relay(project(here, mine, other, near, near_spots, part))
-    sent_far = relay(project(here, mine, other, far, far_spots, part))
+    sent = relay(sent)
+    sent_far = relay(project(here, mine, other, far, far_spots, part, False))
     out = finish(jnp.stack([my_l, my_x]), gate, last(sent))
     return finish(jnp.stack([1 - my_l, my_x]), gate, last(sent_far), out)
 

time: 158 us -> 154 us (0.975)
  waiting for transfers between devices: 61.7 us -> 55.1 us
  local copies, waits for them, and re-layouts: 12.9 us -> 19.4 us
  Pallas kernels: 44 us -> 38.9 us
    ppermute x22 -> x24, waiting for transfers between devices: 54.7 us -> 46.5 us  [shift(): lax.ppermute(array, axes, [(i, (i + by) % size) for i in range(size)])]
    unnamed x30 -> x42, local copies, waits for them, and re-layouts: 8.75 us -> 15 us
    pallas_call x1, Pallas kernels: 4.57 us -> 1.01 us  [layout(): pl.pallas_call(layout_kernel, grid=(n_z,), in_specs=[block] * 3, out_spec...]
    pallas_call x2, Pallas kernels: 8.31 us -> 5.31 us  [finish(): pl.pallas_call(finish_kernel, grid_spec=pltpu.PrefetchScalarGridSpec(num_...]
    pallas_call x1 -> x2, Pallas kernels: 8.56 us -> 10.7 us  [attend(): pl.pallas_call(functools.partial(attend_kernel, slots=slots), grid_spec=p...]
    all_to_all x1, waiting for transfers between devices: 7 us -> 8.65 us  [local(): parts = lax.all_to_all(parts, ('yh', 'z'), 0, 0, tiled=True)]
    ppermute x22 -> x24, starting transfers between devices: 27 us -> 25.9 us  [shift(): lax.ppermute(array, axes, [(i, (i + by) % size) for i in range(size)])]
  transfers between devices with their start and end apart: 23 -> 25, of which waited for: 9 -> 8; matrix products, arithmetic and copies ran while one was open for 7% -> 7% of each run, Pallas kernels for 25% -> 24%
where the time goes in v5:
time: 154 us; the launch traced here: 153 us
  waiting for transfers between devices  55.1 us (36%)
  Pallas kernels  38.9 us (25%)
  starting transfers between devices  34.2 us (22%)
  local copies, waits for them, and re-layouts  19.4 us (13%)
  other arithmetic  4.55 us (3%)
    ppermute x24, waiting for transfers between devices, shift(): lax.ppermute(array, axes, [(i, (i + by) % size) for i in range(size)])  46.5 us
    ppermute x24, starting transfers between devices, shift(): lax.ppermute(array, axes, [(i, (i + by) % size) for i in range(size)])  25.9 us
    pallas_call x2, Pallas kernels, project(): pl.pallas_call(functools.partial(project_kernel, spots=spots, n_piece=len...  20.1 us
    unnamed x42, local copies, waits for them, and re-layouts  15 us
    pallas_call x2, Pallas kernels, attend(): pl.pallas_call(functools.partial(attend_kernel, slots=slots), grid_spec=p...  10.7 us
    all_to_all x1, waiting for transfers between devices, local(): parts = lax.all_to_all(parts, ('yh', 'z'), 0, 0, tiled=True)  8.65 us
    all_to_all x1, starting transfers between devices, local(): parts = lax.all_to_all(parts, ('yh', 'z'), 0, 0, tiled=True)  8.29 us
    pallas_call x2, Pallas kernels, finish(): pl.pallas_call(finish_kernel, grid_spec=pltpu.PrefetchScalarGridSpec(num_...  5.31 us
  transfers between devices with their start and end apart: 25, of which 8 were waited for; matrix products, arithmetic and copies ran while one was open for 7% of the time, Pallas kernels for 24%

profile of v5, /device:TPU:24, one launch (start us, length us, event | category | flops | bytes accessed | tf_op | source)
XLA Modules:
  0.0 152.7 jit_solution(9359047953219902187)
XLA Ops:
  0.0 2.2 %dynamic-slice_bitcast_fusion = (bf16[160,1280]{1,0:T(8,128)(2,1)}, bf16[160,1280]{1,0:T(8,128)(2,1)}) fusion(bf16[5120,320]{0,1:T(8,128)(2,1)} %param.9, s32[]{:T(128)S(6)} %select_n.3, s32[]{:T(128)S(6)} %add.11), kind=kLoop, calls=%fused_computation.4 | loop fusion | bytes 1638408 | tf_op jit(solution)/shard_map/transpose | solution.py:298
  2.2 0.1 collective-permute-start
  2.3 1.9 %collective-permute-start.1 = (bf16[160,1280]{1,0:T(8,128)(2,1)}, bf16[160,1280]{1,0:T(8,128)(2,1)S(1)}, u32[]{:S(2)}, u32[]{:S(2)}) collective-permute-start(bf16[160,1280]{1,0:T(8,128)(2,1)} %get-tuple-element.50), channel_id=1, source_target_pairs={{0,66},{2,0},{64,2},{66,64},{1,67},{3,1},{65,3},{67,65},{4,70},{6,... | collective-permute-start | bytes 1228808 | tf_op jit(solution)/shard_map/ppermute | solution.py:287
  4.2 1.3 copy-done.4
  5.6 1.3 copy-done.5
  6.9 1.0 shard_map.64
  7.9 1.9 %copy-done = bf16[2,4,3,128,640]{4,3,2,1,0:T(8,128)(2,1)} copy-done((bf16[2,4,3,128,640]{4,3,2,1,0:T(8,128)(2,1)}, bf16[2,4,3,128,640]{4,3,2,1,0:T(8,128)(2,1)S(1)}, u32[]{:S(2)}) %copy-start) | copy-done | bytes 3932184
  9.8 1.5 collective-permute-start.2
  11.3 1.7 %collective-permute-start.3 = (bf16[160,1280]{1,0:T(8,128)(2,1)}, bf16[160,1280]{1,0:T(8,128)(2,1)}, u32[]{:S(2)}, u32[]{:S(2)}) collective-permute-start(bf16[160,1280]{1,0:T(8,128)(2,1)} %get-tuple-element.50), channel_id=1, source_target_pairs={{0,12},{4,0},{8,4},{12,8},{1,13},{5,1},{9,5},{13,9},{2,14},{6,2},{... | collective-permute-start | bytes 1228808 | tf_op jit(solution)/shard_map/ppermute | solution.py:287
  13.0 1.0 constant_dynamic-update-slice_fusion.5
  14.1 1.0 constant_dynamic-update-slice_fusion.4
  15.1 0.0 collective-permute-done
  15.1 8.3 %all-to-all-start = ((bf16[8,3,128,640]{3,2,1,0:T(8,128)(2,1)}), bf16[8,3,128,640]{3,2,1,0:T(8,128)(2,1)}, u32[]{:S(2)}, u32[]{:S(2)}) async-start(bf16[8,3,128,640]{3,2,1,0:T(8,128)(2,1)} %bitcast.15), calls=%async_computation | async-start | bytes 7864320 | tf_op jit(solution)/shard_map/all_to_all | solution.py:305
  23.4 1.2 pad_maximum_fusion
  24.6 0.0 copy-start.17
  24.6 1.3 collective-permute-start.4
  25.9 1.2 pad_maximum_fusion.1
  27.1 2.1 %collective-permute-start.5 = (bf16[480,1280]{1,0:T(8,128)(2,1)S(1)}, bf16[480,1280]{1,0:T(8,128)(2,1)}, u32[]{:S(2)}, u32[]{:S(2)}) collective-permute-start(bf16[480,1280]{1,0:T(8,128)(2,1)S(1)} %pad_maximum_fusion.1), channel_id=1, source_target_pairs={{0,12},{4,0},{8,4},{12,8},{1,13},{5,1},{9,5},{13,9},{2,14},{6,2},{... | collective-permute-start | bytes 3686408 | tf_op jit(solution)/shard_map/ppermute | solution.py:287
  29.2 1.0 constant_dynamic-update-slice_fusion.3
  30.3 1.0 constant_dynamic-update-slice_fusion.2
  31.4 0.1 collective-permute-start.6
  31.5 21.6 %collective-permute-done.4.refs_1_ = bf16[480,1280]{1,0:T(8,128)(2,1)} collective-permute-done((bf16[480,1280]{1,0:T(8,128)(2,1)S(1)}, bf16[480,1280]{1,0:T(8,128)(2,1)}, u32[]{:S(2)}, u32[]{:S(2)}) %collective-permute-start.4) | collective-permute-done | bytes 1228832 | tf_op jit(solution)/shard_map/ppermute | solution.py:287
  53.1 1.0 collective-permute-done.5.refs_2_
  54.1 0.1 copy.9
  54.2 0.1 reshape.6
  54.3 0.1 add_add_fusion.1
  54.3 1.0 slice.16
  55.4 0.9 pad_maximum_fusion.2
  56.3 1.5 collective-permute-start.10
  57.8 1.0 slice.17
  58.9 8.6 %all-to-all-done.q_ref.k_ref.v_ref = bf16[8,3,128,640]{3,2,1,0:T(8,128)(2,1)} async-done(((bf16[8,3,128,640]{3,2,1,0:T(8,128)(2,1)}), bf16[8,3,128,640]{3,2,1,0:T(8,128)(2,1)}, u32[]{:S(2)}, u32[]{:S(2)}) %all-to-all-start) | async-done | bytes 3932192 | tf_op jit(solution)/shard_map/all_to_all | solution.py:305
  67.5 5.8 %shard_map.66 = bf16[4,128,640]{2,1,0:T(8,128)(2,1)} custom-call(s32[98]{0:T(128)S(1)} %get-tuple-element.85.meta, bf16[8,3,128,640]{3,2,1,0:T(8,128)(2,1)} %all-to-all-done.q_ref.k_ref.v_ref, bf16[8,3,128,640]{3,2,1,0:T(8,128)(2,1)} %all-to-all-done.q_ref.k_ref.v_ref, bf16[8,3,128,640]{3,2,1,0:T(8,128)(2,1)} %all-to-all-done.q_ref.k_ref.v_ref), custom_call_target="tpu_custom_call" | custom-call | flops 503316480 | bytes 3932160 | tf_op jit(solution)/shard_map/pallas_call | solution.py:87
  73.3 0.9 collective-permute-start.9
  74.2 1.0 pad_maximum_fusion.3
  75.2 2.5 %collective-permute-start.11 = (bf16[320,1280]{1,0:T(8,128)(2,1)}, bf16[320,1280]{1,0:T(8,128)(2,1)}, u32[]{:S(2)}, u32[]{:S(2)}) collective-permute-start(bf16[320,1280]{1,0:T(8,128)(2,1)} %pad_maximum_fusion.3), channel_id=1, source_target_pairs={{0,12},{4,0},{8,4},{12,8},{1,13},{5,1},{9,5},{13,9},{2,14},{6,2},{... | collective-permute-start | bytes 2457608 | tf_op jit(solution)/shard_map/ppermute | solution.py:287
  77.7 0.1 pad_add_fusion.1.meta
  77.7 4.9 %shard_map.65.mine_ref = bf16[4,128,640]{2,1,0:T(8,128)(2,1)S(1)} custom-call(s32[98]{0:T(128)S(1)} %get-tuple-element.86.meta, bf16[8,3,128,640]{3,2,1,0:T(8,128)(2,1)} %all-to-all-done.q_ref.k_ref.v_ref, bf16[8,3,128,640]{3,2,1,0:T(8,128)(2,1)} %all-to-all-done.q_ref.k_ref.v_ref, bf16[8,3,128,640]{3,2,1,0:T(8,128)(2,1)} %all-to-all-done.q_ref.k_ref.v_ref), custom_call_target="tpu_custom_call" | custom-call | flops 503316480 | bytes 3932160 | tf_op jit(solution)/shard_map/pallas_call | solution.py:87
  82.7 8.7 %collective-permute-done.9.other_ref = bf16[4,128,640]{2,1,0:T(8,128)(2,1)} collective-permute-done((bf16[4,128,640]{2,1,0:T(8,128)(2,1)}, bf16[4,128,640]{2,1,0:T(8,128)(2,1)}, u32[]{:S(2)}, u32[]{:S(2)}) %collective-permute-start.9) | collective-permute-done | bytes 655392 | tf_op jit(solution)/shard_map/ppermute | solution.py:287
  91.4 9.8 %shard_map.67 = (bf16[128,2560]{1,0:T(8,128)(2,1)S(1)}, bf16[2,128,1280]{2,1,0:T(8,128)(2,1)}, bf16[2,128,1280]{2,1,0:T(8,128)(2,1)}, bf16[128,1280]{1,0:T(8,128)(2,1)S(1)}, bf16[128,1280]{1,0:T(8,128)(2,1)S(1)}) custom-call(s32[2]{0:T(128)S(1)} %pad_add_fusion.1.meta, bf16[4,128,640]{2,1,0:T(8,128)(2,1)S(1)} %shard_map.65.mine_ref, ...), custom_call_target="tpu_custom_call" | custom-call | flops 3355443200 | bytes 11796480 | tf_op jit(solution)/shard_map/pallas_call | solution.py:180
  101.2 0.8 copy-done.6
  102.1 0.5 collective-permute-start.13
  102.6 1.2 collective-permute-start.20
  103.8 2.0 %collective-permute-start.21 = (bf16[2,128,1280]{2,1,0:T(8,128)(2,1)}, bf16[2,128,1280]{2,1,0:T(8,128)(2,1)S(1)}, u32[]{:S(2)}, u32[]{:S(2)}) collective-permute-start(bf16[2,128,1280]{2,1,0:T(8,128)(2,1)} %get-tuple-element.80), channel_id=1, source_target_pairs={{0,48},{16,0},{32,16},{48,32},{1,49},{17,1},{33,17},{49,33},{2,50}... | collective-permute-start | bytes 1966088 | tf_op jit(solution)/shard_map/ppermute | solution.py:287
  105.8 0.9 copy-done.15
  106.7 0.9 copy-done.16
  107.6 10.3 %shard_map.68 = (bf16[128,2560]{1,0:T(8,128)(2,1)}, bf16[128,1280]{1,0:T(8,128)(2,1)}, bf16[128,1280]{1,0:T(8,128)(2,1)}, bf16[128,1280]{1,0:T(8,128)(2,1)}, bf1...) custom-call(s32[2]{0:T(128)} %copy-done.14, bf16[4,128,640]{2,1,0:T(8,128)(2,1)} %copy-done.2, ...), custom_call_target="tpu_custom_call" | custom-call | flops 3355443200 | bytes 11796480 | tf_op jit(solution)/shard_map/pallas_call | solution.py:180
  118.0 0.0 copy-start.13
  118.0 0.4 collective-permute-start.15
  118.3 2.9 %collective-permute-start.16 = (bf16[128,1280]{1,0:T(8,128)(2,1)}, bf16[128,1280]{1,0:T(8,128)(2,1)S(1)}, u32[]{:S(2)}, u32[]{:S(2)}) collective-permute-start(bf16[128,1280]{1,0:T(8,128)(2,1)} %get-tuple-element.72), channel_id=1, source_target_pairs={{0,48},{16,0},{32,16},{48,32},{1,49},{17,1},{33,17},{49,33},{2,50}... | collective-permute-start | bytes 983048 | tf_op jit(solution)/shard_map/ppermute | solution.py:287
  121.3 0.8 shard_map.70
  122.1 3.2 %collective-permute-start.23 = (bf16[128,1280]{1,0:T(8,128)(2,1)}, bf16[128,1280]{1,0:T(8,128)(2,1)}, u32[]{:S(2)}, u32[]{:S(2)}) collective-permute-start(bf16[128,1280]{1,0:T(8,128)(2,1)} %get-tuple-element.82), channel_id=1, source_target_pairs={{0,48},{16,0},{32,16},{48,32},{1,49},{17,1},{33,17},{49,33},{2,50}... | collective-permute-start | bytes 983048 | tf_op jit(solution)/shard_map/ppermute | solution.py:287
  125.3 4.8 %collective-permute-done.15.x_ref = bf16[128,1280]{1,0:T(8,128)(2,1)S(1)} collective-permute-done((bf16[128,1280]{1,0:T(8,128)(2,1)}, bf16[128,1280]{1,0:T(8,128)(2,1)S(1)}, u32[]{:S(2)}, u32[]{:S(2)}) %collective-permute-start.15) | collective-permute-done | bytes 327712 | tf_op jit(solution)/shard_map/ppermute | solution.py:287
  130.1 1.0 copy-done.11
  131.1 1.0 copy-done.12
  132.1 0.9 shard_map.69
  133.0 2.0 %collective-permute-start.17 = (bf16[128,1280]{1,0:T(8,128)(2,1)}, bf16[128,1280]{1,0:T(8,128)(2,1)}, u32[]{:S(2)}, u32[]{:S(2)}) collective-permute-start(bf16[128,1280]{1,0:T(8,128)(2,1)} %get-tuple-element.73), channel_id=1, source_target_pairs={{0,16},{16,32},{32,48},{48,0},{1,17},{17,33},{33,49},{49,1},{2,18}... | collective-permute-start | bytes 983048 | tf_op jit(solution)/shard_map/ppermute | solution.py:287
  135.0 2.1 %collective-permute-done.22.low_a = bf16[128,1280]{1,0:T(8,128)(2,1)S(1)} collective-permute-done((bf16[128,1280]{1,0:T(8,128)(2,1)S(1)}, bf16[128,1280]{1,0:T(8,128)(2,1)S(1)}, u32[]{:S(2)}, u32[]{:S(2)}) %collective-permute-start.22) | collective-permute-done | bytes 327712 | tf_op jit(solution)/shard_map/ppermute | solution.py:287
  137.1 0.7 copy-done.9
  137.9 0.1 pad_add_fusion
  138.0 1.0 copy-done.10
  138.9 2.6 %shard_map.71.refs_0_ = bf16[1,128,5120]{2,1,0:T(8,128)(2,1)} custom-call(s32[2]{0:T(128)S(1)} %get-tuple-element.88.meta, f32[1,5120]{1,0:T(1,128)S(1)} %copy-done.13, bf16[128,2560]{1,0:T(8,128)(2,1)S(1)} %copy-done.7, bf16[2,128,1280]{2,1,0:T(8,128)(2,1)S(1)} %collective-permute-done.20.x_ref.low_b, bf16[128,1280]{1,0:T(8,128)(2,1)S(1)} %copy-done.10, ...), custom_call_target="tpu_custom_call" | custom-call | flops 1310720 | bytes 2621440 | tf_op jit(solution)/shard_map/pallas_call | solution.py:260
  141.5 2.6 %collective-permute-done.14.low_b = bf16[128,1280]{1,0:T(8,128)(2,1)S(1)} collective-permute-done((bf16[128,1280]{1,0:T(8,128)(2,1)}, bf16[128,1280]{1,0:T(8,128)(2,1)S(1)}, u32[]{:S(2)}, u32[]{:S(2)}) %collective-permute-start.14) | collective-permute-done | bytes 327712 | tf_op jit(solution)/shard_map/ppermute | solution.py:287
  144.2 5.6 %collective-permute-done.17.low_a = bf16[128,1280]{1,0:T(8,128)(2,1)} collective-permute-done((bf16[128,1280]{1,0:T(8,128)(2,1)}, bf16[128,1280]{1,0:T(8,128)(2,1)}, u32[]{:S(2)}, u32[]{:S(2)}) %collective-permute-start.17) | collective-permute-done | bytes 327712 | tf_op jit(solution)/shard_map/ppermute | solution.py:287
  149.8 2.7 %shard_map.72 = bf16[1,128,5120]{2,1,0:T(8,128)(2,1)} custom-call(s32[2]{0:T(128)S(1)} %get-tuple-element.87.meta, f32[1,5120]{1,0:T(1,128)S(1)} %copy-done.13, bf16[128,2560]{1,0:T(8,128)(2,1)S(1)} %copy-done.8, bf16[128,1280]{1,0:T(8,128)(2,1)S(1)} %collective-permute-done.14.low_b, ...), custom_call_target="tpu_custom_call", output_to_operand_aliasing={{}: (7, {})} | custom-call | flops 1310720 | bytes 2621440 | tf_op jit(solution)/shard_map/pallas_call | solution.py:260
  (49 shorter events, 0.2 us)
Async XLA Ops:
  0.0 4.2 %copy-start.3 = (bf16[1,128,5120]{2,1,0:T(8,128)(2,1)S(1)}, bf16[1,128,5120]{2,1,0:T(8,128)(2,1)}, u32[]{:S(2)}) copy-start(bf16[1,128,5120]{2,1,0:T(8,128)(2,1)} %param.6) | copy-start | bytes 3932164
  2.2 12.9 %collective-permute-start = (bf16[160,1280]{1,0:T(8,128)(2,1)}, bf16[160,1280]{1,0:T(8,128)(2,1)S(1)}, u32[]{:S(2)}, u32[]{:S(2)}) collective-permute-start(bf16[160,1280]{1,0:T(8,128)(2,1)} %get-tuple-element.49), channel_id=1, source_target_pairs={{0,2},{2,64},{64,66},{66,0},{1,3},{3,65},{65,67},{67,1},{4,6},{6,6... | collective-permute-start | bytes 1228808 | tf_op jit(solution)/shard_map/ppermute | solution.py:287
  2.3 12.8 %collective-permute-start.1 = (bf16[160,1280]{1,0:T(8,128)(2,1)}, bf16[160,1280]{1,0:T(8,128)(2,1)S(1)}, u32[]{:S(2)}, u32[]{:S(2)}) collective-permute-start(bf16[160,1280]{1,0:T(8,128)(2,1)} %get-tuple-element.50), channel_id=1, source_target_pairs={{0,66},{2,0},{64,2},{66,64},{1,67},{3,1},{65,3},{67,65},{4,70},{6,... | collective-permute-start | bytes 1228808 | tf_op jit(solution)/shard_map/ppermute | solution.py:287
  4.2 1.3 copy-start.4
  5.6 1.3 copy-start.5
  7.9 1.9 %copy-start = (bf16[2,4,3,128,640]{4,3,2,1,0:T(8,128)(2,1)}, bf16[2,4,3,128,640]{4,3,2,1,0:T(8,128)(2,1)S(1)}, u32[]{:S(2)}) copy-start(bf16[2,4,3,128,640]{4,3,2,1,0:T(8,128)(2,1)S(1)} %shard_map.64) | copy-start | bytes 11796484
  9.8 13.6 %collective-permute-start.2 = (bf16[160,1280]{1,0:T(8,128)(2,1)}, bf16[160,1280]{1,0:T(8,128)(2,1)}, u32[]{:S(2)}, u32[]{:S(2)}) collective-permute-start(bf16[160,1280]{1,0:T(8,128)(2,1)} %get-tuple-element.49), channel_id=1, source_target_pairs={{0,4},{4,8},{8,12},{12,0},{1,5},{5,9},{9,13},{13,1},{2,6},{6,10},{... | collective-permute-start | bytes 1228808 | tf_op jit(solution)/shard_map/ppermute | solution.py:287
  11.3 14.6 %collective-permute-start.3 = (bf16[160,1280]{1,0:T(8,128)(2,1)}, bf16[160,1280]{1,0:T(8,128)(2,1)}, u32[]{:S(2)}, u32[]{:S(2)}) collective-permute-start(bf16[160,1280]{1,0:T(8,128)(2,1)} %get-tuple-element.50), channel_id=1, source_target_pairs={{0,12},{4,0},{8,4},{12,8},{1,13},{5,1},{9,5},{13,9},{2,14},{6,2},{... | collective-permute-start | bytes 1228808 | tf_op jit(solution)/shard_map/ppermute | solution.py:287
  15.1 52.4 %all-to-all-start = ((bf16[8,3,128,640]{3,2,1,0:T(8,128)(2,1)}), bf16[8,3,128,640]{3,2,1,0:T(8,128)(2,1)}, u32[]{:S(2)}, u32[]{:S(2)}) async-start(bf16[8,3,128,640]{3,2,1,0:T(8,128)(2,1)} %bitcast.15), calls=%async_computation | async-start | bytes 7864320 | tf_op jit(solution)/shard_map/all_to_all | solution.py:305
  24.6 29.5 %copy-start.17 = (s32[16,6]{0,1:T(8,128)S(1)}, s32[16,6]{0,1:T(8,128)}, u32[]{:S(2)}) copy-start(s32[16,6]{0,1:T(8,128)} %param.11) | copy-start | bytes 1156
  24.6 28.5 %collective-permute-start.4 = (bf16[480,1280]{1,0:T(8,128)(2,1)S(1)}, bf16[480,1280]{1,0:T(8,128)(2,1)}, u32[]{:S(2)}, u32[]{:S(2)}) collective-permute-start(bf16[480,1280]{1,0:T(8,128)(2,1)S(1)} %pad_maximum_fusion), channel_id=1, source_target_pairs={{0,4},{4,8},{8,12},{12,0},{1,5},{5,9},{9,13},{13,1},{2,6},{6,10},{... | collective-permute-start | bytes 3686408 | tf_op jit(solution)/shard_map/ppermute | solution.py:287
  27.1 27.0 %collective-permute-start.5 = (bf16[480,1280]{1,0:T(8,128)(2,1)S(1)}, bf16[480,1280]{1,0:T(8,128)(2,1)}, u32[]{:S(2)}, u32[]{:S(2)}) collective-permute-start(bf16[480,1280]{1,0:T(8,128)(2,1)S(1)} %pad_maximum_fusion.1), channel_id=1, source_target_pairs={{0,12},{4,0},{8,4},{12,8},{1,13},{5,1},{9,5},{13,9},{2,14},{6,2},{... | collective-permute-start | bytes 3686408 | tf_op jit(solution)/shard_map/ppermute | solution.py:287
  31.4 60.0 %copy-start.1 = (bf16[960,1280]{1,0:T(8,128)(2,1)}, bf16[960,1280]{1,0:T(8,128)(2,1)S(1)}, u32[]{:S(2)}) copy-start(bf16[960,1280]{1,0:T(8,128)(2,1)S(1)} %constant_dynamic-update-slice_fusion.refs_0_) | copy-start | bytes 7372804
  31.4 27.5 %collective-permute-start.6 = (bf16[960,1280]{1,0:T(8,128)(2,1)S(1)}, bf16[960,1280]{1,0:T(8,128)(2,1)}, u32[]{:S(2)}, u32[]{:S(2)}) collective-permute-start(bf16[960,1280]{1,0:T(8,128)(2,1)S(1)} %constant_dynamic-update-slice_fusion.refs_0_), channel_id=1, source_target_pairs={{0,1},{1,0},{2,3},{3,2},{4,5},{5,4},{6,7},{7,6},{8,9},{9,8},{10,11... | collective-permute-start | bytes 7372808 | tf_op jit(solution)/shard_map/ppermute | solution.py:287
  53.1 5.8 %collective-permute-start.7 = (bf16[480,1280]{1,0:T(8,128)(2,1)}, bf16[480,1280]{1,0:T(8,128)(2,1)}, u32[]{:S(2)}, u32[]{:S(2)}) collective-permute-start(bf16[480,1280]{1,0:T(8,128)(2,1)} %collective-permute-done.4.refs_1_), channel_id=1, source_target_pairs={{0,1},{1,0},{2,3},{3,2},{4,5},{5,4},{6,7},{7,6},{8,9},{9,8},{10,11... | collective-permute-start | bytes 3686408 | tf_op jit(solution)/shard_map/ppermute | solution.py:287
  54.1 4.8 %collective-permute-start.8 = (bf16[480,1280]{1,0:T(8,128)(2,1)}, bf16[480,1280]{1,0:T(8,128)(2,1)}, u32[]{:S(2)}, u32[]{:S(2)}) collective-permute-start(bf16[480,1280]{1,0:T(8,128)(2,1)} %collective-permute-done.5.refs_2_), channel_id=1, source_target_pairs={{0,1},{1,0},{2,3},{3,2},{4,5},{5,4},{6,7},{7,6},{8,9},{9,8},{10,11... | collective-permute-start | bytes 3686408 | tf_op jit(solution)/shard_map/ppermute | solution.py:287
  56.3 45.7 %collective-permute-start.10 = (bf16[320,1280]{1,0:T(8,128)(2,1)}, bf16[320,1280]{1,0:T(8,128)(2,1)}, u32[]{:S(2)}, u32[]{:S(2)}) collective-permute-start(bf16[320,1280]{1,0:T(8,128)(2,1)} %pad_maximum_fusion.2), channel_id=1, source_target_pairs={{0,4},{4,8},{8,12},{12,0},{1,5},{5,9},{9,13},{13,1},{2,6},{6,10},{... | collective-permute-start | bytes 2457608 | tf_op jit(solution)/shard_map/ppermute | solution.py:287
  73.3 18.1 %collective-permute-start.9 = (bf16[4,128,640]{2,1,0:T(8,128)(2,1)}, bf16[4,128,640]{2,1,0:T(8,128)(2,1)}, u32[]{:S(2)}, u32[]{:S(2)}) collective-permute-start(bf16[4,128,640]{2,1,0:T(8,128)(2,1)} %shard_map.66), channel_id=1, source_target_pairs={{0,64},{64,0},{1,65},{65,1},{2,66},{66,2},{3,67},{67,3},{4,68},{68... | collective-permute-start | bytes 1966088 | tf_op jit(solution)/shard_map/ppermute | solution.py:287
  75.2 26.9 %collective-permute-start.11 = (bf16[320,1280]{1,0:T(8,128)(2,1)}, bf16[320,1280]{1,0:T(8,128)(2,1)}, u32[]{:S(2)}, u32[]{:S(2)}) collective-permute-start(bf16[320,1280]{1,0:T(8,128)(2,1)} %pad_maximum_fusion.3), channel_id=1, source_target_pairs={{0,12},{4,0},{8,4},{12,8},{1,13},{5,1},{9,5},{13,9},{2,14},{6,2},{... | collective-permute-start | bytes 2457608 | tf_op jit(solution)/shard_map/ppermute | solution.py:287
  77.7 13.7 %copy-start.14 = (s32[2]{0:T(128)}, s32[2]{0:T(128)S(1)}, u32[]{:S(2)}) copy-start(s32[2]{0:T(128)S(1)} %pad_add_fusion.1.meta) | copy-start | bytes 28
  82.7 18.5 %copy-start.2 = (bf16[4,128,640]{2,1,0:T(8,128)(2,1)}, bf16[4,128,640]{2,1,0:T(8,128)(2,1)S(1)}, u32[]{:S(2)}) copy-start(bf16[4,128,640]{2,1,0:T(8,128)(2,1)S(1)} %shard_map.65.mine_ref) | copy-start | bytes 1966084
  101.2 0.8 copy-start.6
  102.1 3.8 %collective-permute-start.12 = (bf16[320,1280]{1,0:T(8,128)(2,1)}, bf16[320,1280]{1,0:T(8,128)(2,1)S(1)}, u32[]{:S(2)}, u32[]{:S(2)}) collective-permute-start(bf16[320,1280]{1,0:T(8,128)(2,1)} %collective-permute-done.10.refs_3_), channel_id=1, source_target_pairs={{0,1},{1,0},{2,3},{3,2},{4,5},{5,4},{6,7},{7,6},{8,9},{9,8},{10,11... | collective-permute-start | bytes 2457608 | tf_op jit(solution)/shard_map/ppermute | solution.py:287
  102.1 3.7 %collective-permute-start.13 = (bf16[320,1280]{1,0:T(8,128)(2,1)}, bf16[320,1280]{1,0:T(8,128)(2,1)S(1)}, u32[]{:S(2)}, u32[]{:S(2)}) collective-permute-start(bf16[320,1280]{1,0:T(8,128)(2,1)} %collective-permute-done.11.refs_4_), channel_id=1, source_target_pairs={{0,1},{1,0},{2,3},{3,2},{4,5},{5,4},{6,7},{7,6},{8,9},{9,8},{10,11... | collective-permute-start | bytes 2457608 | tf_op jit(solution)/shard_map/ppermute | solution.py:287
  102.6 18.7 %collective-permute-start.20 = (bf16[2,128,1280]{2,1,0:T(8,128)(2,1)}, bf16[2,128,1280]{2,1,0:T(8,128)(2,1)S(1)}, u32[]{:S(2)}, u32[]{:S(2)}) collective-permute-start(bf16[2,128,1280]{2,1,0:T(8,128)(2,1)} %get-tuple-element.77), channel_id=1, source_target_pairs={{0,16},{16,32},{32,48},{48,0},{1,17},{17,33},{33,49},{49,1},{2,18}... | collective-permute-start | bytes 1966088 | tf_op jit(solution)/shard_map/ppermute | solution.py:287
  103.8 17.5 %collective-permute-start.21 = (bf16[2,128,1280]{2,1,0:T(8,128)(2,1)}, bf16[2,128,1280]{2,1,0:T(8,128)(2,1)S(1)}, u32[]{:S(2)}, u32[]{:S(2)}) collective-permute-start(bf16[2,128,1280]{2,1,0:T(8,128)(2,1)} %get-tuple-element.80), channel_id=1, source_target_pairs={{0,48},{16,0},{32,16},{48,32},{1,49},{17,1},{33,17},{49,33},{2,50}... | collective-permute-start | bytes 1966088 | tf_op jit(solution)/shard_map/ppermute | solution.py:287
  105.8 0.9 copy-start.15
  106.7 0.9 copy-start.16
  118.0 20.0 %copy-start.7 = (bf16[128,2560]{1,0:T(8,128)(2,1)S(1)}, bf16[128,2560]{1,0:T(8,128)(2,1)}, u32[]{:S(2)}) copy-start(bf16[128,2560]{1,0:T(8,128)(2,1)} %copy-done.6) | copy-start | bytes 1966084
  118.0 20.0 %copy-start.13 = (f32[1,5120]{1,0:T(1,128)S(1)}, f32[1,5120]{1,0:T(1,128)}, u32[]{:S(2)}) copy-start(f32[1,5120]{1,0:T(1,128)} %gate_ref.3) | copy-start | bytes 61444
  118.0 12.1 %collective-permute-start.15 = (bf16[128,1280]{1,0:T(8,128)(2,1)}, bf16[128,1280]{1,0:T(8,128)(2,1)S(1)}, u32[]{:S(2)}, u32[]{:S(2)}) collective-permute-start(bf16[128,1280]{1,0:T(8,128)(2,1)} %get-tuple-element.70), channel_id=1, source_target_pairs={{0,16},{16,32},{32,48},{48,0},{1,17},{17,33},{33,49},{49,1},{2,18}... | collective-permute-start | bytes 983048 | tf_op jit(solution)/shard_map/ppermute | solution.py:287
  118.3 11.8 %collective-permute-start.16 = (bf16[128,1280]{1,0:T(8,128)(2,1)}, bf16[128,1280]{1,0:T(8,128)(2,1)S(1)}, u32[]{:S(2)}, u32[]{:S(2)}) collective-permute-start(bf16[128,1280]{1,0:T(8,128)(2,1)} %get-tuple-element.72), channel_id=1, source_target_pairs={{0,48},{16,0},{32,16},{48,32},{1,49},{17,1},{33,17},{49,33},{2,50}... | collective-permute-start | bytes 983048 | tf_op jit(solution)/shard_map/ppermute | solution.py:287
  122.1 15.0 %collective-permute-start.22 = (bf16[128,1280]{1,0:T(8,128)(2,1)S(1)}, bf16[128,1280]{1,0:T(8,128)(2,1)S(1)}, u32[]{:S(2)}, u32[]{:S(2)}) collective-permute-start(bf16[128,1280]{1,0:T(8,128)(2,1)S(1)} %get-tuple-element.81), channel_id=1, source_target_pairs={{0,16},{16,32},{32,48},{48,0},{1,17},{17,33},{33,49},{49,1},{2,18}... | collective-permute-start | bytes 983048 | tf_op jit(solution)/shard_map/ppermute | solution.py:287
  122.1 15.8 %collective-permute-start.23 = (bf16[128,1280]{1,0:T(8,128)(2,1)}, bf16[128,1280]{1,0:T(8,128)(2,1)}, u32[]{:S(2)}, u32[]{:S(2)}) collective-permute-start(bf16[128,1280]{1,0:T(8,128)(2,1)} %get-tuple-element.82), channel_id=1, source_target_pairs={{0,48},{16,0},{32,16},{48,32},{1,49},{17,1},{33,17},{49,33},{2,50}... | collective-permute-start | bytes 983048 | tf_op jit(solution)/shard_map/ppermute | solution.py:287
  125.3 18.8 %collective-permute-start.14 = (bf16[128,1280]{1,0:T(8,128)(2,1)}, bf16[128,1280]{1,0:T(8,128)(2,1)S(1)}, u32[]{:S(2)}, u32[]{:S(2)}) collective-permute-start(bf16[128,1280]{1,0:T(8,128)(2,1)} %get-tuple-element.68), channel_id=1, source_target_pairs={{0,16},{16,32},{32,48},{48,0},{1,17},{17,33},{33,49},{49,1},{2,18}... | collective-permute-start | bytes 983048 | tf_op jit(solution)/shard_map/ppermute | solution.py:287
  130.1 14.0 %collective-permute-start.18 = (bf16[128,1280]{1,0:T(8,128)(2,1)}, bf16[128,1280]{1,0:T(8,128)(2,1)S(1)}, u32[]{:S(2)}, u32[]{:S(2)}) collective-permute-start(bf16[128,1280]{1,0:T(8,128)(2,1)} %get-tuple-element.74), channel_id=1, source_target_pairs={{0,48},{16,0},{32,16},{48,32},{1,49},{17,1},{33,17},{49,33},{2,50}... | collective-permute-start | bytes 983048 | tf_op jit(solution)/shard_map/ppermute | solution.py:287
  130.1 1.0 copy-start.11
  131.1 1.0 copy-start.12
  132.1 17.7 %copy-start.8 = (bf16[128,2560]{1,0:T(8,128)(2,1)S(1)}, bf16[128,2560]{1,0:T(8,128)(2,1)}, u32[]{:S(2)}) copy-start(bf16[128,2560]{1,0:T(8,128)(2,1)} %get-tuple-element.67.own) | copy-start | bytes 1966084
  133.0 16.8 %collective-permute-start.17 = (bf16[128,1280]{1,0:T(8,128)(2,1)}, bf16[128,1280]{1,0:T(8,128)(2,1)}, u32[]{:S(2)}, u32[]{:S(2)}) collective-permute-start(bf16[128,1280]{1,0:T(8,128)(2,1)} %get-tuple-element.73), channel_id=1, source_target_pairs={{0,16},{16,32},{32,48},{48,0},{1,17},{17,33},{33,49},{49,1},{2,18}... | collective-permute-start | bytes 983048 | tf_op jit(solution)/shard_map/ppermute | solution.py:287
  137.1 0.7 copy-start.9
  137.9 11.9 %collective-permute-start.19 = (bf16[128,1280]{1,0:T(8,128)(2,1)}, bf16[128,1280]{1,0:T(8,128)(2,1)}, u32[]{:S(2)}, u32[]{:S(2)}) collective-permute-start(bf16[128,1280]{1,0:T(8,128)(2,1)} %get-tuple-element.75), channel_id=1, source_target_pairs={{0,48},{16,0},{32,16},{48,32},{1,49},{17,1},{33,17},{49,33},{2,50}... | collective-permute-start | bytes 983048 | tf_op jit(solution)/shard_map/ppermute | solution.py:287
  137.9 1.0 copy-start.10

commit v6 on v5

--- a/solution.py
+++ b/solution.py
@@ -194,7 +194,7 @@
             ],
         ),
         out_shape=[shape(rows, width), *sent, half, half],
-        compiler_params=params(16 * MIB if paired else VMEM),
+        compiler_params=params(16 * MIB),
         cost_estimate=pl.CostEstimate(
             flops=4 * n_z * rows * depth * width,
             bytes_accessed=4 * depth * width + 4 * n_z * rows * width,
@@ -299,10 +299,10 @@
     lower, upper, queries = after((lower, upper, queries))
     far_l, far_u = shift(lower, ("yh", "yl"), ring, 1), shift(upper, ("yh", "yl"), ring, ring - 1)
     parts = layout(queries[0], keys[0], values[0], n_y, n_z).reshape(n, 3, rows, cols)
-    parts, lower, upper = after((parts, lower, upper))
     near_l, near_u = right(lower), left(upper)
     parts, far_l, far_u = after((parts, far_l, far_u))
     parts = lax.all_to_all(parts, ("yh", "z"), 0, 0, tiled=True)
+    near_l, near_u, lower, upper = after((near_l, near_u, lower, upper))
     held = jnp.concatenate([lower, upper, near_l, near_u, far_l, far_u], 0)
     low, high = right(upper, near_l, far_l), left(lower, near_u, far_u)
     near = [held, low, high]
@@ -333,8 +333,8 @@
         return stay, low_b, up(late_up), high_a, down(late_down)
 
     here = jnp.stack([my_y, my_c])
+    mine, far = after((mine, far))
     sent = project(here, mine, other, near, near_spots, part, True)
-    far, sent = after((far, sent))
     far = near[:3] + far + near[3:] + [swap(piece) for piece in far]
     sent = relay(sent)
     sent_far = relay(project(here, mine, other, far, far_spots, part, False))

time: 154 us -> 150 us (0.974)
  waiting for transfers between devices: 55.1 us -> 64 us
  local copies, waits for them, and re-layouts: 19.4 us -> 13.2 us
  Pallas kernels: 38.9 us -> 35.7 us
  starting transfers between devices: 34.2 us -> 32.2 us
    ppermute x24, waiting for transfers between devices: 46.5 us -> 57.5 us  [shift(): lax.ppermute(array, axes, [(i, (i + by) % size) for i in range(size)])]
    unnamed x42 -> x44, local copies, waits for them, and re-layouts: 15 us -> 9.71 us
    all_to_all x1, waiting for transfers between devices: 8.65 us -> 6.51 us  [local(): parts = lax.all_to_all(parts, ('yh', 'z'), 0, 0, tiled=True)]
    ppermute x24, starting transfers between devices: 25.9 us -> 23.9 us  [shift(): lax.ppermute(array, axes, [(i, (i + by) % size) for i in range(size)])]
    pallas_call x2, Pallas kernels: 5.31 us -> 3.27 us  [finish(): pl.pallas_call(finish_kernel, grid_spec=pltpu.PrefetchScalarGridSpec(num_...]
  transfers between devices with their start and end apart: 25 -> 25, of which waited for: 8 -> 17; matrix products, arithmetic and copies ran while one was open for 7% -> 5% of each run, Pallas kernels for 24% -> 23%
where the time goes in v6:
time: 150 us; the launch traced here: 149 us
  waiting for transfers between devices  64 us (43%)
  Pallas kernels  35.7 us (24%)
  starting transfers between devices  32.2 us (21%)
  local copies, waits for them, and re-layouts  13.2 us (9%)
  other arithmetic  3.51 us (2%)
    ppermute x24, waiting for transfers between devices, shift(): lax.ppermute(array, axes, [(i, (i + by) % size) for i in range(size)])  57.5 us
    ppermute x24, starting transfers between devices, shift(): lax.ppermute(array, axes, [(i, (i + by) % size) for i in range(size)])  23.9 us
    pallas_call x2, Pallas kernels, project(): pl.pallas_call(functools.partial(project_kernel, spots=spots, n_piece=len...  18.8 us
    pallas_call x2, Pallas kernels, attend(): pl.pallas_call(functools.partial(attend_kernel, slots=slots), grid_spec=p...  10.7 us
    unnamed x44, local copies, waits for them, and re-layouts  9.71 us
    all_to_all x1, starting transfers between devices, local(): parts = lax.all_to_all(parts, ('yh', 'z'), 0, 0, tiled=True)  8.28 us
    all_to_all x1, waiting for transfers between devices, local(): parts = lax.all_to_all(parts, ('yh', 'z'), 0, 0, tiled=True)  6.51 us
    pallas_call x2, Pallas kernels, finish(): pl.pallas_call(finish_kernel, grid_spec=pltpu.PrefetchScalarGridSpec(num_...  3.27 us
  transfers between devices with their start and end apart: 25, of which 17 were waited for; matrix products, arithmetic and copies ran while one was open for 5% of the time, Pallas kernels for 23%

profile of v6, /device:TPU:24, one launch (start us, length us, event | category | flops | bytes accessed | tf_op | source)
XLA Modules:
  0.0 148.9 jit_solution(12049314374457719313)
XLA Ops:
  0.0 1.3 dynamic-slice_bitcast_fusion
  1.3 1.6 %collective-permute-start.2 = (bf16[160,1280]{1,0:T(8,128)(2,1)S(1)}, bf16[160,1280]{1,0:T(8,128)(2,1)S(1)}, u32[]{:S(2)}, u32[]{:S(2)}) collective-permute-start(bf16[160,1280]{1,0:T(8,128)(2,1)S(1)} %get-tuple-element.45), channel_id=1, source_target_pairs={{0,4},{4,8},{8,12},{12,0},{1,5},{5,9},{9,13},{13,1},{2,6},{6,10},{... | collective-permute-start | bytes 1228808 | tf_op jit(solution)/shard_map/ppermute | solution.py:287
  2.9 1.7 %collective-permute-start.3 = (bf16[160,1280]{1,0:T(8,128)(2,1)S(1)}, bf16[160,1280]{1,0:T(8,128)(2,1)}, u32[]{:S(2)}, u32[]{:S(2)}) collective-permute-start(bf16[160,1280]{1,0:T(8,128)(2,1)S(1)} %get-tuple-element.46), channel_id=1, source_target_pairs={{0,12},{4,0},{8,4},{12,8},{1,13},{5,1},{9,5},{13,9},{2,14},{6,2},{... | collective-permute-start | bytes 1228808 | tf_op jit(solution)/shard_map/ppermute | solution.py:287
  4.6 0.1 collective-permute-start
  4.8 1.9 %collective-permute-start.1 = (bf16[160,1280]{1,0:T(8,128)(2,1)S(1)}, bf16[160,1280]{1,0:T(8,128)(2,1)S(1)}, u32[]{:S(2)}, u32[]{:S(2)}) collective-permute-start(bf16[160,1280]{1,0:T(8,128)(2,1)S(1)} %get-tuple-element.46), channel_id=1, source_target_pairs={{0,66},{2,0},{64,2},{66,64},{1,67},{3,1},{65,3},{67,65},{4,70},{6,... | collective-permute-start | bytes 1228808 | tf_op jit(solution)/shard_map/ppermute | solution.py:287
  6.7 1.3 copy-done.6
  8.0 1.3 copy-done.7
  9.3 1.0 shard_map.64
  10.3 1.9 %copy-done = bf16[2,4,3,128,640]{4,3,2,1,0:T(8,128)(2,1)} copy-done((bf16[2,4,3,128,640]{4,3,2,1,0:T(8,128)(2,1)}, bf16[2,4,3,128,640]{4,3,2,1,0:T(8,128)(2,1)S(1)}, u32[]{:S(2)}) %copy-start) | copy-done | bytes 3932184
  12.2 1.6 %collective-permute-done.2 = bf16[160,1280]{1,0:T(8,128)(2,1)S(1)} collective-permute-done((bf16[160,1280]{1,0:T(8,128)(2,1)S(1)}, bf16[160,1280]{1,0:T(8,128)(2,1)S(1)}, u32[]{:S(2)}, u32[]{:S(2)}) %collective-permute-start.2) | collective-permute-done | bytes 409632 | tf_op jit(solution)/shard_map/ppermute | solution.py:287
  13.8 0.1 collective-permute-done.3
  13.9 1.3 collective-permute-done
  15.3 1.2 collective-permute-done.1
  16.5 8.3 %all-to-all-start = ((bf16[8,3,128,640]{3,2,1,0:T(8,128)(2,1)}), bf16[8,3,128,640]{3,2,1,0:T(8,128)(2,1)}, u32[]{:S(2)}, u32[]{:S(2)}) async-start(bf16[8,3,128,640]{3,2,1,0:T(8,128)(2,1)} %bitcast.15), calls=%async_computation | async-start | bytes 7864320 | tf_op jit(solution)/shard_map/all_to_all | solution.py:304
  24.8 1.3 pad_maximum_fusion.1
  26.0 1.6 %collective-permute-start.5 = (bf16[480,1280]{1,0:T(8,128)(2,1)S(1)}, bf16[480,1280]{1,0:T(8,128)(2,1)}, u32[]{:S(2)}, u32[]{:S(2)}) collective-permute-start(bf16[480,1280]{1,0:T(8,128)(2,1)S(1)} %pad_maximum_fusion.1), channel_id=1, source_target_pairs={{0,12},{4,0},{8,4},{12,8},{1,13},{5,1},{9,5},{13,9},{2,14},{6,2},{... | collective-permute-start | bytes 3686408 | tf_op jit(solution)/shard_map/ppermute | solution.py:287
  27.7 0.1 pad_maximum_fusion
  27.8 0.5 collective-permute-start.4
  28.4 1.0 constant_dynamic-update-slice_fusion.2
  29.5 0.1 collective-permute-start.6
  29.6 23.1 %collective-permute-done.5.refs_2_ = bf16[480,1280]{1,0:T(8,128)(2,1)} collective-permute-done((bf16[480,1280]{1,0:T(8,128)(2,1)S(1)}, bf16[480,1280]{1,0:T(8,128)(2,1)}, u32[]{:S(2)}, u32[]{:S(2)}) %collective-permute-start.5) | collective-permute-done | bytes 1228832 | tf_op jit(solution)/shard_map/ppermute | solution.py:287
  52.7 2.8 %collective-permute-done.4.refs_1_ = bf16[480,1280]{1,0:T(8,128)(2,1)} collective-permute-done((bf16[480,1280]{1,0:T(8,128)(2,1)S(1)}, bf16[480,1280]{1,0:T(8,128)(2,1)}, u32[]{:S(2)}, u32[]{:S(2)}) %collective-permute-start.4) | collective-permute-done | bytes 1228832 | tf_op jit(solution)/shard_map/ppermute | solution.py:287
  55.5 1.0 slice.17
  56.5 1.0 pad_maximum_fusion.3
  57.5 0.6 collective-permute-start.10
  58.1 1.0 slice.16
  59.1 0.9 pad_maximum_fusion.2
  60.1 1.4 collective-permute-start.9
  61.5 0.1 copy.9
  61.6 0.1 reshape.6
  61.7 0.1 add_add_fusion.1
  61.8 6.5 %all-to-all-done.q_ref.k_ref.v_ref = bf16[8,3,128,640]{3,2,1,0:T(8,128)(2,1)} async-done(((bf16[8,3,128,640]{3,2,1,0:T(8,128)(2,1)}), bf16[8,3,128,640]{3,2,1,0:T(8,128)(2,1)}, u32[]{:S(2)}, u32[]{:S(2)}) %all-to-all-start) | async-done | bytes 3932192 | tf_op jit(solution)/shard_map/all_to_all | solution.py:304
  68.3 5.8 %shard_map.66 = bf16[4,128,640]{2,1,0:T(8,128)(2,1)} custom-call(s32[98]{0:T(128)S(1)} %get-tuple-element.79.meta, bf16[8,3,128,640]{3,2,1,0:T(8,128)(2,1)} %all-to-all-done.q_ref.k_ref.v_ref, bf16[8,3,128,640]{3,2,1,0:T(8,128)(2,1)} %all-to-all-done.q_ref.k_ref.v_ref, bf16[8,3,128,640]{3,2,1,0:T(8,128)(2,1)} %all-to-all-done.q_ref.k_ref.v_ref), custom_call_target="tpu_custom_call" | custom-call | flops 503316480 | bytes 3932160 | tf_op jit(solution)/shard_map/pallas_call | solution.py:87
  74.1 0.9 collective-permute-start.11
  75.1 4.9 %shard_map.65.mine_ref = bf16[4,128,640]{2,1,0:T(8,128)(2,1)S(1)} custom-call(s32[98]{0:T(128)S(1)} %get-tuple-element.80.meta, bf16[8,3,128,640]{3,2,1,0:T(8,128)(2,1)} %all-to-all-done.q_ref.k_ref.v_ref, bf16[8,3,128,640]{3,2,1,0:T(8,128)(2,1)} %all-to-all-done.q_ref.k_ref.v_ref, bf16[8,3,128,640]{3,2,1,0:T(8,128)(2,1)} %all-to-all-done.q_ref.k_ref.v_ref), custom_call_target="tpu_custom_call" | custom-call | flops 503316480 | bytes 3932160 | tf_op jit(solution)/shard_map/pallas_call | solution.py:87
  80.0 1.7 %collective-permute-done.9.refs_3_ = bf16[320,1280]{1,0:T(8,128)(2,1)} collective-permute-done((bf16[320,1280]{1,0:T(8,128)(2,1)}, bf16[320,1280]{1,0:T(8,128)(2,1)}, u32[]{:S(2)}, u32[]{:S(2)}) %collective-permute-start.9) | collective-permute-done | bytes 819232 | tf_op jit(solution)/shard_map/ppermute | solution.py:287
  81.7 0.5 collective-permute-start.13
  82.3 9.9 %collective-permute-done.11.other_ref = bf16[4,128,640]{2,1,0:T(8,128)(2,1)} collective-permute-done((bf16[4,128,640]{2,1,0:T(8,128)(2,1)}, bf16[4,128,640]{2,1,0:T(8,128)(2,1)}, u32[]{:S(2)}, u32[]{:S(2)}) %collective-permute-start.11) | collective-permute-done | bytes 655392 | tf_op jit(solution)/shard_map/ppermute | solution.py:287
  92.2 9.2 %shard_map.69 = (bf16[128,2560]{1,0:T(8,128)(2,1)S(1)}, bf16[2,128,1280]{2,1,0:T(8,128)(2,1)S(1)}, bf16[2,128,1280]{2,1,0:T(8,128)(2,1)S(1)}, bf16[128,1280]{1,0:T(8,128)(2,1)S(1)}, bf16[128,1280]{1,0:T(8,128)(2,1)S(1)}) custom-call(s32[2]{0:T(128)S(1)} %pad_add_fusion.1.meta, bf16[4,128,640]{2,1,0:T(8,128)(2,1)S(1)} %shard_map.65.mine_ref, ...), custom_call_target="tpu_custom_call" | custom-call | flops 3355443200 | bytes 11796480 | tf_op jit(solution)/shard_map/pallas_call | solution.py:180
  101.4 0.8 copy-done.8
  102.3 1.2 collective-permute-start.20
  103.5 2.0 %collective-permute-start.21 = (bf16[2,128,1280]{2,1,0:T(8,128)(2,1)S(1)}, bf16[2,128,1280]{2,1,0:T(8,128)(2,1)S(1)}, u32[]{:S(2)}, u32[]{:S(2)}) collective-permute-start(bf16[2,128,1280]{2,1,0:T(8,128)(2,1)S(1)} %get-tuple-element.74), channel_id=1, source_target_pairs={{0,48},{16,0},{32,16},{48,32},{1,49},{17,1},{33,17},{49,33},{2,50}... | collective-permute-start | bytes 1966088 | tf_op jit(solution)/shard_map/ppermute | solution.py:287
  105.5 9.6 %shard_map.67 = (bf16[128,2560]{1,0:T(8,128)(2,1)S(1)}, bf16[128,1280]{1,0:T(8,128)(2,1)S(1)}, bf16[128,1280]{1,0:T(8,128)(2,1)}, bf16[128,1280]{1,0:T(8,128)(2,...) custom-call(s32[2]{0:T(128)S(1)} %pad_add_fusion.1.meta, ...), custom_call_target="tpu_custom_call" | custom-call | flops 3355443200 | bytes 11796480 | tf_op jit(solution)/shard_map/pallas_call | solution.py:180
  115.3 3.2 %collective-permute-start.16 = (bf16[128,1280]{1,0:T(8,128)(2,1)S(1)}, bf16[128,1280]{1,0:T(8,128)(2,1)S(1)}, u32[]{:S(2)}, u32[]{:S(2)}) collective-permute-start(bf16[128,1280]{1,0:T(8,128)(2,1)S(1)} %get-tuple-element.66), channel_id=1, source_target_pairs={{0,48},{16,0},{32,16},{48,32},{1,49},{17,1},{33,17},{49,33},{2,50}... | collective-permute-start | bytes 983048 | tf_op jit(solution)/shard_map/ppermute | solution.py:287
  118.5 2.0 %collective-permute-done.20.x_ref.low_b = bf16[2,128,1280]{2,1,0:T(8,128)(2,1)S(1)} collective-permute-done((bf16[2,128,1280]{2,1,0:T(8,128)(2,1)S(1)}, bf16[2,128,1280]{2,1,0:T(8,128)(2,1)S(1)}, u32[]{:S(2)}, u32[]{:S(2)}) %collective-permute-start.20) | collective-permute-done | bytes 655392 | tf_op jit(solution)/shard_map/ppermute | solution.py:287
  120.4 0.7 collective-permute-done.21.y_ref.high_a
  121.2 0.9 shard_map.70
  122.1 0.8 copy-done.1
  123.0 2.0 %collective-permute-start.14 = (bf16[128,1280]{1,0:T(8,128)(2,1)}, bf16[128,1280]{1,0:T(8,128)(2,1)S(1)}, u32[]{:S(2)}, u32[]{:S(2)}) collective-permute-start(bf16[128,1280]{1,0:T(8,128)(2,1)} %get-tuple-element.62), channel_id=1, source_target_pairs={{0,16},{16,32},{32,48},{48,0},{1,17},{17,33},{33,49},{49,1},{2,18}... | collective-permute-start | bytes 983048 | tf_op jit(solution)/shard_map/ppermute | solution.py:287
  125.0 1.2 collective-permute-start.23
  126.2 1.2 collective-permute-done.15.x_ref
  127.5 1.3 collective-permute-start.18
  128.8 0.9 shard_map.68
  129.7 0.7 collective-permute-start.17
  130.4 4.4 %collective-permute-done.22.low_a = bf16[128,1280]{1,0:T(8,128)(2,1)S(1)} collective-permute-done((bf16[128,1280]{1,0:T(8,128)(2,1)S(1)}, bf16[128,1280]{1,0:T(8,128)(2,1)S(1)}, u32[]{:S(2)}, u32[]{:S(2)}) %collective-permute-start.22) | collective-permute-done | bytes 327712 | tf_op jit(solution)/shard_map/ppermute | solution.py:287
  134.8 1.0 collective-permute-start.19
  135.9 1.1 copy-done.2
  137.0 1.1 copy-done.4
  138.1 1.6 %shard_map.71.refs_0_ = bf16[1,128,5120]{2,1,0:T(8,128)(2,1)} custom-call(s32[2]{0:T(128)S(1)} %get-tuple-element.82.meta, f32[1,5120]{1,0:T(1,128)S(1)} %copy-done.12, bf16[128,2560]{1,0:T(8,128)(2,1)S(1)} %copy-done.9, bf16[2,128,1280]{2,1,0:T(8,128)(2,1)S(1)} %copy-done.2, bf16[128,1280]{1,0:T(8,128)(2,1)S(1)} %collective-permute-done.22.low_a, ...), custom_call_target="tpu_custom_call" | custom-call | flops 1310720 | bytes 2621440 | tf_op jit(solution)/shard_map/pallas_call | solution.py:260
  139.7 2.1 %collective-permute-done.14.low_b = bf16[128,1280]{1,0:T(8,128)(2,1)S(1)} collective-permute-done((bf16[128,1280]{1,0:T(8,128)(2,1)}, bf16[128,1280]{1,0:T(8,128)(2,1)S(1)}, u32[]{:S(2)}, u32[]{:S(2)}) %collective-permute-start.14) | collective-permute-done | bytes 327712 | tf_op jit(solution)/shard_map/ppermute | solution.py:287
  141.8 1.0 collective-permute-done.18.high_a
  142.9 4.1 %collective-permute-done.17.low_a = bf16[128,1280]{1,0:T(8,128)(2,1)S(1)} collective-permute-done((bf16[128,1280]{1,0:T(8,128)(2,1)}, bf16[128,1280]{1,0:T(8,128)(2,1)S(1)}, u32[]{:S(2)}, u32[]{:S(2)}) %collective-permute-start.17) | collective-permute-done | bytes 327712 | tf_op jit(solution)/shard_map/ppermute | solution.py:287
  147.0 0.1 collective-permute-done.19.high_b
  147.1 1.6 %shard_map.72 = bf16[1,128,5120]{2,1,0:T(8,128)(2,1)} custom-call(s32[2]{0:T(128)S(1)} %get-tuple-element.81.meta, f32[1,5120]{1,0:T(1,128)S(1)} %copy-done.12, bf16[128,2560]{1,0:T(8,128)(2,1)S(1)} %copy-done.11, bf16[128,1280]{1,0:T(8,128)(2,1)S(1)} %collective-permute-done.14.low_b, ...), custom_call_target="tpu_custom_call", output_to_operand_aliasing={{}: (7, {})} | custom-call | flops 1310720 | bytes 2621440 | tf_op jit(solution)/shard_map/pallas_call | solution.py:260
  (51 shorter events, 0.5 us)
Async XLA Ops:
  0.0 6.6 %copy-start.5 = (bf16[1,128,5120]{2,1,0:T(8,128)(2,1)S(1)}, bf16[1,128,5120]{2,1,0:T(8,128)(2,1)}, u32[]{:S(2)}) copy-start(bf16[1,128,5120]{2,1,0:T(8,128)(2,1)} %param.6) | copy-start | bytes 3932164
  1.3 9.0 %copy-start.13 = (bf16[160,1280]{1,0:T(8,128)(2,1)}, bf16[160,1280]{1,0:T(8,128)(2,1)S(1)}, u32[]{:S(2)}) copy-start(bf16[160,1280]{1,0:T(8,128)(2,1)S(1)} %get-tuple-element.46) | copy-start | bytes 1228804
  1.3 12.6 %copy-start.15 = (bf16[160,1280]{1,0:T(8,128)(2,1)}, bf16[160,1280]{1,0:T(8,128)(2,1)S(1)}, u32[]{:S(2)}) copy-start(bf16[160,1280]{1,0:T(8,128)(2,1)S(1)} %get-tuple-element.45) | copy-start | bytes 1228804
  1.3 12.5 %collective-permute-start.2 = (bf16[160,1280]{1,0:T(8,128)(2,1)S(1)}, bf16[160,1280]{1,0:T(8,128)(2,1)S(1)}, u32[]{:S(2)}, u32[]{:S(2)}) collective-permute-start(bf16[160,1280]{1,0:T(8,128)(2,1)S(1)} %get-tuple-element.45), channel_id=1, source_target_pairs={{0,4},{4,8},{8,12},{12,0},{1,5},{5,9},{9,13},{13,1},{2,6},{6,10},{... | collective-permute-start | bytes 1228808 | tf_op jit(solution)/shard_map/ppermute | solution.py:287
  2.9 11.0 %collective-permute-start.3 = (bf16[160,1280]{1,0:T(8,128)(2,1)S(1)}, bf16[160,1280]{1,0:T(8,128)(2,1)}, u32[]{:S(2)}, u32[]{:S(2)}) collective-permute-start(bf16[160,1280]{1,0:T(8,128)(2,1)S(1)} %get-tuple-element.46), channel_id=1, source_target_pairs={{0,12},{4,0},{8,4},{12,8},{1,13},{5,1},{9,5},{13,9},{2,14},{6,2},{... | collective-permute-start | bytes 1228808 | tf_op jit(solution)/shard_map/ppermute | solution.py:287
  4.6 10.6 %collective-permute-start = (bf16[160,1280]{1,0:T(8,128)(2,1)S(1)}, bf16[160,1280]{1,0:T(8,128)(2,1)S(1)}, u32[]{:S(2)}, u32[]{:S(2)}) collective-permute-start(bf16[160,1280]{1,0:T(8,128)(2,1)S(1)} %get-tuple-element.45), channel_id=1, source_target_pairs={{0,2},{2,64},{64,66},{66,0},{1,3},{3,65},{65,67},{67,1},{4,6},{6,6... | collective-permute-start | bytes 1228808 | tf_op jit(solution)/shard_map/ppermute | solution.py:287
  4.8 11.7 %collective-permute-start.1 = (bf16[160,1280]{1,0:T(8,128)(2,1)S(1)}, bf16[160,1280]{1,0:T(8,128)(2,1)S(1)}, u32[]{:S(2)}, u32[]{:S(2)}) collective-permute-start(bf16[160,1280]{1,0:T(8,128)(2,1)S(1)} %get-tuple-element.46), channel_id=1, source_target_pairs={{0,66},{2,0},{64,2},{66,64},{1,67},{3,1},{65,3},{67,65},{4,70},{6,... | collective-permute-start | bytes 1228808 | tf_op jit(solution)/shard_map/ppermute | solution.py:287
  6.6 1.3 copy-start.6
  8.0 1.3 copy-start.7
  10.3 1.9 %copy-start = (bf16[2,4,3,128,640]{4,3,2,1,0:T(8,128)(2,1)}, bf16[2,4,3,128,640]{4,3,2,1,0:T(8,128)(2,1)S(1)}, u32[]{:S(2)}) copy-start(bf16[2,4,3,128,640]{4,3,2,1,0:T(8,128)(2,1)S(1)} %shard_map.64) | copy-start | bytes 11796484
  13.8 2.7 %copy-start.16 = (bf16[160,1280]{1,0:T(8,128)(2,1)}, bf16[160,1280]{1,0:T(8,128)(2,1)S(1)}, u32[]{:S(2)}) copy-start(bf16[160,1280]{1,0:T(8,128)(2,1)S(1)} %collective-permute-done.2) | copy-start | bytes 1228804
  16.5 51.8 %all-to-all-start = ((bf16[8,3,128,640]{3,2,1,0:T(8,128)(2,1)}), bf16[8,3,128,640]{3,2,1,0:T(8,128)(2,1)}, u32[]{:S(2)}, u32[]{:S(2)}) async-start(bf16[8,3,128,640]{3,2,1,0:T(8,128)(2,1)} %bitcast.15), calls=%async_computation | async-start | bytes 7864320 | tf_op jit(solution)/shard_map/all_to_all | solution.py:304
  24.8 2.9 %copy-start.14 = (bf16[160,1280]{1,0:T(8,128)(2,1)S(1)}, bf16[160,1280]{1,0:T(8,128)(2,1)}, u32[]{:S(2)}) copy-start(bf16[160,1280]{1,0:T(8,128)(2,1)} %copy-done.13) | copy-start | bytes 1228804
  24.8 2.9 %copy-start.17 = (bf16[160,1280]{1,0:T(8,128)(2,1)S(1)}, bf16[160,1280]{1,0:T(8,128)(2,1)}, u32[]{:S(2)}) copy-start(bf16[160,1280]{1,0:T(8,128)(2,1)} %copy-done.16) | copy-start | bytes 1228804
  26.0 26.7 %collective-permute-start.5 = (bf16[480,1280]{1,0:T(8,128)(2,1)S(1)}, bf16[480,1280]{1,0:T(8,128)(2,1)}, u32[]{:S(2)}, u32[]{:S(2)}) collective-permute-start(bf16[480,1280]{1,0:T(8,128)(2,1)S(1)} %pad_maximum_fusion.1), channel_id=1, source_target_pairs={{0,12},{4,0},{8,4},{12,8},{1,13},{5,1},{9,5},{13,9},{2,14},{6,2},{... | collective-permute-start | bytes 3686408 | tf_op jit(solution)/shard_map/ppermute | solution.py:287
  27.8 27.7 %collective-permute-start.4 = (bf16[480,1280]{1,0:T(8,128)(2,1)S(1)}, bf16[480,1280]{1,0:T(8,128)(2,1)}, u32[]{:S(2)}, u32[]{:S(2)}) collective-permute-start(bf16[480,1280]{1,0:T(8,128)(2,1)S(1)} %pad_maximum_fusion), channel_id=1, source_target_pairs={{0,4},{4,8},{8,12},{12,0},{1,5},{5,9},{9,13},{13,1},{2,6},{6,10},{... | collective-permute-start | bytes 3686408 | tf_op jit(solution)/shard_map/ppermute | solution.py:287
  29.5 32.0 %copy-start.18 = (s32[16,6]{0,1:T(8,128)S(1)}, s32[16,6]{0,1:T(8,128)}, u32[]{:S(2)}) copy-start(s32[16,6]{0,1:T(8,128)} %param.11) | copy-start | bytes 1156
  29.5 32.3 %collective-permute-start.6 = (bf16[960,1280]{1,0:T(8,128)(2,1)S(1)}, bf16[960,1280]{1,0:T(8,128)(2,1)}, u32[]{:S(2)}, u32[]{:S(2)}) collective-permute-start(bf16[960,1280]{1,0:T(8,128)(2,1)S(1)} %constant_dynamic-update-slice_fusion.refs_0_), channel_id=1, source_target_pairs={{0,1},{1,0},{2,3},{3,2},{4,5},{5,4},{6,7},{7,6},{8,9},{9,8},{10,11... | collective-permute-start | bytes 7372808 | tf_op jit(solution)/shard_map/ppermute | solution.py:287
  52.7 9.1 %collective-permute-start.8 = (bf16[480,1280]{1,0:T(8,128)(2,1)}, bf16[480,1280]{1,0:T(8,128)(2,1)}, u32[]{:S(2)}, u32[]{:S(2)}) collective-permute-start(bf16[480,1280]{1,0:T(8,128)(2,1)} %collective-permute-done.5.refs_2_), channel_id=1, source_target_pairs={{0,1},{1,0},{2,3},{3,2},{4,5},{5,4},{6,7},{7,6},{8,9},{9,8},{10,11... | collective-permute-start | bytes 3686408 | tf_op jit(solution)/shard_map/ppermute | solution.py:287
  55.5 6.3 %collective-permute-start.7 = (bf16[480,1280]{1,0:T(8,128)(2,1)}, bf16[480,1280]{1,0:T(8,128)(2,1)}, u32[]{:S(2)}, u32[]{:S(2)}) collective-permute-start(bf16[480,1280]{1,0:T(8,128)(2,1)} %collective-permute-done.4.refs_1_), channel_id=1, source_target_pairs={{0,1},{1,0},{2,3},{3,2},{4,5},{5,4},{6,7},{7,6},{8,9},{9,8},{10,11... | collective-permute-start | bytes 3686408 | tf_op jit(solution)/shard_map/ppermute | solution.py:287
  57.5 22.5 %collective-permute-start.10 = (bf16[320,1280]{1,0:T(8,128)(2,1)}, bf16[320,1280]{1,0:T(8,128)(2,1)}, u32[]{:S(2)}, u32[]{:S(2)}) collective-permute-start(bf16[320,1280]{1,0:T(8,128)(2,1)} %pad_maximum_fusion.3), channel_id=1, source_target_pairs={{0,12},{4,0},{8,4},{12,8},{1,13},{5,1},{9,5},{13,9},{2,14},{6,2},{... | collective-permute-start | bytes 2457608 | tf_op jit(solution)/shard_map/ppermute | solution.py:287
  60.1 21.6 %collective-permute-start.9 = (bf16[320,1280]{1,0:T(8,128)(2,1)}, bf16[320,1280]{1,0:T(8,128)(2,1)}, u32[]{:S(2)}, u32[]{:S(2)}) collective-permute-start(bf16[320,1280]{1,0:T(8,128)(2,1)} %pad_maximum_fusion.2), channel_id=1, source_target_pairs={{0,4},{4,8},{8,12},{12,0},{1,5},{5,9},{9,13},{13,1},{2,6},{6,10},{... | collective-permute-start | bytes 2457608 | tf_op jit(solution)/shard_map/ppermute | solution.py:287
  74.1 18.1 %collective-permute-start.11 = (bf16[4,128,640]{2,1,0:T(8,128)(2,1)}, bf16[4,128,640]{2,1,0:T(8,128)(2,1)}, u32[]{:S(2)}, u32[]{:S(2)}) collective-permute-start(bf16[4,128,640]{2,1,0:T(8,128)(2,1)} %shard_map.66), channel_id=1, source_target_pairs={{0,64},{64,0},{1,65},{65,1},{2,66},{66,2},{3,67},{67,3},{4,68},{68... | collective-permute-start | bytes 1966088 | tf_op jit(solution)/shard_map/ppermute | solution.py:287
  81.7 23.8 %collective-permute-start.12 = (bf16[320,1280]{1,0:T(8,128)(2,1)}, bf16[320,1280]{1,0:T(8,128)(2,1)}, u32[]{:S(2)}, u32[]{:S(2)}) collective-permute-start(bf16[320,1280]{1,0:T(8,128)(2,1)} %collective-permute-done.9.refs_3_), channel_id=1, source_target_pairs={{0,1},{1,0},{2,3},{3,2},{4,5},{5,4},{6,7},{7,6},{8,9},{9,8},{10,11... | collective-permute-start | bytes 2457608 | tf_op jit(solution)/shard_map/ppermute | solution.py:287
  81.7 23.8 %collective-permute-start.13 = (bf16[320,1280]{1,0:T(8,128)(2,1)}, bf16[320,1280]{1,0:T(8,128)(2,1)}, u32[]{:S(2)}, u32[]{:S(2)}) collective-permute-start(bf16[320,1280]{1,0:T(8,128)(2,1)} %collective-permute-done.10.refs_4_), channel_id=1, source_target_pairs={{0,1},{1,0},{2,3},{3,2},{4,5},{5,4},{6,7},{7,6},{8,9},{9,8},{10,11... | collective-permute-start | bytes 2457608 | tf_op jit(solution)/shard_map/ppermute | solution.py:287
  101.4 0.8 copy-start.8
  102.3 18.2 %collective-permute-start.20 = (bf16[2,128,1280]{2,1,0:T(8,128)(2,1)S(1)}, bf16[2,128,1280]{2,1,0:T(8,128)(2,1)S(1)}, u32[]{:S(2)}, u32[]{:S(2)}) collective-permute-start(bf16[2,128,1280]{2,1,0:T(8,128)(2,1)S(1)} %get-tuple-element.71), channel_id=1, source_target_pairs={{0,16},{16,32},{32,48},{48,0},{1,17},{17,33},{33,49},{49,1},{2,18}... | collective-permute-start | bytes 1966088 | tf_op jit(solution)/shard_map/ppermute | solution.py:287
  103.5 17.7 %collective-permute-start.21 = (bf16[2,128,1280]{2,1,0:T(8,128)(2,1)S(1)}, bf16[2,128,1280]{2,1,0:T(8,128)(2,1)S(1)}, u32[]{:S(2)}, u32[]{:S(2)}) collective-permute-start(bf16[2,128,1280]{2,1,0:T(8,128)(2,1)S(1)} %get-tuple-element.74), channel_id=1, source_target_pairs={{0,48},{16,0},{32,16},{48,32},{1,49},{17,1},{33,17},{49,33},{2,50}... | collective-permute-start | bytes 1966088 | tf_op jit(solution)/shard_map/ppermute | solution.py:287
  115.1 7.8 %copy-start.10 = (bf16[128,2560]{1,0:T(8,128)(2,1)}, bf16[128,2560]{1,0:T(8,128)(2,1)S(1)}, u32[]{:S(2)}) copy-start(bf16[128,2560]{1,0:T(8,128)(2,1)S(1)} %get-tuple-element.61.own) | copy-start | bytes 1966084
  115.1 20.7 %copy-start.9 = (bf16[128,2560]{1,0:T(8,128)(2,1)S(1)}, bf16[128,2560]{1,0:T(8,128)(2,1)}, u32[]{:S(2)}) copy-start(bf16[128,2560]{1,0:T(8,128)(2,1)} %copy-done.8) | copy-start | bytes 1966084
  115.2 20.7 %copy-start.12 = (f32[1,5120]{1,0:T(1,128)S(1)}, f32[1,5120]{1,0:T(1,128)}, u32[]{:S(2)}) copy-start(f32[1,5120]{1,0:T(1,128)} %gate_ref.3) | copy-start | bytes 61444
  115.2 12.3 %collective-permute-start.15 = (bf16[128,1280]{1,0:T(8,128)(2,1)S(1)}, bf16[128,1280]{1,0:T(8,128)(2,1)S(1)}, u32[]{:S(2)}, u32[]{:S(2)}) collective-permute-start(bf16[128,1280]{1,0:T(8,128)(2,1)S(1)} %get-tuple-element.64), channel_id=1, source_target_pairs={{0,16},{16,32},{32,48},{48,0},{1,17},{17,33},{33,49},{49,1},{2,18}... | collective-permute-start | bytes 983048 | tf_op jit(solution)/shard_map/ppermute | solution.py:287
  115.3 13.5 %collective-permute-start.16 = (bf16[128,1280]{1,0:T(8,128)(2,1)S(1)}, bf16[128,1280]{1,0:T(8,128)(2,1)S(1)}, u32[]{:S(2)}, u32[]{:S(2)}) collective-permute-start(bf16[128,1280]{1,0:T(8,128)(2,1)S(1)} %get-tuple-element.66), channel_id=1, source_target_pairs={{0,48},{16,0},{32,16},{48,32},{1,49},{17,1},{33,17},{49,33},{2,50}... | collective-permute-start | bytes 983048 | tf_op jit(solution)/shard_map/ppermute | solution.py:287
  121.2 0.9 copy-start.3
  122.1 0.8 copy-start.1
  123.0 11.9 %collective-permute-start.22 = (bf16[128,1280]{1,0:T(8,128)(2,1)S(1)}, bf16[128,1280]{1,0:T(8,128)(2,1)S(1)}, u32[]{:S(2)}, u32[]{:S(2)}) collective-permute-start(bf16[128,1280]{1,0:T(8,128)(2,1)S(1)} %get-tuple-element.75), channel_id=1, source_target_pairs={{0,16},{16,32},{32,48},{48,0},{1,17},{17,33},{33,49},{49,1},{2,18}... | collective-permute-start | bytes 983048 | tf_op jit(solution)/shard_map/ppermute | solution.py:287
  123.0 18.9 %collective-permute-start.14 = (bf16[128,1280]{1,0:T(8,128)(2,1)}, bf16[128,1280]{1,0:T(8,128)(2,1)S(1)}, u32[]{:S(2)}, u32[]{:S(2)}) collective-permute-start(bf16[128,1280]{1,0:T(8,128)(2,1)} %get-tuple-element.62), channel_id=1, source_target_pairs={{0,16},{16,32},{32,48},{48,0},{1,17},{17,33},{33,49},{49,1},{2,18}... | collective-permute-start | bytes 983048 | tf_op jit(solution)/shard_map/ppermute | solution.py:287
  125.0 10.9 %collective-permute-start.23 = (bf16[128,1280]{1,0:T(8,128)(2,1)}, bf16[128,1280]{1,0:T(8,128)(2,1)S(1)}, u32[]{:S(2)}, u32[]{:S(2)}) collective-permute-start(bf16[128,1280]{1,0:T(8,128)(2,1)} %get-tuple-element.76), channel_id=1, source_target_pairs={{0,48},{16,0},{32,16},{48,32},{1,49},{17,1},{33,17},{49,33},{2,50}... | collective-permute-start | bytes 983048 | tf_op jit(solution)/shard_map/ppermute | solution.py:287
  127.5 15.4 %collective-permute-start.18 = (bf16[128,1280]{1,0:T(8,128)(2,1)}, bf16[128,1280]{1,0:T(8,128)(2,1)S(1)}, u32[]{:S(2)}, u32[]{:S(2)}) collective-permute-start(bf16[128,1280]{1,0:T(8,128)(2,1)} %get-tuple-element.68), channel_id=1, source_target_pairs={{0,48},{16,0},{32,16},{48,32},{1,49},{17,1},{33,17},{49,33},{2,50}... | collective-permute-start | bytes 983048 | tf_op jit(solution)/shard_map/ppermute | solution.py:287
  128.8 18.3 %copy-start.11 = (bf16[128,2560]{1,0:T(8,128)(2,1)S(1)}, bf16[128,2560]{1,0:T(8,128)(2,1)}, u32[]{:S(2)}) copy-start(bf16[128,2560]{1,0:T(8,128)(2,1)} %copy-done.10) | copy-start | bytes 1966084
  129.7 17.2 %collective-permute-start.17 = (bf16[128,1280]{1,0:T(8,128)(2,1)}, bf16[128,1280]{1,0:T(8,128)(2,1)S(1)}, u32[]{:S(2)}, u32[]{:S(2)}) collective-permute-start(bf16[128,1280]{1,0:T(8,128)(2,1)} %get-tuple-element.67), channel_id=1, source_target_pairs={{0,16},{16,32},{32,48},{48,0},{1,17},{17,33},{33,49},{49,1},{2,18}... | collective-permute-start | bytes 983048 | tf_op jit(solution)/shard_map/ppermute | solution.py:287
  134.8 12.3 %collective-permute-start.19 = (bf16[128,1280]{1,0:T(8,128)(2,1)}, bf16[128,1280]{1,0:T(8,128)(2,1)S(1)}, u32[]{:S(2)}, u32[]{:S(2)}) collective-permute-start(bf16[128,1280]{1,0:T(8,128)(2,1)} %get-tuple-element.69), channel_id=1, source_target_pairs={{0,48},{16,0},{32,16},{48,32},{1,49},{17,1},{33,17},{49,33},{2,50}... | collective-permute-start | bytes 983048 | tf_op jit(solution)/shard_map/ppermute | solution.py:287
  135.9 1.1 copy-start.2
  137.0 1.1 copy-start.4

commit v7 on v6

--- a/solution.py
+++ b/solution.py
@@ -136,30 +136,25 @@
         cols = pl.ds(pl.multiple_of(at * depth, 128), depth)
         acts.append(pltpu.make_async_copy(ref, act.at[:, :, cols], a_sem.at[i]))
         acts[-1].start()
-    load(0)
-    load(1)
+    for x in range(n_x):
+        load(x)
     for copy in acts:
         copy.wait()
 
     stores = []
-    for x in range(n_x):
-        for copy in loads[x]:
-            copy.wait()
-        if x + 2 < n_x:
-            load(x + 2)
+    for late in range(2):
+        xs = range(late * n_x // 2, (late + 1) * n_x // 2)
+        for x in xs:
+            for copy in loads[x]:
+                copy.wait()
         left = act[...].reshape(n_z * rows, 2 * depth)
-        weight = w_buf[x * tile : (x + 1) * tile]
+        weight = w_buf[xs[0] * tile : (xs[-1] + 1) * tile]
         total = lax.dot_general(left, weight, NT, preferred_element_type=jnp.float32)
-        r_buf[x] = total.astype(r_buf.dtype)
-        late, col = divmod(x, n_x // 2)
-        block = lambda r: r_buf.at[x, pl.ds(r * rows, rows)]
-        cols = pl.ds(col * tile, tile)
-        targets = [(block(0), stay.at[:, pl.ds(x * tile, tile)])]
-        if late:
-            there = (up_next, down, down_late)
-        else:
-            there = (up_late, up, down_next)
-        targets += [(block(r + 1), ref.at[:, cols]) for r, ref in enumerate(there)]
+        r_buf[late] = total.astype(r_buf.dtype)
+        block = lambda r: r_buf.at[late, pl.ds(r * rows, rows)]
+        there = (up_next, down, down_late) if late else (up_late, up, down_next)
+        targets = [(block(0), stay.at[:, pl.ds(xs[0] * tile, len(xs) * tile)])]
+        targets += [(block(r + 1), ref) for r, ref in enumerate(there)]
         for src, dst in targets:
             copy = pltpu.make_async_copy(src, dst, r_sem.at[len(stores)])
             copy.start()
@@ -187,14 +182,14 @@
             scratch_shapes=[
                 pltpu.VMEM((n_z, rows, 2 * depth), jnp.bfloat16),
                 pltpu.VMEM((width, 2 * depth), jnp.bfloat16),
-                pltpu.VMEM((n_x, n_z * rows, tile), jnp.bfloat16),
+                pltpu.VMEM((2, n_z * rows, width // 2), jnp.bfloat16),
                 pltpu.SemaphoreType.DMA((2,)),
                 pltpu.SemaphoreType.DMA((4 * n_x,)),
-                pltpu.SemaphoreType.DMA((n_x * n_z,)),
+                pltpu.SemaphoreType.DMA((2 * n_z,)),
             ],
         ),
         out_shape=[shape(rows, width), *sent, half, half],
-        compiler_params=params(16 * MIB),
+        compiler_params=params(20 * MIB),
         cost_estimate=pl.CostEstimate(
             flops=4 * n_z * rows * depth * width,
             bytes_accessed=4 * depth * width + 4 * n_z * rows * width,

time: 150 us -> 148 us (0.987)
  Pallas kernels: 35.7 us -> 33.4 us
    pallas_call x2, Pallas kernels: 18.8 us -> 16.5 us  [project(): pl.pallas_call(functools.partial(project_kernel, spots=spots, n_piece=len...]
  transfers between devices with their start and end apart: 25 -> 25, of which waited for: 17 -> 16; matrix products, arithmetic and copies ran while one was open for 5% -> 5% of each run, Pallas kernels for 23% -> 21%
where the time goes in v7:
time: 148 us
  waiting for transfers between devices  64.4 us (44%)
  Pallas kernels  33.4 us (23%)
  starting transfers between devices  32.8 us (22%)
  local copies, waits for them, and re-layouts  13.2 us (9%)
  other arithmetic  3.51 us (2%)
    ppermute x24, waiting for transfers between devices, shift(): lax.ppermute(array, axes, [(i, (i + by) % size) for i in range(size)])  57.9 us
    ppermute x24, starting transfers between devices, shift(): lax.ppermute(array, axes, [(i, (i + by) % size) for i in range(size)])  24.6 us
    pallas_call x2, Pallas kernels, project(): pl.pallas_call(functools.partial(project_kernel, spots=spots, n_piece=len...  16.5 us
    pallas_call x2, Pallas kernels, attend(): pl.pallas_call(functools.partial(attend_kernel, slots=slots), grid_spec=p...  10.7 us
    unnamed x44, local copies, waits for them, and re-layouts  9.71 us
    all_to_all x1, starting transfers between devices, local(): parts = lax.all_to_all(parts, ('yh', 'z'), 0, 0, tiled=True)  8.28 us
    all_to_all x1, waiting for transfers between devices, local(): parts = lax.all_to_all(parts, ('yh', 'z'), 0, 0, tiled=True)  6.51 us
    pallas_call x2, Pallas kernels, finish(): pl.pallas_call(finish_kernel, grid_spec=pltpu.PrefetchScalarGridSpec(num_...  3.27 us
  transfers between devices with their start and end apart: 25, of which 16 were waited for; matrix products, arithmetic and copies ran while one was open for 5% of the time, Pallas kernels for 21%

profile of v7, /device:TPU:24, one launch (start us, length us, event | category | flops | bytes accessed | tf_op | source)
XLA Modules:
  0.0 147.7 jit_solution(16159707714925407120)
XLA Ops:
  0.0 1.3 dynamic-slice_bitcast_fusion
  1.3 1.6 %collective-permute-start.2 = (bf16[160,1280]{1,0:T(8,128)(2,1)S(1)}, bf16[160,1280]{1,0:T(8,128)(2,1)S(1)}, u32[]{:S(2)}, u32[]{:S(2)}) collective-permute-start(bf16[160,1280]{1,0:T(8,128)(2,1)S(1)} %get-tuple-element.45), channel_id=1, source_target_pairs={{0,4},{4,8},{8,12},{12,0},{1,5},{5,9},{9,13},{13,1},{2,6},{6,10},{... | collective-permute-start | bytes 1228808 | tf_op jit(solution)/shard_map/ppermute | solution.py:282
  2.9 1.7 %collective-permute-start.3 = (bf16[160,1280]{1,0:T(8,128)(2,1)S(1)}, bf16[160,1280]{1,0:T(8,128)(2,1)}, u32[]{:S(2)}, u32[]{:S(2)}) collective-permute-start(bf16[160,1280]{1,0:T(8,128)(2,1)S(1)} %get-tuple-element.46), channel_id=1, source_target_pairs={{0,12},{4,0},{8,4},{12,8},{1,13},{5,1},{9,5},{13,9},{2,14},{6,2},{... | collective-permute-start | bytes 1228808 | tf_op jit(solution)/shard_map/ppermute | solution.py:282
  4.6 0.1 collective-permute-start
  4.8 1.9 %collective-permute-start.1 = (bf16[160,1280]{1,0:T(8,128)(2,1)S(1)}, bf16[160,1280]{1,0:T(8,128)(2,1)S(1)}, u32[]{:S(2)}, u32[]{:S(2)}) collective-permute-start(bf16[160,1280]{1,0:T(8,128)(2,1)S(1)} %get-tuple-element.46), channel_id=1, source_target_pairs={{0,66},{2,0},{64,2},{66,64},{1,67},{3,1},{65,3},{67,65},{4,70},{6,... | collective-permute-start | bytes 1228808 | tf_op jit(solution)/shard_map/ppermute | solution.py:282
  6.7 1.3 copy-done.6
  8.0 1.3 copy-done.7
  9.3 1.0 shard_map.64
  10.3 1.9 %copy-done = bf16[2,4,3,128,640]{4,3,2,1,0:T(8,128)(2,1)} copy-done((bf16[2,4,3,128,640]{4,3,2,1,0:T(8,128)(2,1)}, bf16[2,4,3,128,640]{4,3,2,1,0:T(8,128)(2,1)S(1)}, u32[]{:S(2)}) %copy-start) | copy-done | bytes 3932184
  12.2 1.6 %collective-permute-done.2 = bf16[160,1280]{1,0:T(8,128)(2,1)S(1)} collective-permute-done((bf16[160,1280]{1,0:T(8,128)(2,1)S(1)}, bf16[160,1280]{1,0:T(8,128)(2,1)S(1)}, u32[]{:S(2)}, u32[]{:S(2)}) %collective-permute-start.2) | collective-permute-done | bytes 409632 | tf_op jit(solution)/shard_map/ppermute | solution.py:282
  13.8 0.1 collective-permute-done.3
  13.9 1.3 collective-permute-done
  15.3 1.2 collective-permute-done.1
  16.5 8.3 %all-to-all-start = ((bf16[8,3,128,640]{3,2,1,0:T(8,128)(2,1)}), bf16[8,3,128,640]{3,2,1,0:T(8,128)(2,1)}, u32[]{:S(2)}, u32[]{:S(2)}) async-start(bf16[8,3,128,640]{3,2,1,0:T(8,128)(2,1)} %bitcast.15), calls=%async_computation | async-start | bytes 7864320 | tf_op jit(solution)/shard_map/all_to_all | solution.py:299
  24.8 1.3 pad_maximum_fusion.1
  26.0 1.6 %collective-permute-start.5 = (bf16[480,1280]{1,0:T(8,128)(2,1)S(1)}, bf16[480,1280]{1,0:T(8,128)(2,1)}, u32[]{:S(2)}, u32[]{:S(2)}) collective-permute-start(bf16[480,1280]{1,0:T(8,128)(2,1)S(1)} %pad_maximum_fusion.1), channel_id=1, source_target_pairs={{0,12},{4,0},{8,4},{12,8},{1,13},{5,1},{9,5},{13,9},{2,14},{6,2},{... | collective-permute-start | bytes 3686408 | tf_op jit(solution)/shard_map/ppermute | solution.py:282
  27.7 0.1 pad_maximum_fusion
  27.8 0.5 collective-permute-start.4
  28.4 1.0 constant_dynamic-update-slice_fusion.2
  29.5 0.1 collective-permute-start.6
  29.6 23.1 %collective-permute-done.5.refs_2_ = bf16[480,1280]{1,0:T(8,128)(2,1)} collective-permute-done((bf16[480,1280]{1,0:T(8,128)(2,1)S(1)}, bf16[480,1280]{1,0:T(8,128)(2,1)}, u32[]{:S(2)}, u32[]{:S(2)}) %collective-permute-start.5) | collective-permute-done | bytes 1228832 | tf_op jit(solution)/shard_map/ppermute | solution.py:282
  52.7 2.8 %collective-permute-done.4.refs_1_ = bf16[480,1280]{1,0:T(8,128)(2,1)} collective-permute-done((bf16[480,1280]{1,0:T(8,128)(2,1)S(1)}, bf16[480,1280]{1,0:T(8,128)(2,1)}, u32[]{:S(2)}, u32[]{:S(2)}) %collective-permute-start.4) | collective-permute-done | bytes 1228832 | tf_op jit(solution)/shard_map/ppermute | solution.py:282
  55.5 1.0 slice.17
  56.5 1.0 pad_maximum_fusion.3
  57.5 0.6 collective-permute-start.10
  58.1 1.0 slice.16
  59.1 0.9 pad_maximum_fusion.2
  60.1 1.4 collective-permute-start.9
  61.5 0.1 copy.9
  61.6 0.1 reshape.6
  61.7 0.1 add_add_fusion.1
  61.8 6.5 %all-to-all-done.q_ref.k_ref.v_ref = bf16[8,3,128,640]{3,2,1,0:T(8,128)(2,1)} async-done(((bf16[8,3,128,640]{3,2,1,0:T(8,128)(2,1)}), bf16[8,3,128,640]{3,2,1,0:T(8,128)(2,1)}, u32[]{:S(2)}, u32[]{:S(2)}) %all-to-all-start) | async-done | bytes 3932192 | tf_op jit(solution)/shard_map/all_to_all | solution.py:299
  68.3 5.8 %shard_map.66 = bf16[4,128,640]{2,1,0:T(8,128)(2,1)} custom-call(s32[98]{0:T(128)S(1)} %get-tuple-element.79.meta, bf16[8,3,128,640]{3,2,1,0:T(8,128)(2,1)} %all-to-all-done.q_ref.k_ref.v_ref, bf16[8,3,128,640]{3,2,1,0:T(8,128)(2,1)} %all-to-all-done.q_ref.k_ref.v_ref, bf16[8,3,128,640]{3,2,1,0:T(8,128)(2,1)} %all-to-all-done.q_ref.k_ref.v_ref), custom_call_target="tpu_custom_call" | custom-call | flops 503316480 | bytes 3932160 | tf_op jit(solution)/shard_map/pallas_call | solution.py:87
  74.1 0.9 collective-permute-start.11
  75.1 4.9 %shard_map.65.mine_ref = bf16[4,128,640]{2,1,0:T(8,128)(2,1)S(1)} custom-call(s32[98]{0:T(128)S(1)} %get-tuple-element.80.meta, bf16[8,3,128,640]{3,2,1,0:T(8,128)(2,1)} %all-to-all-done.q_ref.k_ref.v_ref, bf16[8,3,128,640]{3,2,1,0:T(8,128)(2,1)} %all-to-all-done.q_ref.k_ref.v_ref, bf16[8,3,128,640]{3,2,1,0:T(8,128)(2,1)} %all-to-all-done.q_ref.k_ref.v_ref), custom_call_target="tpu_custom_call" | custom-call | flops 503316480 | bytes 3932160 | tf_op jit(solution)/shard_map/pallas_call | solution.py:87
  80.0 1.7 %collective-permute-done.9.refs_3_ = bf16[320,1280]{1,0:T(8,128)(2,1)} collective-permute-done((bf16[320,1280]{1,0:T(8,128)(2,1)}, bf16[320,1280]{1,0:T(8,128)(2,1)}, u32[]{:S(2)}, u32[]{:S(2)}) %collective-permute-start.9) | collective-permute-done | bytes 819232 | tf_op jit(solution)/shard_map/ppermute | solution.py:282
  81.7 0.5 collective-permute-start.13
  82.3 9.9 %collective-permute-done.11.other_ref = bf16[4,128,640]{2,1,0:T(8,128)(2,1)} collective-permute-done((bf16[4,128,640]{2,1,0:T(8,128)(2,1)}, bf16[4,128,640]{2,1,0:T(8,128)(2,1)}, u32[]{:S(2)}, u32[]{:S(2)}) %collective-permute-start.11) | collective-permute-done | bytes 655392 | tf_op jit(solution)/shard_map/ppermute | solution.py:282
  92.2 8.1 %shard_map.69 = (bf16[128,2560]{1,0:T(8,128)(2,1)S(1)}, bf16[2,128,1280]{2,1,0:T(8,128)(2,1)S(1)}, bf16[2,128,1280]{2,1,0:T(8,128)(2,1)S(1)}, bf16[128,1280]{1,0:T(8,128)(2,1)S(1)}, bf16[128,1280]{1,0:T(8,128)(2,1)S(1)}) custom-call(s32[2]{0:T(128)S(1)} %pad_add_fusion.1.meta, bf16[4,128,640]{2,1,0:T(8,128)(2,1)S(1)} %shard_map.65.mine_ref, ...), custom_call_target="tpu_custom_call" | custom-call | flops 3355443200 | bytes 11796480 | tf_op jit(solution)/shard_map/pallas_call | solution.py:175
  100.3 0.8 copy-done.8
  101.1 1.2 collective-permute-start.20
  102.3 2.0 %collective-permute-start.21 = (bf16[2,128,1280]{2,1,0:T(8,128)(2,1)S(1)}, bf16[2,128,1280]{2,1,0:T(8,128)(2,1)S(1)}, u32[]{:S(2)}, u32[]{:S(2)}) collective-permute-start(bf16[2,128,1280]{2,1,0:T(8,128)(2,1)S(1)} %get-tuple-element.74), channel_id=1, source_target_pairs={{0,48},{16,0},{32,16},{48,32},{1,49},{17,1},{33,17},{49,33},{2,50}... | collective-permute-start | bytes 1966088 | tf_op jit(solution)/shard_map/ppermute | solution.py:282
  104.4 8.5 %shard_map.67 = (bf16[128,2560]{1,0:T(8,128)(2,1)S(1)}, bf16[128,1280]{1,0:T(8,128)(2,1)S(1)}, bf16[128,1280]{1,0:T(8,128)(2,1)}, bf16[128,1280]{1,0:T(8,128)(2,...) custom-call(s32[2]{0:T(128)S(1)} %pad_add_fusion.1.meta, ...), custom_call_target="tpu_custom_call" | custom-call | flops 3355443200 | bytes 11796480 | tf_op jit(solution)/shard_map/pallas_call | solution.py:175
  112.9 0.1 collective-permute-start.15
  113.0 3.2 %collective-permute-start.16 = (bf16[128,1280]{1,0:T(8,128)(2,1)S(1)}, bf16[128,1280]{1,0:T(8,128)(2,1)S(1)}, u32[]{:S(2)}, u32[]{:S(2)}) collective-permute-start(bf16[128,1280]{1,0:T(8,128)(2,1)S(1)} %get-tuple-element.66), channel_id=1, source_target_pairs={{0,48},{16,0},{32,16},{48,32},{1,49},{17,1},{33,17},{49,33},{2,50}... | collective-permute-start | bytes 983048 | tf_op jit(solution)/shard_map/ppermute | solution.py:282
  116.2 3.8 %collective-permute-done.20.x_ref.low_b = bf16[2,128,1280]{2,1,0:T(8,128)(2,1)S(1)} collective-permute-done((bf16[2,128,1280]{2,1,0:T(8,128)(2,1)S(1)}, bf16[2,128,1280]{2,1,0:T(8,128)(2,1)S(1)}, u32[]{:S(2)}, u32[]{:S(2)}) %collective-permute-start.20) | collective-permute-done | bytes 655392 | tf_op jit(solution)/shard_map/ppermute | solution.py:282
  120.0 0.9 shard_map.70
  121.0 0.8 copy-done.1
  121.8 2.0 %collective-permute-start.14 = (bf16[128,1280]{1,0:T(8,128)(2,1)}, bf16[128,1280]{1,0:T(8,128)(2,1)S(1)}, u32[]{:S(2)}, u32[]{:S(2)}) collective-permute-start(bf16[128,1280]{1,0:T(8,128)(2,1)} %get-tuple-element.62), channel_id=1, source_target_pairs={{0,16},{16,32},{32,48},{48,0},{1,17},{17,33},{33,49},{49,1},{2,18}... | collective-permute-start | bytes 983048 | tf_op jit(solution)/shard_map/ppermute | solution.py:282
  123.8 1.3 collective-permute-start.23
  125.1 1.9 %collective-permute-done.15.x_ref = bf16[128,1280]{1,0:T(8,128)(2,1)S(1)} collective-permute-done((bf16[128,1280]{1,0:T(8,128)(2,1)S(1)}, bf16[128,1280]{1,0:T(8,128)(2,1)S(1)}, u32[]{:S(2)}, u32[]{:S(2)}) %collective-permute-start.15) | collective-permute-done | bytes 327712 | tf_op jit(solution)/shard_map/ppermute | solution.py:282
  127.0 0.6 collective-permute-start.18
  127.6 0.9 shard_map.68
  128.6 1.4 collective-permute-start.17
  130.0 4.1 %collective-permute-done.22.low_a = bf16[128,1280]{1,0:T(8,128)(2,1)S(1)} collective-permute-done((bf16[128,1280]{1,0:T(8,128)(2,1)S(1)}, bf16[128,1280]{1,0:T(8,128)(2,1)S(1)}, u32[]{:S(2)}, u32[]{:S(2)}) %collective-permute-start.22) | collective-permute-done | bytes 327712 | tf_op jit(solution)/shard_map/ppermute | solution.py:282
  134.0 1.6 %collective-permute-start.19 = (bf16[128,1280]{1,0:T(8,128)(2,1)}, bf16[128,1280]{1,0:T(8,128)(2,1)S(1)}, u32[]{:S(2)}, u32[]{:S(2)}) collective-permute-start(bf16[128,1280]{1,0:T(8,128)(2,1)} %get-tuple-element.69), channel_id=1, source_target_pairs={{0,48},{16,0},{32,16},{48,32},{1,49},{17,1},{33,17},{49,33},{2,50}... | collective-permute-start | bytes 983048 | tf_op jit(solution)/shard_map/ppermute | solution.py:282
  135.8 1.1 copy-done.2
  136.9 1.1 copy-done.4
  137.9 1.6 %shard_map.71.refs_0_ = bf16[1,128,5120]{2,1,0:T(8,128)(2,1)} custom-call(s32[2]{0:T(128)S(1)} %get-tuple-element.82.meta, f32[1,5120]{1,0:T(1,128)S(1)} %copy-done.12, bf16[128,2560]{1,0:T(8,128)(2,1)S(1)} %copy-done.9, bf16[2,128,1280]{2,1,0:T(8,128)(2,1)S(1)} %copy-done.2, bf16[128,1280]{1,0:T(8,128)(2,1)S(1)} %collective-permute-done.22.low_a, ...), custom_call_target="tpu_custom_call" | custom-call | flops 1310720 | bytes 2621440 | tf_op jit(solution)/shard_map/pallas_call | solution.py:255
  139.6 1.5 collective-permute-done.14.low_b
  141.1 1.2 collective-permute-done.18.high_a
  142.3 3.5 %collective-permute-done.17.low_a = bf16[128,1280]{1,0:T(8,128)(2,1)S(1)} collective-permute-done((bf16[128,1280]{1,0:T(8,128)(2,1)}, bf16[128,1280]{1,0:T(8,128)(2,1)S(1)}, u32[]{:S(2)}, u32[]{:S(2)}) %collective-permute-start.17) | collective-permute-done | bytes 327712 | tf_op jit(solution)/shard_map/ppermute | solution.py:282
  145.8 0.1 collective-permute-done.19.high_b
  146.0 1.6 %shard_map.72 = bf16[1,128,5120]{2,1,0:T(8,128)(2,1)} custom-call(s32[2]{0:T(128)S(1)} %get-tuple-element.81.meta, f32[1,5120]{1,0:T(1,128)S(1)} %copy-done.12, bf16[128,2560]{1,0:T(8,128)(2,1)S(1)} %copy-done.11, bf16[128,1280]{1,0:T(8,128)(2,1)S(1)} %collective-permute-done.14.low_b, ...), custom_call_target="tpu_custom_call", output_to_operand_aliasing={{}: (7, {})} | custom-call | flops 1310720 | bytes 2621440 | tf_op jit(solution)/shard_map/pallas_call | solution.py:255
  (51 shorter events, 0.5 us)
Async XLA Ops:
  0.0 6.6 %copy-start.5 = (bf16[1,128,5120]{2,1,0:T(8,128)(2,1)S(1)}, bf16[1,128,5120]{2,1,0:T(8,128)(2,1)}, u32[]{:S(2)}) copy-start(bf16[1,128,5120]{2,1,0:T(8,128)(2,1)} %param.6) | copy-start | bytes 3932164
  1.3 9.0 %copy-start.13 = (bf16[160,1280]{1,0:T(8,128)(2,1)}, bf16[160,1280]{1,0:T(8,128)(2,1)S(1)}, u32[]{:S(2)}) copy-start(bf16[160,1280]{1,0:T(8,128)(2,1)S(1)} %get-tuple-element.46) | copy-start | bytes 1228804
  1.3 12.6 %copy-start.15 = (bf16[160,1280]{1,0:T(8,128)(2,1)}, bf16[160,1280]{1,0:T(8,128)(2,1)S(1)}, u32[]{:S(2)}) copy-start(bf16[160,1280]{1,0:T(8,128)(2,1)S(1)} %get-tuple-element.45) | copy-start | bytes 1228804
  1.3 12.5 %collective-permute-start.2 = (bf16[160,1280]{1,0:T(8,128)(2,1)S(1)}, bf16[160,1280]{1,0:T(8,128)(2,1)S(1)}, u32[]{:S(2)}, u32[]{:S(2)}) collective-permute-start(bf16[160,1280]{1,0:T(8,128)(2,1)S(1)} %get-tuple-element.45), channel_id=1, source_target_pairs={{0,4},{4,8},{8,12},{12,0},{1,5},{5,9},{9,13},{13,1},{2,6},{6,10},{... | collective-permute-start | bytes 1228808 | tf_op jit(solution)/shard_map/ppermute | solution.py:282
  2.9 11.0 %collective-permute-start.3 = (bf16[160,1280]{1,0:T(8,128)(2,1)S(1)}, bf16[160,1280]{1,0:T(8,128)(2,1)}, u32[]{:S(2)}, u32[]{:S(2)}) collective-permute-start(bf16[160,1280]{1,0:T(8,128)(2,1)S(1)} %get-tuple-element.46), channel_id=1, source_target_pairs={{0,12},{4,0},{8,4},{12,8},{1,13},{5,1},{9,5},{13,9},{2,14},{6,2},{... | collective-permute-start | bytes 1228808 | tf_op jit(solution)/shard_map/ppermute | solution.py:282
  4.6 10.6 %collective-permute-start = (bf16[160,1280]{1,0:T(8,128)(2,1)S(1)}, bf16[160,1280]{1,0:T(8,128)(2,1)S(1)}, u32[]{:S(2)}, u32[]{:S(2)}) collective-permute-start(bf16[160,1280]{1,0:T(8,128)(2,1)S(1)} %get-tuple-element.45), channel_id=1, source_target_pairs={{0,2},{2,64},{64,66},{66,0},{1,3},{3,65},{65,67},{67,1},{4,6},{6,6... | collective-permute-start | bytes 1228808 | tf_op jit(solution)/shard_map/ppermute | solution.py:282
  4.8 11.7 %collective-permute-start.1 = (bf16[160,1280]{1,0:T(8,128)(2,1)S(1)}, bf16[160,1280]{1,0:T(8,128)(2,1)S(1)}, u32[]{:S(2)}, u32[]{:S(2)}) collective-permute-start(bf16[160,1280]{1,0:T(8,128)(2,1)S(1)} %get-tuple-element.46), channel_id=1, source_target_pairs={{0,66},{2,0},{64,2},{66,64},{1,67},{3,1},{65,3},{67,65},{4,70},{6,... | collective-permute-start | bytes 1228808 | tf_op jit(solution)/shard_map/ppermute | solution.py:282
  6.6 1.3 copy-start.6
  8.0 1.3 copy-start.7
  10.3 1.9 %copy-start = (bf16[2,4,3,128,640]{4,3,2,1,0:T(8,128)(2,1)}, bf16[2,4,3,128,640]{4,3,2,1,0:T(8,128)(2,1)S(1)}, u32[]{:S(2)}) copy-start(bf16[2,4,3,128,640]{4,3,2,1,0:T(8,128)(2,1)S(1)} %shard_map.64) | copy-start | bytes 11796484
  13.8 2.7 %copy-start.16 = (bf16[160,1280]{1,0:T(8,128)(2,1)}, bf16[160,1280]{1,0:T(8,128)(2,1)S(1)}, u32[]{:S(2)}) copy-start(bf16[160,1280]{1,0:T(8,128)(2,1)S(1)} %collective-permute-done.2) | copy-start | bytes 1228804
  16.5 51.8 %all-to-all-start = ((bf16[8,3,128,640]{3,2,1,0:T(8,128)(2,1)}), bf16[8,3,128,640]{3,2,1,0:T(8,128)(2,1)}, u32[]{:S(2)}, u32[]{:S(2)}) async-start(bf16[8,3,128,640]{3,2,1,0:T(8,128)(2,1)} %bitcast.15), calls=%async_computation | async-start | bytes 7864320 | tf_op jit(solution)/shard_map/all_to_all | solution.py:299
  24.8 2.9 %copy-start.14 = (bf16[160,1280]{1,0:T(8,128)(2,1)S(1)}, bf16[160,1280]{1,0:T(8,128)(2,1)}, u32[]{:S(2)}) copy-start(bf16[160,1280]{1,0:T(8,128)(2,1)} %copy-done.13) | copy-start | bytes 1228804
  24.8 2.9 %copy-start.17 = (bf16[160,1280]{1,0:T(8,128)(2,1)S(1)}, bf16[160,1280]{1,0:T(8,128)(2,1)}, u32[]{:S(2)}) copy-start(bf16[160,1280]{1,0:T(8,128)(2,1)} %copy-done.16) | copy-start | bytes 1228804
  26.0 26.7 %collective-permute-start.5 = (bf16[480,1280]{1,0:T(8,128)(2,1)S(1)}, bf16[480,1280]{1,0:T(8,128)(2,1)}, u32[]{:S(2)}, u32[]{:S(2)}) collective-permute-start(bf16[480,1280]{1,0:T(8,128)(2,1)S(1)} %pad_maximum_fusion.1), channel_id=1, source_target_pairs={{0,12},{4,0},{8,4},{12,8},{1,13},{5,1},{9,5},{13,9},{2,14},{6,2},{... | collective-permute-start | bytes 3686408 | tf_op jit(solution)/shard_map/ppermute | solution.py:282
  27.8 27.7 %collective-permute-start.4 = (bf16[480,1280]{1,0:T(8,128)(2,1)S(1)}, bf16[480,1280]{1,0:T(8,128)(2,1)}, u32[]{:S(2)}, u32[]{:S(2)}) collective-permute-start(bf16[480,1280]{1,0:T(8,128)(2,1)S(1)} %pad_maximum_fusion), channel_id=1, source_target_pairs={{0,4},{4,8},{8,12},{12,0},{1,5},{5,9},{9,13},{13,1},{2,6},{6,10},{... | collective-permute-start | bytes 3686408 | tf_op jit(solution)/shard_map/ppermute | solution.py:282
  29.5 32.0 %copy-start.18 = (s32[16,6]{0,1:T(8,128)S(1)}, s32[16,6]{0,1:T(8,128)}, u32[]{:S(2)}) copy-start(s32[16,6]{0,1:T(8,128)} %param.11) | copy-start | bytes 1156
  29.5 32.3 %collective-permute-start.6 = (bf16[960,1280]{1,0:T(8,128)(2,1)S(1)}, bf16[960,1280]{1,0:T(8,128)(2,1)}, u32[]{:S(2)}, u32[]{:S(2)}) collective-permute-start(bf16[960,1280]{1,0:T(8,128)(2,1)S(1)} %constant_dynamic-update-slice_fusion.refs_0_), channel_id=1, source_target_pairs={{0,1},{1,0},{2,3},{3,2},{4,5},{5,4},{6,7},{7,6},{8,9},{9,8},{10,11... | collective-permute-start | bytes 7372808 | tf_op jit(solution)/shard_map/ppermute | solution.py:282
  52.7 9.1 %collective-permute-start.8 = (bf16[480,1280]{1,0:T(8,128)(2,1)}, bf16[480,1280]{1,0:T(8,128)(2,1)}, u32[]{:S(2)}, u32[]{:S(2)}) collective-permute-start(bf16[480,1280]{1,0:T(8,128)(2,1)} %collective-permute-done.5.refs_2_), channel_id=1, source_target_pairs={{0,1},{1,0},{2,3},{3,2},{4,5},{5,4},{6,7},{7,6},{8,9},{9,8},{10,11... | collective-permute-start | bytes 3686408 | tf_op jit(solution)/shard_map/ppermute | solution.py:282
  55.5 6.3 %collective-permute-start.7 = (bf16[480,1280]{1,0:T(8,128)(2,1)}, bf16[480,1280]{1,0:T(8,128)(2,1)}, u32[]{:S(2)}, u32[]{:S(2)}) collective-permute-start(bf16[480,1280]{1,0:T(8,128)(2,1)} %collective-permute-done.4.refs_1_), channel_id=1, source_target_pairs={{0,1},{1,0},{2,3},{3,2},{4,5},{5,4},{6,7},{7,6},{8,9},{9,8},{10,11... | collective-permute-start | bytes 3686408 | tf_op jit(solution)/shard_map/ppermute | solution.py:282
  57.5 22.5 %collective-permute-start.10 = (bf16[320,1280]{1,0:T(8,128)(2,1)}, bf16[320,1280]{1,0:T(8,128)(2,1)}, u32[]{:S(2)}, u32[]{:S(2)}) collective-permute-start(bf16[320,1280]{1,0:T(8,128)(2,1)} %pad_maximum_fusion.3), channel_id=1, source_target_pairs={{0,12},{4,0},{8,4},{12,8},{1,13},{5,1},{9,5},{13,9},{2,14},{6,2},{... | collective-permute-start | bytes 2457608 | tf_op jit(solution)/shard_map/ppermute | solution.py:282
  60.1 21.6 %collective-permute-start.9 = (bf16[320,1280]{1,0:T(8,128)(2,1)}, bf16[320,1280]{1,0:T(8,128)(2,1)}, u32[]{:S(2)}, u32[]{:S(2)}) collective-permute-start(bf16[320,1280]{1,0:T(8,128)(2,1)} %pad_maximum_fusion.2), channel_id=1, source_target_pairs={{0,4},{4,8},{8,12},{12,0},{1,5},{5,9},{9,13},{13,1},{2,6},{6,10},{... | collective-permute-start | bytes 2457608 | tf_op jit(solution)/shard_map/ppermute | solution.py:282
  74.1 18.1 %collective-permute-start.11 = (bf16[4,128,640]{2,1,0:T(8,128)(2,1)}, bf16[4,128,640]{2,1,0:T(8,128)(2,1)}, u32[]{:S(2)}, u32[]{:S(2)}) collective-permute-start(bf16[4,128,640]{2,1,0:T(8,128)(2,1)} %shard_map.66), channel_id=1, source_target_pairs={{0,64},{64,0},{1,65},{65,1},{2,66},{66,2},{3,67},{67,3},{4,68},{68... | collective-permute-start | bytes 1966088 | tf_op jit(solution)/shard_map/ppermute | solution.py:282
  81.7 22.7 %collective-permute-start.12 = (bf16[320,1280]{1,0:T(8,128)(2,1)}, bf16[320,1280]{1,0:T(8,128)(2,1)}, u32[]{:S(2)}, u32[]{:S(2)}) collective-permute-start(bf16[320,1280]{1,0:T(8,128)(2,1)} %collective-permute-done.9.refs_3_), channel_id=1, source_target_pairs={{0,1},{1,0},{2,3},{3,2},{4,5},{5,4},{6,7},{7,6},{8,9},{9,8},{10,11... | collective-permute-start | bytes 2457608 | tf_op jit(solution)/shard_map/ppermute | solution.py:282
  81.7 22.7 %collective-permute-start.13 = (bf16[320,1280]{1,0:T(8,128)(2,1)}, bf16[320,1280]{1,0:T(8,128)(2,1)}, u32[]{:S(2)}, u32[]{:S(2)}) collective-permute-start(bf16[320,1280]{1,0:T(8,128)(2,1)} %collective-permute-done.10.refs_4_), channel_id=1, source_target_pairs={{0,1},{1,0},{2,3},{3,2},{4,5},{5,4},{6,7},{7,6},{8,9},{9,8},{10,11... | collective-permute-start | bytes 2457608 | tf_op jit(solution)/shard_map/ppermute | solution.py:282
  100.3 0.8 copy-start.8
  101.1 18.9 %collective-permute-start.20 = (bf16[2,128,1280]{2,1,0:T(8,128)(2,1)S(1)}, bf16[2,128,1280]{2,1,0:T(8,128)(2,1)S(1)}, u32[]{:S(2)}, u32[]{:S(2)}) collective-permute-start(bf16[2,128,1280]{2,1,0:T(8,128)(2,1)S(1)} %get-tuple-element.71), channel_id=1, source_target_pairs={{0,16},{16,32},{32,48},{48,0},{1,17},{17,33},{33,49},{49,1},{2,18}... | collective-permute-start | bytes 1966088 | tf_op jit(solution)/shard_map/ppermute | solution.py:282
  102.3 17.7 %collective-permute-start.21 = (bf16[2,128,1280]{2,1,0:T(8,128)(2,1)S(1)}, bf16[2,128,1280]{2,1,0:T(8,128)(2,1)S(1)}, u32[]{:S(2)}, u32[]{:S(2)}) collective-permute-start(bf16[2,128,1280]{2,1,0:T(8,128)(2,1)S(1)} %get-tuple-element.74), channel_id=1, source_target_pairs={{0,48},{16,0},{32,16},{48,32},{1,49},{17,1},{33,17},{49,33},{2,50}... | collective-permute-start | bytes 1966088 | tf_op jit(solution)/shard_map/ppermute | solution.py:282
  112.8 9.0 %copy-start.10 = (bf16[128,2560]{1,0:T(8,128)(2,1)}, bf16[128,2560]{1,0:T(8,128)(2,1)S(1)}, u32[]{:S(2)}) copy-start(bf16[128,2560]{1,0:T(8,128)(2,1)S(1)} %get-tuple-element.61.own) | copy-start | bytes 1966084
  112.9 22.9 %copy-start.9 = (bf16[128,2560]{1,0:T(8,128)(2,1)S(1)}, bf16[128,2560]{1,0:T(8,128)(2,1)}, u32[]{:S(2)}) copy-start(bf16[128,2560]{1,0:T(8,128)(2,1)} %copy-done.8) | copy-start | bytes 1966084
  112.9 22.9 %copy-start.12 = (f32[1,5120]{1,0:T(1,128)S(1)}, f32[1,5120]{1,0:T(1,128)}, u32[]{:S(2)}) copy-start(f32[1,5120]{1,0:T(1,128)} %gate_ref.3) | copy-start | bytes 61444
  112.9 14.2 %collective-permute-start.15 = (bf16[128,1280]{1,0:T(8,128)(2,1)S(1)}, bf16[128,1280]{1,0:T(8,128)(2,1)S(1)}, u32[]{:S(2)}, u32[]{:S(2)}) collective-permute-start(bf16[128,1280]{1,0:T(8,128)(2,1)S(1)} %get-tuple-element.64), channel_id=1, source_target_pairs={{0,16},{16,32},{32,48},{48,0},{1,17},{17,33},{33,49},{49,1},{2,18}... | collective-permute-start | bytes 983048 | tf_op jit(solution)/shard_map/ppermute | solution.py:282
  113.0 14.7 %collective-permute-start.16 = (bf16[128,1280]{1,0:T(8,128)(2,1)S(1)}, bf16[128,1280]{1,0:T(8,128)(2,1)S(1)}, u32[]{:S(2)}, u32[]{:S(2)}) collective-permute-start(bf16[128,1280]{1,0:T(8,128)(2,1)S(1)} %get-tuple-element.66), channel_id=1, source_target_pairs={{0,48},{16,0},{32,16},{48,32},{1,49},{17,1},{33,17},{49,33},{2,50}... | collective-permute-start | bytes 983048 | tf_op jit(solution)/shard_map/ppermute | solution.py:282
  120.0 0.9 copy-start.3
  121.0 0.8 copy-start.1
  121.8 12.2 %collective-permute-start.22 = (bf16[128,1280]{1,0:T(8,128)(2,1)S(1)}, bf16[128,1280]{1,0:T(8,128)(2,1)S(1)}, u32[]{:S(2)}, u32[]{:S(2)}) collective-permute-start(bf16[128,1280]{1,0:T(8,128)(2,1)S(1)} %get-tuple-element.75), channel_id=1, source_target_pairs={{0,16},{16,32},{32,48},{48,0},{1,17},{17,33},{33,49},{49,1},{2,18}... | collective-permute-start | bytes 983048 | tf_op jit(solution)/shard_map/ppermute | solution.py:282
  121.8 19.3 %collective-permute-start.14 = (bf16[128,1280]{1,0:T(8,128)(2,1)}, bf16[128,1280]{1,0:T(8,128)(2,1)S(1)}, u32[]{:S(2)}, u32[]{:S(2)}) collective-permute-start(bf16[128,1280]{1,0:T(8,128)(2,1)} %get-tuple-element.62), channel_id=1, source_target_pairs={{0,16},{16,32},{32,48},{48,0},{1,17},{17,33},{33,49},{49,1},{2,18}... | collective-permute-start | bytes 983048 | tf_op jit(solution)/shard_map/ppermute | solution.py:282
  123.8 11.9 %collective-permute-start.23 = (bf16[128,1280]{1,0:T(8,128)(2,1)}, bf16[128,1280]{1,0:T(8,128)(2,1)S(1)}, u32[]{:S(2)}, u32[]{:S(2)}) collective-permute-start(bf16[128,1280]{1,0:T(8,128)(2,1)} %get-tuple-element.76), channel_id=1, source_target_pairs={{0,48},{16,0},{32,16},{48,32},{1,49},{17,1},{33,17},{49,33},{2,50}... | collective-permute-start | bytes 983048 | tf_op jit(solution)/shard_map/ppermute | solution.py:282
  127.0 15.3 %collective-permute-start.18 = (bf16[128,1280]{1,0:T(8,128)(2,1)}, bf16[128,1280]{1,0:T(8,128)(2,1)S(1)}, u32[]{:S(2)}, u32[]{:S(2)}) collective-permute-start(bf16[128,1280]{1,0:T(8,128)(2,1)} %get-tuple-element.68), channel_id=1, source_target_pairs={{0,48},{16,0},{32,16},{48,32},{1,49},{17,1},{33,17},{49,33},{2,50}... | collective-permute-start | bytes 983048 | tf_op jit(solution)/shard_map/ppermute | solution.py:282
  127.6 18.3 %copy-start.11 = (bf16[128,2560]{1,0:T(8,128)(2,1)S(1)}, bf16[128,2560]{1,0:T(8,128)(2,1)}, u32[]{:S(2)}) copy-start(bf16[128,2560]{1,0:T(8,128)(2,1)} %copy-done.10) | copy-start | bytes 1966084
  128.6 17.2 %collective-permute-start.17 = (bf16[128,1280]{1,0:T(8,128)(2,1)}, bf16[128,1280]{1,0:T(8,128)(2,1)S(1)}, u32[]{:S(2)}, u32[]{:S(2)}) collective-permute-start(bf16[128,1280]{1,0:T(8,128)(2,1)} %get-tuple-element.67), channel_id=1, source_target_pairs={{0,16},{16,32},{32,48},{48,0},{1,17},{17,33},{33,49},{49,1},{2,18}... | collective-permute-start | bytes 983048 | tf_op jit(solution)/shard_map/ppermute | solution.py:282
  134.0 11.9 %collective-permute-start.19 = (bf16[128,1280]{1,0:T(8,128)(2,1)}, bf16[128,1280]{1,0:T(8,128)(2,1)S(1)}, u32[]{:S(2)}, u32[]{:S(2)}) collective-permute-start(bf16[128,1280]{1,0:T(8,128)(2,1)} %get-tuple-element.69), channel_id=1, source_target_pairs={{0,48},{16,0},{32,16},{48,32},{1,49},{17,1},{33,17},{49,33},{2,50}... | collective-permute-start | bytes 983048 | tf_op jit(solution)/shard_map/ppermute | solution.py:282
  135.8 1.1 copy-start.2
  136.9 1.1 copy-start.4

commit v8 on v7

--- a/solution.py
+++ b/solution.py
@@ -42,14 +42,26 @@
     )(q, k, v)
 
 
-def attend_kernel(meta, q_ref, k_ref, v_ref, o_ref, *, slots):
+def attend_kernel(meta, parts_ref, o_ref, q_ref, k_ref, v_ref, sem, *, slots, groups):
     blocks, rows, width = q_ref.shape
     per = rows // FRAME
-    heads = width // HEAD_DIM
     n_key = slots * FRAME
     scale = 1.0 / math.sqrt(HEAD_DIM)
+    loads, at = [], 0
+    for n, group in enumerate(groups):
+        cols = pl.ds(at * HEAD_DIM, group * HEAD_DIM)
+        mine = parts_ref.at[pl.ds(meta[0] * blocks, blocks), 0, :, cols]
+        copies = [pltpu.make_async_copy(mine, q_ref.at[:, :, cols], sem.at[3 * n])]
+        for which, ref in ((1, k_ref), (2, v_ref)):
+            source = parts_ref.at[:, which, :, cols]
+            copies.append(pltpu.make_async_copy(source, ref.at[:, :, cols], sem.at[3 * n + which]))
+        for copy in copies:
+            copy.start()
+        loads.append((copies, range(at, at + group)))
+        at += group
+
     lane = lax.broadcasted_iota(jnp.int32, (1, n_key), 1)
-    work = []
+    frames = []
     for r in range(blocks):
         block = lax.rem(meta[1] + r, blocks)
         for p in range(per):
@@ -62,46 +74,51 @@
                 bias = jnp.where(inside, jnp.where(g >= 0, 0.0, -1e30), bias)
                 g = jnp.maximum(g, 0)
                 picks.append((g // per, pl.multiple_of((g % per) * FRAME, FRAME)))
-            for h in range(heads):
-                work.append((r, p, slice(h * HEAD_DIM, (h + 1) * HEAD_DIM), block, picks, bias))
-    scores = []
-    for r, p, cols, block, picks, bias in work:
-        key = jnp.concatenate([k_ref[b, pl.ds(o, FRAME), cols] for b, o in picks], 0)
-        query = q_ref[block, p * FRAME : (p + 1) * FRAME, cols]
-        score = lax.dot_general(query, key, NT, preferred_element_type=jnp.float32)
-        scores.append(score * scale + bias)
-    tops = [jnp.max(s, axis=1, keepdims=True) for s in scores]
-    probs = [jnp.exp(s - t) for s, t in zip(scores, tops)]
-    denoms = [jnp.sum(p, axis=1, keepdims=True) for p in probs]
-    for (r, p, cols, block, picks, bias), prob, denom in zip(work, probs, denoms):
-        val = jnp.concatenate([v_ref[b, pl.ds(o, FRAME), cols] for b, o in picks], 0)
-        accum = jnp.dot(prob.astype(jnp.bfloat16), val, preferred_element_type=jnp.float32)
-        o_ref[r, p * FRAME : (p + 1) * FRAME, cols] = (accum / denom).astype(jnp.bfloat16)
+            frames.append((r, p, block, picks, bias))
+    for copies, heads in loads:
+        for copy in copies:
+            copy.wait()
+        work = [(*frame, slice(h * HEAD_DIM, (h + 1) * HEAD_DIM)) for frame in frames for h in heads]
+        scores = []
+        for r, p, block, picks, bias, cols in work:
+            key = jnp.concatenate([k_ref[b, pl.ds(o, FRAME), cols] for b, o in picks], 0)
+            query = q_ref[block, p * FRAME : (p + 1) * FRAME, cols]
+            score = lax.dot_general(query, key, NT, preferred_element_type=jnp.float32)
+            scores.append(score * scale + bias)
+        tops = [jnp.max(s, axis=1, keepdims=True) for s in scores]
+        probs = [jnp.exp(s - t) for s, t in zip(scores, tops)]
+        denoms = [jnp.sum(p, axis=1, keepdims=True) for p in probs]
+        for (r, p, block, picks, bias, cols), prob, denom in zip(work, probs, denoms):
+            val = jnp.concatenate([v_ref[b, pl.ds(o, FRAME), cols] for b, o in picks], 0)
+            accum = jnp.dot(prob.astype(jnp.bfloat16), val, preferred_element_type=jnp.float32)
+            o_ref[r, p * FRAME : (p + 1) * FRAME, cols] = (accum / denom).astype(jnp.bfloat16)
 
 
 def attend(meta, parts, slots, n_y):
     blocks, _, rows, width = parts.shape
     n_z = blocks // n_y
-    whole = lambda which: pl.BlockSpec((blocks, None, rows, width), lambda i, m: (0, which, 0, 0))
     work = n_z * rows * slots * FRAME * width
-    return pl.pallas_call(
-        functools.partial(attend_kernel, slots=slots),
+    groups = (2, 3)
+    return pl.pallas_call(
+        functools.partial(attend_kernel, slots=slots, groups=groups),
         grid_spec=pltpu.PrefetchScalarGridSpec(
             num_scalar_prefetch=1,
             grid=(1,),
-            in_specs=[
-                pl.BlockSpec((n_z, None, rows, width), lambda i, m: (m[0], 0, 0, 0)),
-                whole(1),
-                whole(2),
+            in_specs=[pl.BlockSpec(memory_space=pl.ANY)],
+            out_specs=pl.BlockSpec((n_z, rows, width), lambda i, m: (0, 0, 0)),
+            scratch_shapes=[
+                pltpu.VMEM((n_z, rows, width), jnp.bfloat16),
+                pltpu.VMEM((blocks, rows, width), jnp.bfloat16),
+                pltpu.VMEM((blocks, rows, width), jnp.bfloat16),
+                pltpu.SemaphoreType.DMA((3 * len(groups),)),
             ],
-            out_specs=pl.BlockSpec((n_z, rows, width), lambda i, m: (0, 0, 0)),
         ),
         out_shape=jax.ShapeDtypeStruct((n_z, rows, width), jnp.bfloat16),
         compiler_params=params(32 * MIB),
         cost_estimate=pl.CostEstimate(
             flops=work * 4, bytes_accessed=3 * blocks * rows * width * 2, transcendentals=work // HEAD_DIM
         ),
-    )(meta, parts, parts, parts)
+    )(meta, parts)
 
 
 def project_kernel(meta, mine_ref, other_ref, *refs, spots, n_piece, paired):

time: 148 us -> 148 us (level)
  no operation moved by 1% of the time
where the time goes in v8:
time: 148 us
  waiting for transfers between devices  64.7 us (44%)
  starting transfers between devices  32.9 us (22%)
  Pallas kernels  32.9 us (22%)
  local copies, waits for them, and re-layouts  13.2 us (9%)
  other arithmetic  3.51 us (2%)
    ppermute x24, waiting for transfers between devices, shift(): lax.ppermute(array, axes, [(i, (i + by) % size) for i in range(size)])  58.2 us
    ppermute x24, starting transfers between devices, shift(): lax.ppermute(array, axes, [(i, (i + by) % size) for i in range(size)])  24.6 us
    pallas_call x2, Pallas kernels, project(): pl.pallas_call(functools.partial(project_kernel, spots=spots, n_piece=len...  16.5 us
    pallas_call x2, Pallas kernels, attend(): pl.pallas_call(functools.partial(attend_kernel, slots=slots, groups=group...  10.3 us
    unnamed x44, local copies, waits for them, and re-layouts  9.71 us
    all_to_all x1, starting transfers between devices, local(): parts = lax.all_to_all(parts, ('yh', 'z'), 0, 0, tiled=True)  8.28 us
    all_to_all x1, waiting for transfers between devices, local(): parts = lax.all_to_all(parts, ('yh', 'z'), 0, 0, tiled=True)  6.51 us
    pallas_call x2, Pallas kernels, finish(): pl.pallas_call(finish_kernel, grid_spec=pltpu.PrefetchScalarGridSpec(num_...  3.27 us
  transfers between devices with their start and end apart: 25, of which 16 were waited for; matrix products, arithmetic and copies ran while one was open for 5% of the time, Pallas kernels for 21%

profile of v8, /device:TPU:24, one launch (start us, length us, event | category | flops | bytes accessed | tf_op | source)
XLA Modules:
  0.0 147.6 jit_solution(796191843589885322)
XLA Ops:
  0.0 1.3 dynamic-slice_bitcast_fusion
  1.3 1.6 %collective-permute-start.2 = (bf16[160,1280]{1,0:T(8,128)(2,1)S(1)}, bf16[160,1280]{1,0:T(8,128)(2,1)S(1)}, u32[]{:S(2)}, u32[]{:S(2)}) collective-permute-start(bf16[160,1280]{1,0:T(8,128)(2,1)S(1)} %get-tuple-element.45), channel_id=1, source_target_pairs={{0,4},{4,8},{8,12},{12,0},{1,5},{5,9},{9,13},{13,1},{2,6},{6,10},{... | collective-permute-start | bytes 1228808 | tf_op jit(solution)/shard_map/ppermute | solution.py:299
  2.9 1.7 %collective-permute-start.3 = (bf16[160,1280]{1,0:T(8,128)(2,1)S(1)}, bf16[160,1280]{1,0:T(8,128)(2,1)}, u32[]{:S(2)}, u32[]{:S(2)}) collective-permute-start(bf16[160,1280]{1,0:T(8,128)(2,1)S(1)} %get-tuple-element.46), channel_id=1, source_target_pairs={{0,12},{4,0},{8,4},{12,8},{1,13},{5,1},{9,5},{13,9},{2,14},{6,2},{... | collective-permute-start | bytes 1228808 | tf_op jit(solution)/shard_map/ppermute | solution.py:299
  4.6 0.1 collective-permute-start
  4.8 1.9 %collective-permute-start.1 = (bf16[160,1280]{1,0:T(8,128)(2,1)S(1)}, bf16[160,1280]{1,0:T(8,128)(2,1)S(1)}, u32[]{:S(2)}, u32[]{:S(2)}) collective-permute-start(bf16[160,1280]{1,0:T(8,128)(2,1)S(1)} %get-tuple-element.46), channel_id=1, source_target_pairs={{0,66},{2,0},{64,2},{66,64},{1,67},{3,1},{65,3},{67,65},{4,70},{6,... | collective-permute-start | bytes 1228808 | tf_op jit(solution)/shard_map/ppermute | solution.py:299
  6.7 1.3 copy-done.6
  8.0 1.3 copy-done.7
  9.3 1.0 shard_map.64
  10.3 1.9 %copy-done = bf16[2,4,3,128,640]{4,3,2,1,0:T(8,128)(2,1)} copy-done((bf16[2,4,3,128,640]{4,3,2,1,0:T(8,128)(2,1)}, bf16[2,4,3,128,640]{4,3,2,1,0:T(8,128)(2,1)S(1)}, u32[]{:S(2)}) %copy-start) | copy-done | bytes 3932184
  12.2 1.6 %collective-permute-done.2 = bf16[160,1280]{1,0:T(8,128)(2,1)S(1)} collective-permute-done((bf16[160,1280]{1,0:T(8,128)(2,1)S(1)}, bf16[160,1280]{1,0:T(8,128)(2,1)S(1)}, u32[]{:S(2)}, u32[]{:S(2)}) %collective-permute-start.2) | collective-permute-done | bytes 409632 | tf_op jit(solution)/shard_map/ppermute | solution.py:299
  13.8 0.1 collective-permute-done.3
  13.9 1.3 collective-permute-done
  15.3 1.2 collective-permute-done.1
  16.5 8.3 %all-to-all-start = ((bf16[8,3,128,640]{3,2,1,0:T(8,128)(2,1)}), bf16[8,3,128,640]{3,2,1,0:T(8,128)(2,1)}, u32[]{:S(2)}, u32[]{:S(2)}) async-start(bf16[8,3,128,640]{3,2,1,0:T(8,128)(2,1)} %bitcast.15), calls=%async_computation | async-start | bytes 7864320 | tf_op jit(solution)/shard_map/all_to_all | solution.py:316
  24.8 1.3 pad_maximum_fusion.1
  26.0 1.6 %collective-permute-start.5 = (bf16[480,1280]{1,0:T(8,128)(2,1)S(1)}, bf16[480,1280]{1,0:T(8,128)(2,1)}, u32[]{:S(2)}, u32[]{:S(2)}) collective-permute-start(bf16[480,1280]{1,0:T(8,128)(2,1)S(1)} %pad_maximum_fusion.1), channel_id=1, source_target_pairs={{0,12},{4,0},{8,4},{12,8},{1,13},{5,1},{9,5},{13,9},{2,14},{6,2},{... | collective-permute-start | bytes 3686408 | tf_op jit(solution)/shard_map/ppermute | solution.py:299
  27.7 0.1 pad_maximum_fusion
  27.8 0.5 collective-permute-start.4
  28.4 1.0 constant_dynamic-update-slice_fusion.2
  29.5 0.1 collective-permute-start.6
  29.6 23.1 %collective-permute-done.5.refs_2_ = bf16[480,1280]{1,0:T(8,128)(2,1)} collective-permute-done((bf16[480,1280]{1,0:T(8,128)(2,1)S(1)}, bf16[480,1280]{1,0:T(8,128)(2,1)}, u32[]{:S(2)}, u32[]{:S(2)}) %collective-permute-start.5) | collective-permute-done | bytes 1228832 | tf_op jit(solution)/shard_map/ppermute | solution.py:299
  52.7 2.8 %collective-permute-done.4.refs_1_ = bf16[480,1280]{1,0:T(8,128)(2,1)} collective-permute-done((bf16[480,1280]{1,0:T(8,128)(2,1)S(1)}, bf16[480,1280]{1,0:T(8,128)(2,1)}, u32[]{:S(2)}, u32[]{:S(2)}) %collective-permute-start.4) | collective-permute-done | bytes 1228832 | tf_op jit(solution)/shard_map/ppermute | solution.py:299
  55.5 1.0 slice.17
  56.5 1.0 pad_maximum_fusion.3
  57.5 0.6 collective-permute-start.10
  58.1 1.0 slice.16
  59.1 0.9 pad_maximum_fusion.2
  60.1 1.4 collective-permute-start.9
  61.5 0.1 copy.9
  61.6 0.1 reshape.6
  61.7 0.1 add_add_fusion.1
  61.8 6.5 %all-to-all-done.parts_ref = bf16[8,3,128,640]{3,2,1,0:T(8,128)(2,1)} async-done(((bf16[8,3,128,640]{3,2,1,0:T(8,128)(2,1)}), bf16[8,3,128,640]{3,2,1,0:T(8,128)(2,1)}, u32[]{:S(2)}, u32[]{:S(2)}) %all-to-all-start) | async-done | bytes 3932192 | tf_op jit(solution)/shard_map/all_to_all | solution.py:316
  68.3 5.6 %shard_map.66 = bf16[4,128,640]{2,1,0:T(8,128)(2,1)} custom-call(s32[98]{0:T(128)S(1)} %get-tuple-element.79.meta, bf16[8,3,128,640]{3,2,1,0:T(8,128)(2,1)} %all-to-all-done.parts_ref), custom_call_target="tpu_custom_call" | custom-call | flops 503316480 | bytes 3932160 | tf_op jit(solution)/shard_map/pallas_call | solution.py:102
  73.9 1.0 collective-permute-start.11
  74.9 4.7 %shard_map.65.mine_ref = bf16[4,128,640]{2,1,0:T(8,128)(2,1)S(1)} custom-call(s32[98]{0:T(128)S(1)} %get-tuple-element.80.meta, bf16[8,3,128,640]{3,2,1,0:T(8,128)(2,1)} %all-to-all-done.parts_ref), custom_call_target="tpu_custom_call" | custom-call | flops 503316480 | bytes 3932160 | tf_op jit(solution)/shard_map/pallas_call | solution.py:102
  79.6 2.1 %collective-permute-done.9.refs_3_ = bf16[320,1280]{1,0:T(8,128)(2,1)} collective-permute-done((bf16[320,1280]{1,0:T(8,128)(2,1)}, bf16[320,1280]{1,0:T(8,128)(2,1)}, u32[]{:S(2)}, u32[]{:S(2)}) %collective-permute-start.9) | collective-permute-done | bytes 819232 | tf_op jit(solution)/shard_map/ppermute | solution.py:299
  81.7 0.5 collective-permute-start.13
  82.2 0.1 pad_add_fusion.1.meta
  82.3 9.8 %collective-permute-done.11.other_ref = bf16[4,128,640]{2,1,0:T(8,128)(2,1)} collective-permute-done((bf16[4,128,640]{2,1,0:T(8,128)(2,1)}, bf16[4,128,640]{2,1,0:T(8,128)(2,1)}, u32[]{:S(2)}, u32[]{:S(2)}) %collective-permute-start.11) | collective-permute-done | bytes 655392 | tf_op jit(solution)/shard_map/ppermute | solution.py:299
  92.1 8.1 %shard_map.69 = (bf16[128,2560]{1,0:T(8,128)(2,1)S(1)}, bf16[2,128,1280]{2,1,0:T(8,128)(2,1)S(1)}, bf16[2,128,1280]{2,1,0:T(8,128)(2,1)S(1)}, bf16[128,1280]{1,0:T(8,128)(2,1)S(1)}, bf16[128,1280]{1,0:T(8,128)(2,1)S(1)}) custom-call(s32[2]{0:T(128)S(1)} %pad_add_fusion.1.meta, bf16[4,128,640]{2,1,0:T(8,128)(2,1)S(1)} %shard_map.65.mine_ref, ...), custom_call_target="tpu_custom_call" | custom-call | flops 3355443200 | bytes 11796480 | tf_op jit(solution)/shard_map/pallas_call | solution.py:192
  100.2 0.8 copy-done.8
  101.0 1.2 collective-permute-start.20
  102.2 2.0 %collective-permute-start.21 = (bf16[2,128,1280]{2,1,0:T(8,128)(2,1)S(1)}, bf16[2,128,1280]{2,1,0:T(8,128)(2,1)S(1)}, u32[]{:S(2)}, u32[]{:S(2)}) collective-permute-start(bf16[2,128,1280]{2,1,0:T(8,128)(2,1)S(1)} %get-tuple-element.74), channel_id=1, source_target_pairs={{0,48},{16,0},{32,16},{48,32},{1,49},{17,1},{33,17},{49,33},{2,50}... | collective-permute-start | bytes 1966088 | tf_op jit(solution)/shard_map/ppermute | solution.py:299
  104.2 8.5 %shard_map.67 = (bf16[128,2560]{1,0:T(8,128)(2,1)S(1)}, bf16[128,1280]{1,0:T(8,128)(2,1)S(1)}, bf16[128,1280]{1,0:T(8,128)(2,1)}, bf16[128,1280]{1,0:T(8,128)(2,...) custom-call(s32[2]{0:T(128)S(1)} %pad_add_fusion.1.meta, ...), custom_call_target="tpu_custom_call" | custom-call | flops 3355443200 | bytes 11796480 | tf_op jit(solution)/shard_map/pallas_call | solution.py:192
  112.8 3.2 %collective-permute-start.16 = (bf16[128,1280]{1,0:T(8,128)(2,1)S(1)}, bf16[128,1280]{1,0:T(8,128)(2,1)S(1)}, u32[]{:S(2)}, u32[]{:S(2)}) collective-permute-start(bf16[128,1280]{1,0:T(8,128)(2,1)S(1)} %get-tuple-element.66), channel_id=1, source_target_pairs={{0,48},{16,0},{32,16},{48,32},{1,49},{17,1},{33,17},{49,33},{2,50}... | collective-permute-start | bytes 983048 | tf_op jit(solution)/shard_map/ppermute | solution.py:299
  116.0 3.8 %collective-permute-done.20.x_ref.low_b = bf16[2,128,1280]{2,1,0:T(8,128)(2,1)S(1)} collective-permute-done((bf16[2,128,1280]{2,1,0:T(8,128)(2,1)S(1)}, bf16[2,128,1280]{2,1,0:T(8,128)(2,1)S(1)}, u32[]{:S(2)}, u32[]{:S(2)}) %collective-permute-start.20) | collective-permute-done | bytes 655392 | tf_op jit(solution)/shard_map/ppermute | solution.py:299
  119.9 0.9 shard_map.70
  120.8 0.8 copy-done.1
  121.7 2.0 %collective-permute-start.14 = (bf16[128,1280]{1,0:T(8,128)(2,1)}, bf16[128,1280]{1,0:T(8,128)(2,1)S(1)}, u32[]{:S(2)}, u32[]{:S(2)}) collective-permute-start(bf16[128,1280]{1,0:T(8,128)(2,1)} %get-tuple-element.62), channel_id=1, source_target_pairs={{0,16},{16,32},{32,48},{48,0},{1,17},{17,33},{33,49},{49,1},{2,18}... | collective-permute-start | bytes 983048 | tf_op jit(solution)/shard_map/ppermute | solution.py:299
  123.7 1.3 collective-permute-start.23
  125.0 1.9 %collective-permute-done.15.x_ref = bf16[128,1280]{1,0:T(8,128)(2,1)S(1)} collective-permute-done((bf16[128,1280]{1,0:T(8,128)(2,1)S(1)}, bf16[128,1280]{1,0:T(8,128)(2,1)S(1)}, u32[]{:S(2)}, u32[]{:S(2)}) %collective-permute-start.15) | collective-permute-done | bytes 327712 | tf_op jit(solution)/shard_map/ppermute | solution.py:299
  126.9 0.6 collective-permute-start.18
  127.5 0.9 shard_map.68
  128.4 1.4 collective-permute-start.17
  129.8 4.1 %collective-permute-done.22.low_a = bf16[128,1280]{1,0:T(8,128)(2,1)S(1)} collective-permute-done((bf16[128,1280]{1,0:T(8,128)(2,1)S(1)}, bf16[128,1280]{1,0:T(8,128)(2,1)S(1)}, u32[]{:S(2)}, u32[]{:S(2)}) %collective-permute-start.22) | collective-permute-done | bytes 327712 | tf_op jit(solution)/shard_map/ppermute | solution.py:299
  133.9 1.6 %collective-permute-start.19 = (bf16[128,1280]{1,0:T(8,128)(2,1)}, bf16[128,1280]{1,0:T(8,128)(2,1)S(1)}, u32[]{:S(2)}, u32[]{:S(2)}) collective-permute-start(bf16[128,1280]{1,0:T(8,128)(2,1)} %get-tuple-element.69), channel_id=1, source_target_pairs={{0,48},{16,0},{32,16},{48,32},{1,49},{17,1},{33,17},{49,33},{2,50}... | collective-permute-start | bytes 983048 | tf_op jit(solution)/shard_map/ppermute | solution.py:299
  135.6 1.1 copy-done.2
  136.7 1.1 copy-done.4
  137.8 1.6 %shard_map.71.refs_0_ = bf16[1,128,5120]{2,1,0:T(8,128)(2,1)} custom-call(s32[2]{0:T(128)S(1)} %get-tuple-element.82.meta, f32[1,5120]{1,0:T(1,128)S(1)} %copy-done.12, bf16[128,2560]{1,0:T(8,128)(2,1)S(1)} %copy-done.9, bf16[2,128,1280]{2,1,0:T(8,128)(2,1)S(1)} %copy-done.2, bf16[128,1280]{1,0:T(8,128)(2,1)S(1)} %collective-permute-done.22.low_a, ...), custom_call_target="tpu_custom_call" | custom-call | flops 1310720 | bytes 2621440 | tf_op jit(solution)/shard_map/pallas_call | solution.py:272
  139.4 1.5 %collective-permute-done.14.low_b = bf16[128,1280]{1,0:T(8,128)(2,1)S(1)} collective-permute-done((bf16[128,1280]{1,0:T(8,128)(2,1)}, bf16[128,1280]{1,0:T(8,128)(2,1)S(1)}, u32[]{:S(2)}, u32[]{:S(2)}) %collective-permute-start.14) | collective-permute-done | bytes 327712 | tf_op jit(solution)/shard_map/ppermute | solution.py:299
  140.9 1.2 collective-permute-done.18.high_a
  142.2 3.5 %collective-permute-done.17.low_a = bf16[128,1280]{1,0:T(8,128)(2,1)S(1)} collective-permute-done((bf16[128,1280]{1,0:T(8,128)(2,1)}, bf16[128,1280]{1,0:T(8,128)(2,1)S(1)}, u32[]{:S(2)}, u32[]{:S(2)}) %collective-permute-start.17) | collective-permute-done | bytes 327712 | tf_op jit(solution)/shard_map/ppermute | solution.py:299
  145.7 0.1 collective-permute-done.19.high_b
  145.8 1.6 %shard_map.72 = bf16[1,128,5120]{2,1,0:T(8,128)(2,1)} custom-call(s32[2]{0:T(128)S(1)} %get-tuple-element.81.meta, f32[1,5120]{1,0:T(1,128)S(1)} %copy-done.12, bf16[128,2560]{1,0:T(8,128)(2,1)S(1)} %copy-done.11, bf16[128,1280]{1,0:T(8,128)(2,1)S(1)} %collective-permute-done.14.low_b, ...), custom_call_target="tpu_custom_call", output_to_operand_aliasing={{}: (7, {})} | custom-call | flops 1310720 | bytes 2621440 | tf_op jit(solution)/shard_map/pallas_call | solution.py:272
  (51 shorter events, 0.5 us)
Async XLA Ops:
  0.0 6.6 %copy-start.5 = (bf16[1,128,5120]{2,1,0:T(8,128)(2,1)S(1)}, bf16[1,128,5120]{2,1,0:T(8,128)(2,1)}, u32[]{:S(2)}) copy-start(bf16[1,128,5120]{2,1,0:T(8,128)(2,1)} %param.6) | copy-start | bytes 3932164
  1.3 9.0 %copy-start.13 = (bf16[160,1280]{1,0:T(8,128)(2,1)}, bf16[160,1280]{1,0:T(8,128)(2,1)S(1)}, u32[]{:S(2)}) copy-start(bf16[160,1280]{1,0:T(8,128)(2,1)S(1)} %get-tuple-element.46) | copy-start | bytes 1228804
  1.3 12.6 %copy-start.15 = (bf16[160,1280]{1,0:T(8,128)(2,1)}, bf16[160,1280]{1,0:T(8,128)(2,1)S(1)}, u32[]{:S(2)}) copy-start(bf16[160,1280]{1,0:T(8,128)(2,1)S(1)} %get-tuple-element.45) | copy-start | bytes 1228804
  1.3 12.5 %collective-permute-start.2 = (bf16[160,1280]{1,0:T(8,128)(2,1)S(1)}, bf16[160,1280]{1,0:T(8,128)(2,1)S(1)}, u32[]{:S(2)}, u32[]{:S(2)}) collective-permute-start(bf16[160,1280]{1,0:T(8,128)(2,1)S(1)} %get-tuple-element.45), channel_id=1, source_target_pairs={{0,4},{4,8},{8,12},{12,0},{1,5},{5,9},{9,13},{13,1},{2,6},{6,10},{... | collective-permute-start | bytes 1228808 | tf_op jit(solution)/shard_map/ppermute | solution.py:299
  2.9 11.0 %collective-permute-start.3 = (bf16[160,1280]{1,0:T(8,128)(2,1)S(1)}, bf16[160,1280]{1,0:T(8,128)(2,1)}, u32[]{:S(2)}, u32[]{:S(2)}) collective-permute-start(bf16[160,1280]{1,0:T(8,128)(2,1)S(1)} %get-tuple-element.46), channel_id=1, source_target_pairs={{0,12},{4,0},{8,4},{12,8},{1,13},{5,1},{9,5},{13,9},{2,14},{6,2},{... | collective-permute-start | bytes 1228808 | tf_op jit(solution)/shard_map/ppermute | solution.py:299
  4.6 10.6 %collective-permute-start = (bf16[160,1280]{1,0:T(8,128)(2,1)S(1)}, bf16[160,1280]{1,0:T(8,128)(2,1)S(1)}, u32[]{:S(2)}, u32[]{:S(2)}) collective-permute-start(bf16[160,1280]{1,0:T(8,128)(2,1)S(1)} %get-tuple-element.45), channel_id=1, source_target_pairs={{0,2},{2,64},{64,66},{66,0},{1,3},{3,65},{65,67},{67,1},{4,6},{6,6... | collective-permute-start | bytes 1228808 | tf_op jit(solution)/shard_map/ppermute | solution.py:299
  4.8 11.7 %collective-permute-start.1 = (bf16[160,1280]{1,0:T(8,128)(2,1)S(1)}, bf16[160,1280]{1,0:T(8,128)(2,1)S(1)}, u32[]{:S(2)}, u32[]{:S(2)}) collective-permute-start(bf16[160,1280]{1,0:T(8,128)(2,1)S(1)} %get-tuple-element.46), channel_id=1, source_target_pairs={{0,66},{2,0},{64,2},{66,64},{1,67},{3,1},{65,3},{67,65},{4,70},{6,... | collective-permute-start | bytes 1228808 | tf_op jit(solution)/shard_map/ppermute | solution.py:299
  6.6 1.3 copy-start.6
  8.0 1.3 copy-start.7
  10.3 1.9 %copy-start = (bf16[2,4,3,128,640]{4,3,2,1,0:T(8,128)(2,1)}, bf16[2,4,3,128,640]{4,3,2,1,0:T(8,128)(2,1)S(1)}, u32[]{:S(2)}) copy-start(bf16[2,4,3,128,640]{4,3,2,1,0:T(8,128)(2,1)S(1)} %shard_map.64) | copy-start | bytes 11796484
  13.8 2.7 %copy-start.16 = (bf16[160,1280]{1,0:T(8,128)(2,1)}, bf16[160,1280]{1,0:T(8,128)(2,1)S(1)}, u32[]{:S(2)}) copy-start(bf16[160,1280]{1,0:T(8,128)(2,1)S(1)} %collective-permute-done.2) | copy-start | bytes 1228804
  16.5 51.8 %all-to-all-start = ((bf16[8,3,128,640]{3,2,1,0:T(8,128)(2,1)}), bf16[8,3,128,640]{3,2,1,0:T(8,128)(2,1)}, u32[]{:S(2)}, u32[]{:S(2)}) async-start(bf16[8,3,128,640]{3,2,1,0:T(8,128)(2,1)} %bitcast.15), calls=%async_computation | async-start | bytes 7864320 | tf_op jit(solution)/shard_map/all_to_all | solution.py:316
  24.8 2.9 %copy-start.14 = (bf16[160,1280]{1,0:T(8,128)(2,1)S(1)}, bf16[160,1280]{1,0:T(8,128)(2,1)}, u32[]{:S(2)}) copy-start(bf16[160,1280]{1,0:T(8,128)(2,1)} %copy-done.13) | copy-start | bytes 1228804
  24.8 2.9 %copy-start.17 = (bf16[160,1280]{1,0:T(8,128)(2,1)S(1)}, bf16[160,1280]{1,0:T(8,128)(2,1)}, u32[]{:S(2)}) copy-start(bf16[160,1280]{1,0:T(8,128)(2,1)} %copy-done.16) | copy-start | bytes 1228804
  26.0 26.7 %collective-permute-start.5 = (bf16[480,1280]{1,0:T(8,128)(2,1)S(1)}, bf16[480,1280]{1,0:T(8,128)(2,1)}, u32[]{:S(2)}, u32[]{:S(2)}) collective-permute-start(bf16[480,1280]{1,0:T(8,128)(2,1)S(1)} %pad_maximum_fusion.1), channel_id=1, source_target_pairs={{0,12},{4,0},{8,4},{12,8},{1,13},{5,1},{9,5},{13,9},{2,14},{6,2},{... | collective-permute-start | bytes 3686408 | tf_op jit(solution)/shard_map/ppermute | solution.py:299
  27.8 27.7 %collective-permute-start.4 = (bf16[480,1280]{1,0:T(8,128)(2,1)S(1)}, bf16[480,1280]{1,0:T(8,128)(2,1)}, u32[]{:S(2)}, u32[]{:S(2)}) collective-permute-start(bf16[480,1280]{1,0:T(8,128)(2,1)S(1)} %pad_maximum_fusion), channel_id=1, source_target_pairs={{0,4},{4,8},{8,12},{12,0},{1,5},{5,9},{9,13},{13,1},{2,6},{6,10},{... | collective-permute-start | bytes 3686408 | tf_op jit(solution)/shard_map/ppermute | solution.py:299
  29.5 32.0 %copy-start.18 = (s32[16,6]{0,1:T(8,128)S(1)}, s32[16,6]{0,1:T(8,128)}, u32[]{:S(2)}) copy-start(s32[16,6]{0,1:T(8,128)} %param.11) | copy-start | bytes 1156
  29.5 32.3 %collective-permute-start.6 = (bf16[960,1280]{1,0:T(8,128)(2,1)S(1)}, bf16[960,1280]{1,0:T(8,128)(2,1)}, u32[]{:S(2)}, u32[]{:S(2)}) collective-permute-start(bf16[960,1280]{1,0:T(8,128)(2,1)S(1)} %constant_dynamic-update-slice_fusion.refs_0_), channel_id=1, source_target_pairs={{0,1},{1,0},{2,3},{3,2},{4,5},{5,4},{6,7},{7,6},{8,9},{9,8},{10,11... | collective-permute-start | bytes 7372808 | tf_op jit(solution)/shard_map/ppermute | solution.py:299
  52.7 9.1 %collective-permute-start.8 = (bf16[480,1280]{1,0:T(8,128)(2,1)}, bf16[480,1280]{1,0:T(8,128)(2,1)}, u32[]{:S(2)}, u32[]{:S(2)}) collective-permute-start(bf16[480,1280]{1,0:T(8,128)(2,1)} %collective-permute-done.5.refs_2_), channel_id=1, source_target_pairs={{0,1},{1,0},{2,3},{3,2},{4,5},{5,4},{6,7},{7,6},{8,9},{9,8},{10,11... | collective-permute-start | bytes 3686408 | tf_op jit(solution)/shard_map/ppermute | solution.py:299
  55.5 6.3 %collective-permute-start.7 = (bf16[480,1280]{1,0:T(8,128)(2,1)}, bf16[480,1280]{1,0:T(8,128)(2,1)}, u32[]{:S(2)}, u32[]{:S(2)}) collective-permute-start(bf16[480,1280]{1,0:T(8,128)(2,1)} %collective-permute-done.4.refs_1_), channel_id=1, source_target_pairs={{0,1},{1,0},{2,3},{3,2},{4,5},{5,4},{6,7},{7,6},{8,9},{9,8},{10,11... | collective-permute-start | bytes 3686408 | tf_op jit(solution)/shard_map/ppermute | solution.py:299
  57.5 22.1 %collective-permute-start.10 = (bf16[320,1280]{1,0:T(8,128)(2,1)}, bf16[320,1280]{1,0:T(8,128)(2,1)}, u32[]{:S(2)}, u32[]{:S(2)}) collective-permute-start(bf16[320,1280]{1,0:T(8,128)(2,1)} %pad_maximum_fusion.3), channel_id=1, source_target_pairs={{0,12},{4,0},{8,4},{12,8},{1,13},{5,1},{9,5},{13,9},{2,14},{6,2},{... | collective-permute-start | bytes 2457608 | tf_op jit(solution)/shard_map/ppermute | solution.py:299
  60.1 21.6 %collective-permute-start.9 = (bf16[320,1280]{1,0:T(8,128)(2,1)}, bf16[320,1280]{1,0:T(8,128)(2,1)}, u32[]{:S(2)}, u32[]{:S(2)}) collective-permute-start(bf16[320,1280]{1,0:T(8,128)(2,1)} %pad_maximum_fusion.2), channel_id=1, source_target_pairs={{0,4},{4,8},{8,12},{12,0},{1,5},{5,9},{9,13},{13,1},{2,6},{6,10},{... | collective-permute-start | bytes 2457608 | tf_op jit(solution)/shard_map/ppermute | solution.py:299
  73.9 18.2 %collective-permute-start.11 = (bf16[4,128,640]{2,1,0:T(8,128)(2,1)}, bf16[4,128,640]{2,1,0:T(8,128)(2,1)}, u32[]{:S(2)}, u32[]{:S(2)}) collective-permute-start(bf16[4,128,640]{2,1,0:T(8,128)(2,1)} %shard_map.66), channel_id=1, source_target_pairs={{0,64},{64,0},{1,65},{65,1},{2,66},{66,2},{3,67},{67,3},{4,68},{68... | collective-permute-start | bytes 1966088 | tf_op jit(solution)/shard_map/ppermute | solution.py:299
  81.7 22.5 %collective-permute-start.12 = (bf16[320,1280]{1,0:T(8,128)(2,1)}, bf16[320,1280]{1,0:T(8,128)(2,1)}, u32[]{:S(2)}, u32[]{:S(2)}) collective-permute-start(bf16[320,1280]{1,0:T(8,128)(2,1)} %collective-permute-done.9.refs_3_), channel_id=1, source_target_pairs={{0,1},{1,0},{2,3},{3,2},{4,5},{5,4},{6,7},{7,6},{8,9},{9,8},{10,11... | collective-permute-start | bytes 2457608 | tf_op jit(solution)/shard_map/ppermute | solution.py:299
  81.7 22.5 %collective-permute-start.13 = (bf16[320,1280]{1,0:T(8,128)(2,1)}, bf16[320,1280]{1,0:T(8,128)(2,1)}, u32[]{:S(2)}, u32[]{:S(2)}) collective-permute-start(bf16[320,1280]{1,0:T(8,128)(2,1)} %collective-permute-done.10.refs_4_), channel_id=1, source_target_pairs={{0,1},{1,0},{2,3},{3,2},{4,5},{5,4},{6,7},{7,6},{8,9},{9,8},{10,11... | collective-permute-start | bytes 2457608 | tf_op jit(solution)/shard_map/ppermute | solution.py:299
  100.1 0.8 copy-start.8
  101.0 18.9 %collective-permute-start.20 = (bf16[2,128,1280]{2,1,0:T(8,128)(2,1)S(1)}, bf16[2,128,1280]{2,1,0:T(8,128)(2,1)S(1)}, u32[]{:S(2)}, u32[]{:S(2)}) collective-permute-start(bf16[2,128,1280]{2,1,0:T(8,128)(2,1)S(1)} %get-tuple-element.71), channel_id=1, source_target_pairs={{0,16},{16,32},{32,48},{48,0},{1,17},{17,33},{33,49},{49,1},{2,18}... | collective-permute-start | bytes 1966088 | tf_op jit(solution)/shard_map/ppermute | solution.py:299
  102.2 17.7 %collective-permute-start.21 = (bf16[2,128,1280]{2,1,0:T(8,128)(2,1)S(1)}, bf16[2,128,1280]{2,1,0:T(8,128)(2,1)S(1)}, u32[]{:S(2)}, u32[]{:S(2)}) collective-permute-start(bf16[2,128,1280]{2,1,0:T(8,128)(2,1)S(1)} %get-tuple-element.74), channel_id=1, source_target_pairs={{0,48},{16,0},{32,16},{48,32},{1,49},{17,1},{33,17},{49,33},{2,50}... | collective-permute-start | bytes 1966088 | tf_op jit(solution)/shard_map/ppermute | solution.py:299
  112.7 9.0 %copy-start.10 = (bf16[128,2560]{1,0:T(8,128)(2,1)}, bf16[128,2560]{1,0:T(8,128)(2,1)S(1)}, u32[]{:S(2)}) copy-start(bf16[128,2560]{1,0:T(8,128)(2,1)S(1)} %get-tuple-element.61.own) | copy-start | bytes 1966084
  112.7 22.9 %copy-start.9 = (bf16[128,2560]{1,0:T(8,128)(2,1)S(1)}, bf16[128,2560]{1,0:T(8,128)(2,1)}, u32[]{:S(2)}) copy-start(bf16[128,2560]{1,0:T(8,128)(2,1)} %copy-done.8) | copy-start | bytes 1966084
  112.7 22.9 %copy-start.12 = (f32[1,5120]{1,0:T(1,128)S(1)}, f32[1,5120]{1,0:T(1,128)}, u32[]{:S(2)}) copy-start(f32[1,5120]{1,0:T(1,128)} %gate_ref.3) | copy-start | bytes 61444
  112.7 14.1 %collective-permute-start.15 = (bf16[128,1280]{1,0:T(8,128)(2,1)S(1)}, bf16[128,1280]{1,0:T(8,128)(2,1)S(1)}, u32[]{:S(2)}, u32[]{:S(2)}) collective-permute-start(bf16[128,1280]{1,0:T(8,128)(2,1)S(1)} %get-tuple-element.64), channel_id=1, source_target_pairs={{0,16},{16,32},{32,48},{48,0},{1,17},{17,33},{33,49},{49,1},{2,18}... | collective-permute-start | bytes 983048 | tf_op jit(solution)/shard_map/ppermute | solution.py:299
  112.8 14.7 %collective-permute-start.16 = (bf16[128,1280]{1,0:T(8,128)(2,1)S(1)}, bf16[128,1280]{1,0:T(8,128)(2,1)S(1)}, u32[]{:S(2)}, u32[]{:S(2)}) collective-permute-start(bf16[128,1280]{1,0:T(8,128)(2,1)S(1)} %get-tuple-element.66), channel_id=1, source_target_pairs={{0,48},{16,0},{32,16},{48,32},{1,49},{17,1},{33,17},{49,33},{2,50}... | collective-permute-start | bytes 983048 | tf_op jit(solution)/shard_map/ppermute | solution.py:299
  119.9 0.9 copy-start.3
  120.8 0.8 copy-start.1
  121.7 12.2 %collective-permute-start.22 = (bf16[128,1280]{1,0:T(8,128)(2,1)S(1)}, bf16[128,1280]{1,0:T(8,128)(2,1)S(1)}, u32[]{:S(2)}, u32[]{:S(2)}) collective-permute-start(bf16[128,1280]{1,0:T(8,128)(2,1)S(1)} %get-tuple-element.75), channel_id=1, source_target_pairs={{0,16},{16,32},{32,48},{48,0},{1,17},{17,33},{33,49},{49,1},{2,18}... | collective-permute-start | bytes 983048 | tf_op jit(solution)/shard_map/ppermute | solution.py:299
  121.7 19.3 %collective-permute-start.14 = (bf16[128,1280]{1,0:T(8,128)(2,1)}, bf16[128,1280]{1,0:T(8,128)(2,1)S(1)}, u32[]{:S(2)}, u32[]{:S(2)}) collective-permute-start(bf16[128,1280]{1,0:T(8,128)(2,1)} %get-tuple-element.62), channel_id=1, source_target_pairs={{0,16},{16,32},{32,48},{48,0},{1,17},{17,33},{33,49},{49,1},{2,18}... | collective-permute-start | bytes 983048 | tf_op jit(solution)/shard_map/ppermute | solution.py:299
  123.7 11.9 %collective-permute-start.23 = (bf16[128,1280]{1,0:T(8,128)(2,1)}, bf16[128,1280]{1,0:T(8,128)(2,1)S(1)}, u32[]{:S(2)}, u32[]{:S(2)}) collective-permute-start(bf16[128,1280]{1,0:T(8,128)(2,1)} %get-tuple-element.76), channel_id=1, source_target_pairs={{0,48},{16,0},{32,16},{48,32},{1,49},{17,1},{33,17},{49,33},{2,50}... | collective-permute-start | bytes 983048 | tf_op jit(solution)/shard_map/ppermute | solution.py:299
  126.9 15.3 %collective-permute-start.18 = (bf16[128,1280]{1,0:T(8,128)(2,1)}, bf16[128,1280]{1,0:T(8,128)(2,1)S(1)}, u32[]{:S(2)}, u32[]{:S(2)}) collective-permute-start(bf16[128,1280]{1,0:T(8,128)(2,1)} %get-tuple-element.68), channel_id=1, source_target_pairs={{0,48},{16,0},{32,16},{48,32},{1,49},{17,1},{33,17},{49,33},{2,50}... | collective-permute-start | bytes 983048 | tf_op jit(solution)/shard_map/ppermute | solution.py:299
  127.5 18.3 %copy-start.11 = (bf16[128,2560]{1,0:T(8,128)(2,1)S(1)}, bf16[128,2560]{1,0:T(8,128)(2,1)}, u32[]{:S(2)}) copy-start(bf16[128,2560]{1,0:T(8,128)(2,1)} %copy-done.10) | copy-start | bytes 1966084
  128.4 17.3 %collective-permute-start.17 = (bf16[128,1280]{1,0:T(8,128)(2,1)}, bf16[128,1280]{1,0:T(8,128)(2,1)S(1)}, u32[]{:S(2)}, u32[]{:S(2)}) collective-permute-start(bf16[128,1280]{1,0:T(8,128)(2,1)} %get-tuple-element.67), channel_id=1, source_target_pairs={{0,16},{16,32},{32,48},{48,0},{1,17},{17,33},{33,49},{49,1},{2,18}... | collective-permute-start | bytes 983048 | tf_op jit(solution)/shard_map/ppermute | solution.py:299
  133.9 11.9 %collective-permute-start.19 = (bf16[128,1280]{1,0:T(8,128)(2,1)}, bf16[128,1280]{1,0:T(8,128)(2,1)S(1)}, u32[]{:S(2)}, u32[]{:S(2)}) collective-permute-start(bf16[128,1280]{1,0:T(8,128)(2,1)} %get-tuple-element.69), channel_id=1, source_target_pairs={{0,48},{16,0},{32,16},{48,32},{1,49},{17,1},{33,17},{49,33},{2,50}... | collective-permute-start | bytes 983048 | tf_op jit(solution)/shard_map/ppermute | solution.py:299
  135.6 1.1 copy-start.2
  136.7 1.1 copy-start.4
